TPU v7x, 32 devices: a whole 2x2x4 slice. The times are simulated.
32 devices in a mesh: seq: 4 (over y, core), head: 8 (over z, x).
Axes of the slice: x: 2, y: 2, z: 4, core: 2. Of those that a mesh axis runs over, the one named last changes fastest.
Arguments:
- out_grad: bfloat16 [8192, 4096], P(('seq', 'head')), may hold values from -6 to 6
- out_weight: bfloat16 [4096, 4096], P('head'), may hold values from -0.09375 to 0.09375
- queries: bfloat16 [8192, 4096], P('seq', 'head'), may hold values from -4 to 4
- key_rows: bfloat16 [8192, 4096], P('seq', 'head'), may hold values from -4 to 4
- value_rows: bfloat16 [8192, 4096], P('seq', 'head')
- gate_out: bfloat16 [8192, 4096], P('seq', 'head'), may hold values from -6 to 6
- doc_starts: int32 [3], replicated, may hold values from 0 to 8191, as said below
Outputs:
- grad_queries: bfloat16 [8192, 4096], P('seq', 'head')
- grad_keys: bfloat16 [8192, 4096], P('seq', 'head')
- grad_values: bfloat16 [8192, 4096], P('seq', 'head')
- grad_gate: bfloat16 [8192, 4096], P('seq', 'head')
Inputs may be any that keep to these rules, and one draw needn't show every extreme that they name: `doc_starts`: strictly increasing token offsets; the first is 0 and the last is 8191.
All inputs are finite; a program needn't handle non-finite values.
Results may differ from a plain program's by a relative error of at most 0.0058.
Values may be sent and summed in bfloat16 or wider, within the bound.
No kernel may reach another device: no remote copies, remote signals or barrier semaphores. Data moves between devices by JAX's collectives and lax.ppermute only.
A program may use at most 128 MiB of HBM per device.

v0:
```python
import functools

import jax
import jax.numpy as jnp
from jax import lax
from jax.experimental import pallas as pl
from jax.experimental.pallas import tpu as pltpu
from jax.sharding import PartitionSpec as P

HEAD_DIM = 128
BLK = 512
SUB = 256
EPS = 1e-06
F32 = jnp.float32
BF16 = jnp.bfloat16
VMEM_LIMIT = 48 * 1024 * 1024


def dot(a, b):
    return lax.dot_general(a, b, (((1,), (0,)), ((), ())), preferred_element_type=F32)


def dot_nt(a, b):
    return lax.dot_general(a, b, (((1,), (1,)), ((), ())), preferred_element_type=F32)


def dot_tn(a, b):
    return lax.dot_general(a, b, (((0,), (0,)), ((), ())), preferred_element_type=F32)


def doc_of(info, count, pos):
    total = jnp.zeros_like(pos)
    for i in range(count):
        total = total + jnp.where(info[i] <= pos, 1, 0)
    return total


def same(a, b):
    return jnp.where(a == b, F32(1.0), F32(0.0))


def column_docs(info, count, start, size):
    return doc_of(info, count, start + lax.broadcasted_iota(jnp.int32, (size, 1), 0))


def row_docs(info, count, start, size):
    return doc_of(info, count, start + lax.broadcasted_iota(jnp.int32, (1, size), 1))


def causal_masks(info, count, start, transposed):
    cols = [column_docs(info, count, start + i * SUB, SUB) for i in range(BLK // SUB)]
    rows = [row_docs(info, count, start + i * SUB, SUB) for i in range(BLK // SUB)]
    down = lax.broadcasted_iota(jnp.int32, (SUB, SUB), 0)
    over = lax.broadcasted_iota(jnp.int32, (SUB, SUB), 1)
    masks = []
    for r in range(BLK // SUB):
        line = []
        for c in range(BLK // SUB):
            equal = cols[r] == rows[c]
            if r == c:
                line.append(equal & ((down <= over) if transposed else (over <= down)))
            elif (r < c) == transposed:
                line.append(equal)
            else:
                line.append(None)
        masks.append(line)
    return masks


def lane_sums(x):
    return jnp.sum(x.T, axis=0, keepdims=True)


def to_columns(row):
    return jnp.broadcast_to(row, (HEAD_DIM, row.shape[1])).T


def head_slice(h):
    return slice(h * HEAD_DIM, (h + 1) * HEAD_DIM)


def key_state_kernel(count, heads, info, k_ref, v_ref, before_ref, total_ref, state):
    b = pl.program_id(0)

    @pl.when(b == 0)
    def _():
        state[...] = jnp.zeros_like(state)

    start = info[count] + b * BLK
    last_doc = doc_of(info, count, start + BLK - 1)
    keep_out = same(column_docs(info, count, start, BLK), last_doc).astype(BF16)
    carry = same(doc_of(info, count, start - 1), last_doc)
    for h in range(heads):
        before_ref[0, h] = state[h]
        element = dot_tn(k_ref[:, head_slice(h)] * keep_out, v_ref[:, head_slice(h)])
        state[h] = element + carry * state[h]
    total_ref[...] = state[...]


def attention_kernel(
    count, heads, info, q_ref, k_ref, v_ref, before_ref, into_ref, attn_ref, square_ref, low_ref
):
    b = pl.program_id(0)
    first = info[count]
    start = first + b * BLK
    prior = doc_of(info, count, start - 1)
    carry = same(prior, doc_of(info, count, first - 1))
    masks = causal_masks(info, count, start, False)
    keep_in = [
        same(column_docs(info, count, start + r * SUB, SUB), prior) for r in range(BLK // SUB)
    ]
    squares = [jnp.zeros((SUB, HEAD_DIM), F32) for _ in range(BLK // SUB)]
    for h in range(heads):
        low = (before_ref[0, h] + carry * into_ref[h]).astype(BF16)
        low_ref[0, h] = low
        for r in range(BLK // SUB):
            rows = slice(r * SUB, (r + 1) * SUB)
            q = q_ref[rows, head_slice(h)]
            out = keep_in[r] * dot(q, low)
            for c in range(r + 1):
                cols = slice(c * SUB, (c + 1) * SUB)
                scores = dot_nt(q, k_ref[cols, head_slice(h)])
                probs = jnp.where(masks[r][c], scores, 0.0).astype(BF16)
                out = out + dot(probs, v_ref[cols, head_slice(h)])
            attn_ref[rows, head_slice(h)] = out
            squares[r] = squares[r] + out * out
    for r in range(BLK // SUB):
        square_ref[:, r * SUB : (r + 1) * SUB] = lane_sums(squares[r])


def cross_kernel(heads, mix_ref, gate_ref, attn_ref, cross_ref):
    total = jnp.zeros((BLK, HEAD_DIM), F32)
    for h in range(heads):
        at = head_slice(h)
        total = total + mix_ref[:, at].astype(F32) * gate_ref[:, at].astype(F32) * attn_ref[:, at]
    cross_ref[...] = lane_sums(total)


def grad_attn_kernel(
    count,
    heads,
    width,
    info,
    mix_ref,
    gate_ref,
    attn_ref,
    q_ref,
    square_ref,
    cross_ref,
    grad_ref,
    gate_grad_ref,
    after_ref,
    total_ref,
    state,
):
    @pl.when(pl.program_id(0) == 0)
    def _():
        state[...] = jnp.zeros_like(state)

    b = pl.num_programs(0) - 1 - pl.program_id(0)
    start = info[count] + b * BLK
    prior = doc_of(info, count, start - 1)
    keep_in = same(column_docs(info, count, start, BLK), prior).astype(BF16)
    carry = same(doc_of(info, count, start + BLK - 1), prior)
    rms = jnp.sqrt(square_ref[...] / width + EPS)
    inverse = to_columns(1.0 / rms)
    pull = to_columns(cross_ref[...] / (width * (rms * rms * rms)))
    for h in range(heads):
        at = head_slice(h)
        mix = mix_ref[:, at].astype(F32)
        attn = attn_ref[:, at]
        gate_grad_ref[:, at] = (mix * attn * inverse).astype(BF16)
        grad = (mix * gate_ref[:, at].astype(F32) * inverse - attn * pull).astype(BF16)
        grad_ref[:, at] = grad
        after_ref[0, h] = state[h]
        state[h] = dot_tn(q_ref[:, at] * keep_in, grad) + carry * state[h]
    total_ref[...] = state[...]


def grad_query_kernel(count, heads, info, grad_ref, k_ref, v_ref, low_ref, out_ref):
    start = info[count] + pl.program_id(0) * BLK
    prior = doc_of(info, count, start - 1)
    masks = causal_masks(info, count, start, False)
    keep_in = [
        same(column_docs(info, count, start + r * SUB, SUB), prior) for r in range(BLK // SUB)
    ]
    for h in range(heads):
        at = head_slice(h)
        for r in range(BLK // SUB):
            rows = slice(r * SUB, (r + 1) * SUB)
            grad = grad_ref[rows, at]
            out = keep_in[r] * dot_nt(grad, low_ref[0, h])
            for c in range(r + 1):
                cols = slice(c * SUB, (c + 1) * SUB)
                scores = dot_nt(grad, v_ref[cols, at])
                dprob = jnp.where(masks[r][c], scores, 0.0).astype(BF16)
                out = out + dot(dprob, k_ref[cols, at])
            out_ref[rows, at] = out.astype(BF16)


def grad_key_value_kernel(
    count, heads, length, info, grad_ref, q_ref, k_ref, v_ref, after_ref, into_ref, dk_ref, dv_ref
):
    first = info[count]
    start = first + pl.program_id(0) * BLK
    last_doc = doc_of(info, count, start + BLK - 1)
    carry = same(last_doc, doc_of(info, count, first + length - 1))
    masks = causal_masks(info, count, start, True)
    keep_out = [
        same(column_docs(info, count, start + r * SUB, SUB), last_doc) for r in range(BLK // SUB)
    ]
    for h in range(heads):
        at = head_slice(h)
        low = (after_ref[0, h] + carry * into_ref[h]).astype(BF16)
        for r in range(BLK // SUB):
            rows = slice(r * SUB, (r + 1) * SUB)
            k = k_ref[rows, at]
            v = v_ref[rows, at]
            dk = keep_out[r] * dot_nt(v, low)
            dv = keep_out[r] * dot(k, low)
            for c in range(r, BLK // SUB):
                cols = slice(c * SUB, (c + 1) * SUB)
                q = q_ref[cols, at]
                grad = grad_ref[cols, at]
                dprob = jnp.where(masks[r][c], dot_nt(v, grad), 0.0).astype(BF16)
                probs = jnp.where(masks[r][c], dot_nt(k, q), 0.0).astype(BF16)
                dk = dk + dot(dprob, q)
                dv = dv + dot(probs, grad)
            dk_ref[rows, at] = dk.astype(BF16)
            dv_ref[rows, at] = dv.astype(BF16)


def call(kernel, name, info, args, in_specs, outs, out_specs, scratch=(), flops=0):
    nblocks = max(a.shape[0] for a in args if a.ndim == 2) // BLK
    size = sum(a.size * a.dtype.itemsize for a in list(args) + list(outs))
    return pl.pallas_call(
        kernel,
        grid_spec=pltpu.PrefetchScalarGridSpec(
            num_scalar_prefetch=1,
            grid=(nblocks,),
            in_specs=in_specs,
            out_specs=out_specs,
            scratch_shapes=list(scratch),
        ),
        out_shape=outs,
        name=name,
        cost_estimate=pl.CostEstimate(flops=flops, bytes_accessed=size, transcendentals=0),
        compiler_params=pltpu.CompilerParams(vmem_limit_bytes=VMEM_LIMIT),
    )(info, *args)


def shaped(shape, dtype):
    return jax.ShapeDtypeStruct(shape, dtype)


def flip(a, axis, bit):
    return lax.ppermute(a, axis, [(i, i ^ bit) for i in range(lax.axis_size(axis))])


def body(out_grad, out_weight, queries, key_rows, value_rows, gate_out, doc_starts):
    length, width = queries.shape
    heads = width // HEAD_DIM
    nblocks = length // BLK
    count = doc_starts.shape[0]
    nseq = lax.axis_size("seq")
    full_width = width * lax.axis_size("head")
    place = lax.axis_index("seq")
    first = place * length
    info = jnp.concatenate([doc_starts, first[None].astype(jnp.int32)])

    def doc_at(pos):
        return jnp.sum((doc_starts <= pos).astype(jnp.int32))

    block = pl.BlockSpec((BLK, width), lambda b, s: (b, 0))
    line = pl.BlockSpec((1, BLK), lambda b, s: (0, b))
    states = pl.BlockSpec((1, heads, HEAD_DIM, HEAD_DIM), lambda b, s: (b, 0, 0, 0))
    state = pl.BlockSpec((heads, HEAD_DIM, HEAD_DIM), lambda b, s: (0, 0, 0))
    one_state = shaped((heads, HEAD_DIM, HEAD_DIM), F32)
    all_states = shaped((nblocks, heads, HEAD_DIM, HEAD_DIM), F32)
    low_states = shaped((nblocks, heads, HEAD_DIM, HEAD_DIM), BF16)
    tokens16 = shaped((length, width), BF16)
    tokens32 = shaped((length, width), F32)
    row = shaped((1, length), F32)
    scratch = [pltpu.VMEM((heads, HEAD_DIM, HEAD_DIM), F32)]
    unit = 2 * length * width * HEAD_DIM
    intra = 2 * length * width * BLK

    rows_all = lax.all_gather(out_grad, "head", axis=0, tiled=True)

    with jax.named_scope("key_states"):
        before, key_total = call(
            functools.partial(key_state_kernel, count, heads),
            "key_states",
            info,
            [key_rows, value_rows],
            [block, block],
            [all_states, one_state],
            [states, state],
            scratch,
            unit,
        )
    key_totals = lax.all_gather(key_total, "seq")
    into = jnp.zeros((heads, HEAD_DIM, HEAD_DIM), F32)
    for other in range(nseq):
        takes = (other < place) & (doc_at((other + 1) * length - 1) == doc_at(first - 1))
        into = into + jnp.where(takes, key_totals[other], 0.0)
    with jax.named_scope("attention"):
        attn, square, low = call(
            functools.partial(attention_kernel, count, heads),
            "attention",
            info,
            [queries, key_rows, value_rows, before, into],
            [block, block, block, states, state],
            [tokens32, row, low_states],
            [block, line, states],
            (),
            2 * intra,
        )
    square = lax.psum(square, "head")

    mix = lax.dot_general(
        rows_all, out_weight, (((1,), (1,)), ((), ())), preferred_element_type=F32
    ).astype(BF16)

    with jax.named_scope("cross"):
        cross = call(
            lambda info, *refs: cross_kernel(heads, *refs),
            "cross",
            info,
            [mix, gate_out, attn],
            [block, block, block],
            [row],
            [line],
        )[0]
    n_head = lax.axis_size("head")
    bit = 1
    while bit < n_head:
        cross = cross + flip(cross, "head", bit)
        bit *= 2

    back = lambda spec_shape, f: pl.BlockSpec(spec_shape, lambda b, s: f(nblocks - 1 - b))
    block_r = back((BLK, width), lambda b: (b, 0))
    line_r = back((1, BLK), lambda b: (0, b))
    states_r = back((1, heads, HEAD_DIM, HEAD_DIM), lambda b: (b, 0, 0, 0))
    with jax.named_scope("grad_attn"):
        grad, grad_gate, after, query_total = call(
            functools.partial(grad_attn_kernel, count, heads, full_width),
            "grad_attn",
            info,
            [mix, gate_out, attn, queries, square, cross],
            [block_r, block_r, block_r, block_r, line_r, line_r],
            [tokens16, tokens16, all_states, one_state],
            [block_r, block_r, states_r, state],
            scratch,
            unit,
        )
    last = first + length - 1
    out_of = jnp.zeros((heads, HEAD_DIM, HEAD_DIM), F32)
    for step in range(1, nseq):
        other = place ^ step
        takes = (other > place) & (doc_at(other * length - 1) == doc_at(last))
        out_of = out_of + jnp.where(takes, flip(query_total, "seq", step), 0.0)
    with jax.named_scope("grad_queries"):
        grad_queries = call(
            functools.partial(grad_query_kernel, count, heads),
            "grad_queries",
            info,
            [grad, key_rows, value_rows, low],
            [block, block, block, states],
            [tokens16],
            [block],
            (),
            2 * intra,
        )[0]
    with jax.named_scope("grad_keys_values"):
        grad_keys, grad_values = call(
            functools.partial(grad_key_value_kernel, count, heads, length),
            "grad_keys_values",
            info,
            [grad, queries, key_rows, value_rows, after, out_of],
            [block, block, block, block, states, state],
            [tokens16, tokens16],
            [block, block],
            (),
            4 * intra,
        )
    return (grad_queries, grad_keys, grad_values, grad_gate)


def solution(mesh):
    return jax.shard_map(
        body,
        mesh=mesh,
        in_specs=(
            P(("seq", "head"), None),
            P("head", None),
            P("seq", "head"),
            P("seq", "head"),
            P("seq", "head"),
            P("seq", "head"),
            P(),
        ),
        out_specs=(P("seq", "head"), P("seq", "head"), P("seq", "head"), P("seq", "head")),
        check_vma=False,
    )
```

profile of v0, /device:TPU:0, one launch (start us, length us, event | category | flops | bytes accessed | tf_op | source)
XLA Modules:
  0.0 360.8 jit_solution(1332449848499377614)
XLA Ops:
  8.0 1.6 copy-done
  9.5 1.6 copy-done.2
  11.1 3.1 key_states.1
  14.2 1.0 copy-done.11
  21.9 12.9 %all-gather.6.cloned.1.call-done = f32[16,128,128]{2,1,0:T(8,128)} async-done(((f32[4,128,128]{2,1,0:T(8,128)}), f32[16,128,128]{2,1,0:T(8,128)}) %all-gather.6.cloned.1.call-update) | async-done | bytes 1048592 | tf_op jit(solution)/shard_map/all_gather | solution.py:302
  34.8 1.3 fusion.into_ref
  36.1 1.6 copy-done.9
  37.7 1.2 copy-done.12
  38.9 10.9 %attention.1 = (f32[2048,512]{1,0:T(8,128)}, f32[1,2048]{1,0:T(1,128)S(1)}, bf16[4,4,128,128]{3,2,1,0:T(8,128)(2,1)S(1)}) custom-call(s32[4]{0:T(128)S(1)} %pad_add_fusion.info, bf16[2048,512]{1,0:T(8,128)(2,1)S(1)} %copy-done.9, bf16[2048,512]{1,0:T(8,128)(2,1)S(1)} %copy-done.1, bf16[2048,512]{1,0:T(8,128)(2,1)} %v_ref.7, ...), custom_call_target="tpu_custom_call" | custom-call | flops 2147483648 | bytes 12328960 | tf_op jit(solution)/shard_map/attention/attention/pallas_call | solution.py:236
  49.8 214.7 %all-gather.4.cloned.1.call-done = bf16[2048,4096]{1,0:T(8,128)(2,1)} async-done(((bf16[256,4096]{1,0:T(8,128)(2,1)}), bf16[2048,4096]{1,0:T(8,128)(2,1)}) %all-gather.4.cloned.1.call-update) | async-done | bytes 16777232 | tf_op jit(solution)/shard_map/all_gather | solution.py:288
  264.6 13.8 %convolution_convert_fusion.refs_0_.mix_ref = bf16[2048,512]{1,0:T(8,128)(2,1)S(1)} fusion(bf16[2048,4096]{1,0:T(8,128)(2,1)} %all-gather.4.cloned.1.call-done, bf16[512,4096]{1,0:T(8,128)(2,1)} %param.8), kind=kOutput, calls=%fused_computation | convolution fusion | flops 8590983168 | bytes 23068672 | tf_op jit(solution)/shard_map/dot_general | solution.py:321
  278.4 4.1 %cross.1 = f32[1,2048]{1,0:T(1,128)S(1)} custom-call(s32[4]{0:T(128)S(1)} %pad_add_fusion.info, bf16[2048,512]{1,0:T(8,128)(2,1)S(1)} %convolution_convert_fusion.refs_0_.mix_ref, bf16[2048,512]{1,0:T(8,128)(2,1)S(1)} %copy-done.3, f32[2048,512]{1,0:T(8,128)} %get-tuple-element.17.refs_2_.attn_ref), custom_call_target="tpu_custom_call" | custom-call | bytes 8396800 | tf_op jit(solution)/shard_map/cross/cross/pallas_call | solution.py:236
  283.1 3.1 collective-permute-done
  286.3 3.6 %collective-permute-done.1 = f32[1,2048]{1,0:T(1,128)S(1)} collective-permute-done((f32[1,2048]{1,0:T(1,128)S(1)}, f32[1,2048]{1,0:T(1,128)S(1)}, u32[]{:S(2)}, u32[]{:S(2)}) %collective-permute-start.1) | collective-permute-done | bytes 8224 | tf_op jit(solution)/shard_map/ppermute | solution.py:257
  289.9 1.6 collective-permute-start.2
  291.5 18.4 %psum.7.square_ref = f32[1,2048]{1,0:T(1,128)S(1)} all-reduce(f32[1,2048]{1,0:T(1,128)S(1)} %get-tuple-element.18), channel_id=1, replica_groups=mesh['seq'=4,'head'=8] {'head'}, use_global_device_ids=true, to_apply=%region_5.6 | all-reduce | flops 2048 | bytes 16384 | tf_op jit(solution)/shard_map/psum | solution.py:319
  310.0 1.6 copy-done.5
  311.5 6.9 %grad_attn.1 = (bf16[2048,512]{1,0:T(8,128)(2,1)S(1)}, bf16[2048,512]{1,0:T(8,128)(2,1)}, f32[4,4,128,128]{3,2,1,0:T(8,128)S(1)}, f32[4,128,128]{2,1,0:T(8,128)S(1)}) custom-call(s32[4]{0:T(128)S(1)} %pad_add_fusion.info, bf16[2048,512]{1,0:T(8,128)(2,1)S(1)} %copy-done.5, bf16[2048,512]{1,0:T(8,128)(2,1)} %gate_ref.1, ...), custom_call_target="tpu_custom_call" | custom-call | flops 268435456 | bytes 16007168 | tf_op jit(solution)/shard_map/grad_attn/grad_attn/pallas_call | solution.py:236
  318.5 1.3 copy-done.6
  320.7 1.5 collective-permute-start.4
  326.5 1.6 copy-done.7
  328.1 10.6 %grad_queries.1 = bf16[2048,512]{1,0:T(8,128)(2,1)} custom-call(s32[4]{0:T(128)S(1)} %pad_add_fusion.info, bf16[2048,512]{1,0:T(8,128)(2,1)S(1)} %copy-done.7, bf16[2048,512]{1,0:T(8,128)(2,1)S(1)} %copy-done.1, bf16[2048,512]{1,0:T(8,128)(2,1)} %v_ref.7, bf16[4,4,128,128]{3,2,1,0:T(8,128)(2,1)S(1)} %get-tuple-element.20.low_ref), custom_call_target="tpu_custom_call" | custom-call | flops 2147483648 | bytes 8912896 | tf_op jit(solution)/shard_map/grad_queries/grad_queries/pallas_call | solution.py:236
  338.7 1.0 select_add_fusion.into_ref
  339.8 14.2 %grad_keys_values.1 = (bf16[2048,512]{1,0:T(8,128)(2,1)}, bf16[2048,512]{1,0:T(8,128)(2,1)}) custom-call(s32[4]{0:T(128)S(1)} %pad_add_fusion.info, bf16[2048,512]{1,0:T(8,128)(2,1)S(1)} %copy-done.8, bf16[2048,512]{1,0:T(8,128)(2,1)S(1)} %copy-done.10, bf16[2048,512]{1,0:T(8,128)(2,1)} %k_ref.7, bf16[2048,512]{1,0:T(8,128)(2,1)} %v_ref.7, ...), custom_call_target="tpu_custom_call" | custom-call | flops 4294967296 | bytes 13893632 | tf_op jit(solution)/shard_map/grad_keys_values/grad_keys_values/pallas_call | solution.py:236
  (41 shorter events, 4.4 us)
Async XLA Ops:
  7.2 27.6 %all-gather.6.cloned.1.call-start = ((), (), s32[]{:S(2)}) async-start(), calls=%async_computation.1 | async-start | bytes 1310720 | tf_op jit(solution)/shard_map/all_gather | solution.py:302
  7.9 1.6 copy-start
  9.5 1.6 copy-start.2
  14.2 1.0 copy-start.11
  15.2 0.8 copy-start.15
  15.2 20.9 %copy-start.1 = (bf16[2048,512]{1,0:T(8,128)(2,1)S(1)}, bf16[2048,512]{1,0:T(8,128)(2,1)}, u32[]{:S(2)}) copy-start(bf16[2048,512]{1,0:T(8,128)(2,1)} %k_ref.7) | copy-start | bytes 6291460
  15.2 249.3 %all-gather.4.cloned.1.call-start = ((), (), s32[]{:S(2)}) async-start(), calls=%async_computation | async-start | bytes 18874368 | tf_op jit(solution)/shard_map/all_gather | solution.py:288
  36.1 1.6 copy-start.9
  37.7 1.2 copy-start.12
  264.6 13.8 %copy-start.3 = (bf16[2048,512]{1,0:T(8,128)(2,1)S(1)}, bf16[2048,512]{1,0:T(8,128)(2,1)}, u32[]{:S(2)}) copy-start(bf16[2048,512]{1,0:T(8,128)(2,1)} %gate_ref.1) | copy-start | bytes 6291460
  278.4 4.1 %copy-start.4 = (bf16[2048,512]{1,0:T(8,128)(2,1)}, bf16[2048,512]{1,0:T(8,128)(2,1)S(1)}, u32[]{:S(2)}) copy-start(bf16[2048,512]{1,0:T(8,128)(2,1)S(1)} %convolution_convert_fusion.refs_0_.mix_ref) | copy-start | bytes 6291460
  282.5 3.7 %collective-permute-start = (f32[1,2048]{1,0:T(1,128)S(1)}, f32[1,2048]{1,0:T(1,128)S(1)}, u32[]{:S(2)}, u32[]{:S(2)}) collective-permute-start(f32[1,2048]{1,0:T(1,128)S(1)} %cross.1), channel_id=1, source_target_pairs={{0,1},{1,0},{2,3},{3,2},{4,5},{5,4},{6,7},{7,6},{8,9},{9,8},{10,11... | collective-permute-start | bytes 24584 | tf_op jit(solution)/shard_map/ppermute | solution.py:257
  286.2 3.7 %collective-permute-start.1 = (f32[1,2048]{1,0:T(1,128)S(1)}, f32[1,2048]{1,0:T(1,128)S(1)}, u32[]{:S(2)}, u32[]{:S(2)}) collective-permute-start(f32[1,2048]{1,0:T(1,128)S(1)} %add.42), channel_id=1, source_target_pairs={{0,2},{1,3},{2,0},{3,1},{4,6},{5,7},{6,4},{7,5},{8,10},{9,11},{10,... | collective-permute-start | bytes 24584 | tf_op jit(solution)/shard_map/ppermute | solution.py:257
  289.9 20.0 %collective-permute-start.2 = (f32[1,2048]{1,0:T(1,128)S(1)}, f32[1,2048]{1,0:T(1,128)S(1)}, u32[]{:S(2)}, u32[]{:S(2)}) collective-permute-start(f32[1,2048]{1,0:T(1,128)S(1)} %add.43), channel_id=1, source_target_pairs={{0,4},{1,5},{2,6},{3,7},{4,0},{5,1},{6,2},{7,3},{8,12},{9,13},{10,... | collective-permute-start | bytes 24584 | tf_op jit(solution)/shard_map/ppermute | solution.py:257
  309.9 1.6 copy-start.5
  318.5 1.3 copy-start.6
  319.8 1.0 copy-start.13
  320.7 17.9 %collective-permute-start.5 = (f32[4,128,128]{2,1,0:T(8,128)S(1)}, f32[4,128,128]{2,1,0:T(8,128)S(1)}, u32[]{:S(2)}, u32[]{:S(2)}) collective-permute-start(f32[4,128,128]{2,1,0:T(8,128)S(1)} %get-tuple-element.22), channel_id=1, source_target_pairs={{0,24},{8,16},{16,8},{24,0},{1,25},{9,17},{17,9},{25,1},{2,26},{10... | collective-permute-start | bytes 786440 | tf_op jit(solution)/shard_map/ppermute | solution.py:257
  320.7 17.9 %collective-permute-start.4 = (f32[4,128,128]{2,1,0:T(8,128)S(1)}, f32[4,128,128]{2,1,0:T(8,128)S(1)}, u32[]{:S(2)}, u32[]{:S(2)}) collective-permute-start(f32[4,128,128]{2,1,0:T(8,128)S(1)} %get-tuple-element.22), channel_id=1, source_target_pairs={{0,16},{8,24},{16,0},{24,8},{1,17},{9,25},{17,1},{25,9},{2,18},{10... | collective-permute-start | bytes 786440 | tf_op jit(solution)/shard_map/ppermute | solution.py:257
  322.3 16.4 %collective-permute-start.3 = (f32[4,128,128]{2,1,0:T(8,128)S(1)}, f32[4,128,128]{2,1,0:T(8,128)}, u32[]{:S(2)}, u32[]{:S(2)}) collective-permute-start(f32[4,128,128]{2,1,0:T(8,128)S(1)} %get-tuple-element.22), channel_id=1, source_target_pairs={{0,8},{8,0},{16,24},{24,16},{1,9},{9,1},{17,25},{25,17},{2,10},{10... | collective-permute-start | bytes 786440 | tf_op jit(solution)/shard_map/ppermute | solution.py:257
  326.5 1.6 copy-start.7
  328.1 11.6 %copy-start.8 = (bf16[2048,512]{1,0:T(8,128)(2,1)S(1)}, bf16[2048,512]{1,0:T(8,128)(2,1)}, u32[]{:S(2)}) copy-start(bf16[2048,512]{1,0:T(8,128)(2,1)} %copy-done.6) | copy-start | bytes 6291460
  328.1 11.7 %copy-start.10 = (bf16[2048,512]{1,0:T(8,128)(2,1)S(1)}, bf16[2048,512]{1,0:T(8,128)(2,1)}, u32[]{:S(2)}) copy-start(bf16[2048,512]{1,0:T(8,128)(2,1)} %q_ref.5) | copy-start | bytes 6291460
  328.1 11.7 %copy-start.14 = (f32[4,4,128,128]{3,2,1,0:T(8,128)S(1)}, f32[4,4,128,128]{3,2,1,0:T(8,128)}, u32[]{:S(2)}) copy-start(f32[4,4,128,128]{3,2,1,0:T(8,128)} %copy-done.13) | copy-start | bytes 3145732
Sparse Core Ops, SparseCore 0:
  15.3 19.4 all-gather.5
  36.9 227.5 all-gather.3
where the time goes:
time: 361 us
  waiting for transfers between devices  235 us (65%)
  Pallas kernels  49.8 us (14%)
  between operations  23.2 us (6%)
  blocking collectives  18.4 us (5%)
  matrix products  13.8 us (4%)
  local copies, waits for them, and re-layouts  12.4 us (3%)
  starting transfers between devices  4.22 us (1%)
  other arithmetic  3.85 us (1%)
    all_gather x1, waiting for transfers between devices, body(): rows_all = lax.all_gather(out_grad, 'head', axis=0, tiled=True)  215 us
    pallas_call x6, Pallas kernels, call(): pl.pallas_call(kernel, grid_spec=pltpu.PrefetchScalarGridSpec(num_scalar_...  49.8 us
    psum x1, blocking collectives, body(): square = lax.psum(square, 'head')  18.4 us
    dot_general x1, matrix products, body(): lax.dot_general(rows_all, out_weight, (((1,), (1,)), ((), ())), preferred...  13.8 us
    all_gather x1, waiting for transfers between devices, body(): key_totals = lax.all_gather(key_total, 'seq')  12.9 us
    unnamed x32, local copies, waits for them, and re-layouts  12.4 us
  transfers between devices with their start and end apart: 8, of which 4 were waited for; matrix products, arithmetic and copies ran while one was open for 1% of the time, Pallas kernels for 6%

commit v1 on v0

--- a/solution.py
+++ b/solution.py
@@ -13,7 +13,10 @@
 EPS = 1e-06
 F32 = jnp.float32
 BF16 = jnp.bfloat16
-VMEM_LIMIT = 48 * 1024 * 1024
+VMEM_LIMIT = 56 * 1024 * 1024
+PROJECT_VMEM = 32 * 1024 * 1024
+SHARE = 4
+PIECES = 2
 
 
 def dot(a, b):
@@ -145,8 +148,7 @@
     gate_ref,
     attn_ref,
     q_ref,
-    square_ref,
-    cross_ref,
+    sums_ref,
     grad_ref,
     gate_grad_ref,
     after_ref,
@@ -162,9 +164,9 @@
     prior = doc_of(info, count, start - 1)
     keep_in = same(column_docs(info, count, start, BLK), prior).astype(BF16)
     carry = same(doc_of(info, count, start + BLK - 1), prior)
-    rms = jnp.sqrt(square_ref[...] / width + EPS)
+    rms = jnp.sqrt(sums_ref[0:1, :] / width + EPS)
     inverse = to_columns(1.0 / rms)
-    pull = to_columns(cross_ref[...] / (width * (rms * rms * rms)))
+    pull = to_columns(sums_ref[1:2, :] / (width * (rms * rms * rms)))
     for h in range(heads):
         at = head_slice(h)
         mix = mix_ref[:, at].astype(F32)
@@ -230,6 +232,120 @@
             dv_ref[rows, at] = dv.astype(BF16)
 
 
+def project_kernel(depth, info, own_ref, pair_ref, *refs):
+    *parts, out_ref = refs
+    rows = own_ref.shape[0]
+    side = info[0]
+    for place, ref in ((side, own_ref), (1 - side, pair_ref)):
+        total = None
+        for j, part in enumerate(parts):
+            if len(parts) == 1:
+                left = ref[...]
+            else:
+                left = ref[:, pl.ds(pl.multiple_of((info[1] ^ j) * depth, depth), depth)]
+            term = dot_nt(left, part[...])
+            total = term if total is None else total + term
+        out_ref[pl.ds(pl.multiple_of(place * rows, rows), rows), :] = total.astype(BF16)
+
+
+def project(info, own, pair, parts):
+    features, depth = parts[0].shape
+    rows = own.shape[0]
+    args = [own, pair, *parts]
+    size = sum(a.size * 2 for a in args) + 4 * rows * features
+    return pl.pallas_call(
+        functools.partial(project_kernel, depth),
+        grid_spec=pltpu.PrefetchScalarGridSpec(
+            num_scalar_prefetch=1,
+            grid=(1,),
+            in_specs=[pl.BlockSpec(a.shape, lambda i, s: (0, 0)) for a in args],
+            out_specs=pl.BlockSpec((2 * rows, features), lambda i, s: (0, 0)),
+        ),
+        out_shape=jax.ShapeDtypeStruct((2 * rows, features), BF16),
+        name="project",
+        cost_estimate=pl.CostEstimate(
+            flops=4 * rows * features * own.shape[1], bytes_accessed=size, transcendentals=0
+        ),
+        compiler_params=pltpu.CompilerParams(vmem_limit_bytes=PROJECT_VMEM),
+    )(info, *args)
+
+
+def after(arrays, *done):
+    return lax.optimization_barrier((tuple(arrays), done))[0]
+
+
+def grad_mixture(out_grad, out_weight, length, early, late):
+    n_head = lax.axis_size("head")
+    n_pairs = n_head // 2
+    rows, depth = out_grad.shape
+    width = out_weight.shape[0]
+    half = width // PIECES
+    part_depth = depth // SHARE
+    me = lax.axis_index("head")
+    side, pair = me % 2, me // 2
+    slot = lax.axis_index("seq") % SHARE
+    info = jnp.stack([side, slot]).astype(jnp.int32)
+    hops = sorted(range(1, n_pairs), key=lambda k: (bin(k).count("1"), -k))
+    order = [(0, hop) for hop in hops if hop & (hop - 1) == 0]
+    order += [(1, hop) for hop in hops[:1]]
+    order += [(0, hop) for hop in hops if hop & (hop - 1) != 0]
+    order += [(1, hop) for hop in hops[1:]]
+    waves = [order[i : i + 2] for i in range(0, len(order), 2)]
+
+    fetched = {
+        (piece, 0): lax.dynamic_slice(
+            out_weight, (piece * half, slot * part_depth), (half, part_depth)
+        )
+        for piece in range(PIECES)
+    }
+    products = []
+    shards = {}
+    own_rows = out_grad
+    pair_rows = None
+    beside = None
+    ready = ()
+    exchanged = []
+    for step in range(len(waves) + 2):
+        wave = waves[step] if step < len(waves) else []
+        sources = [fetched[(piece, hop ^ (hop & -hop))] for piece, hop in wave]
+        sources = after(sources, *ready) if ready else sources
+        landing = [
+            flip(source, "head", 2 * (hop & -hop)) for source, (piece, hop) in zip(sources, wave)
+        ]
+        if step == 0:
+            pair_rows = flip(out_grad, "head", 1)
+        previous = waves[step - 1] if 0 < step <= len(waves) else []
+        mine = [fetched[key] for key in previous]
+        mine = after(mine, *ready) if ready and mine else mine
+        across = [flip(part, "seq", 2) for part in mine]
+        beside_mine = [flip(part, "seq", 1) for part in mine]
+        if exchanged:
+            keys, mine_e, across_e, beside_e = exchanged
+            last = [flip(part, "seq", 1) for part in across_e]
+            for key, m, x, c, l in zip(keys, mine_e, across_e, beside_e, last):
+                shards[key] = [m, c, x, l]
+                product = project(info, own_rows, pair_rows, shards[key])
+                products.append((key, flip(product, "head", 2 * key[1])))
+        if step == 0:
+            extra = early()
+        elif step == 1:
+            extra = late()
+        elif step == 2:
+            extra = project(info, own_rows, pair_rows, [out_weight])
+            own_product = extra
+        else:
+            extra = ()
+        exchanged = (previous, mine, across, beside_mine) if previous else ()
+        for key, part in zip(wave, landing):
+            fetched[key] = part
+        ready = tuple(landing) + tuple(across) + tuple(jax.tree.leaves(extra))
+    mix = jnp.zeros((length, width), BF16)
+    mix = lax.dynamic_update_slice(mix, own_product, (pair * 2 * rows, 0))
+    for (piece, hop), product in products:
+        mix = lax.dynamic_update_slice(mix, product, ((pair ^ hop) * 2 * rows, piece * half))
+    return mix
+
+
 def call(kernel, name, info, args, in_specs, outs, out_specs, scratch=(), flops=0):
     nblocks = max(a.shape[0] for a in args if a.ndim == 2) // BLK
     size = sum(a.size * a.dtype.itemsize for a in list(args) + list(outs))
@@ -285,42 +401,46 @@
     unit = 2 * length * width * HEAD_DIM
     intra = 2 * length * width * BLK
 
-    rows_all = lax.all_gather(out_grad, "head", axis=0, tiled=True)
-
-    with jax.named_scope("key_states"):
-        before, key_total = call(
-            functools.partial(key_state_kernel, count, heads),
-            "key_states",
-            info,
-            [key_rows, value_rows],
-            [block, block],
-            [all_states, one_state],
-            [states, state],
-            scratch,
-            unit,
-        )
-    key_totals = lax.all_gather(key_total, "seq")
-    into = jnp.zeros((heads, HEAD_DIM, HEAD_DIM), F32)
-    for other in range(nseq):
-        takes = (other < place) & (doc_at((other + 1) * length - 1) == doc_at(first - 1))
-        into = into + jnp.where(takes, key_totals[other], 0.0)
-    with jax.named_scope("attention"):
-        attn, square, low = call(
-            functools.partial(attention_kernel, count, heads),
-            "attention",
-            info,
-            [queries, key_rows, value_rows, before, into],
-            [block, block, block, states, state],
-            [tokens32, row, low_states],
-            [block, line, states],
-            (),
-            2 * intra,
-        )
-    square = lax.psum(square, "head")
-
-    mix = lax.dot_general(
-        rows_all, out_weight, (((1,), (1,)), ((), ())), preferred_element_type=F32
-    ).astype(BF16)
+    kept = {}
+
+    def early():
+        with jax.named_scope("key_states"):
+            before, key_total = call(
+                functools.partial(key_state_kernel, count, heads),
+                "key_states",
+                info,
+                [key_rows, value_rows],
+                [block, block],
+                [all_states, one_state],
+                [states, state],
+                scratch,
+                unit,
+            )
+        key_totals = lax.all_gather(key_total, "seq")
+        into = jnp.zeros((heads, HEAD_DIM, HEAD_DIM), F32)
+        for other in range(nseq):
+            takes = (other < place) & (doc_at((other + 1) * length - 1) == doc_at(first - 1))
+            into = into + jnp.where(takes, key_totals[other], 0.0)
+        kept["before"], kept["into"] = before, into
+        return before
+
+    def late():
+        with jax.named_scope("attention"):
+            kept["attn"], kept["square"], kept["low"] = call(
+                functools.partial(attention_kernel, count, heads),
+                "attention",
+                info,
+                [queries, key_rows, value_rows, kept["before"], kept["into"]],
+                [block, block, block, states, state],
+                [tokens32, row, low_states],
+                [block, line, states],
+                (),
+                2 * intra,
+            )
+        return kept["square"]
+
+    mix = grad_mixture(out_grad, out_weight, length, early, late)
+    attn, square, low = kept["attn"], kept["square"], kept["low"]
 
     with jax.named_scope("cross"):
         cross = call(
@@ -333,22 +453,23 @@
             [line],
         )[0]
     n_head = lax.axis_size("head")
+    sums = jnp.concatenate([square, cross], axis=0)
     bit = 1
     while bit < n_head:
-        cross = cross + flip(cross, "head", bit)
+        sums = sums + flip(sums, "head", bit)
         bit *= 2
 
     back = lambda spec_shape, f: pl.BlockSpec(spec_shape, lambda b, s: f(nblocks - 1 - b))
     block_r = back((BLK, width), lambda b: (b, 0))
-    line_r = back((1, BLK), lambda b: (0, b))
+    line_r = back((2, BLK), lambda b: (0, b))
     states_r = back((1, heads, HEAD_DIM, HEAD_DIM), lambda b: (b, 0, 0, 0))
     with jax.named_scope("grad_attn"):
         grad, grad_gate, after, query_total = call(
             functools.partial(grad_attn_kernel, count, heads, full_width),
             "grad_attn",
             info,
-            [mix, gate_out, attn, queries, square, cross],
-            [block_r, block_r, block_r, block_r, line_r, line_r],
+            [mix, gate_out, attn, queries, sums],
+            [block_r, block_r, block_r, block_r, line_r],
             [tokens16, tokens16, all_states, one_state],
             [block_r, block_r, states_r, state],
             scratch,

time: 361 us -> 247 us (0.68)
  waiting for transfers between devices: 235 us -> 82.4 us
  starting transfers between devices: 4.22 us -> 40.1 us
  Pallas kernels: 49.8 us -> 84.8 us
  blocking collectives: 18.4 us -> 0 us
  matrix products: 13.8 us -> 0 us
  local copies, waits for them, and re-layouts: 12.4 us -> 8.35 us
  other arithmetic: 3.85 us -> 7.68 us
    all_gather x2 -> x1, waiting for transfers between devices: 228 us -> 0.01 us  [early(): key_totals = lax.all_gather(key_total, 'seq')]
    ppermute x6 -> x37, waiting for transfers between devices: 6.74 us -> 82.3 us  [flip(): lax.ppermute(a, axis, [(i, i ^ bit) for i in range(lax.axis_size(axis))])]
    ppermute x6 -> x37, starting transfers between devices: 4.14 us -> 40.1 us  [flip(): lax.ppermute(a, axis, [(i, i ^ bit) for i in range(lax.axis_size(axis))])]
    pallas_call x0 -> x7, Pallas kernels: none -> 27.3 us  [project(): pl.pallas_call(functools.partial(project_kernel, depth), grid_spec=pltpu....]
    psum x1 -> x0, blocking collectives: 18.4 us -> none  [body(): square = lax.psum(square, 'head')]
    dot_general x1 -> x0, matrix products: 13.8 us -> none  [body(): lax.dot_general(rows_all, out_weight, (((1,), (1,)), ((), ())), preferred...]
    pallas_call x6, Pallas kernels: 49.8 us -> 57.6 us  [call(): pl.pallas_call(kernel, grid_spec=pltpu.PrefetchScalarGridSpec(num_scalar_...]
    unnamed x32 -> x22, local copies, waits for them, and re-layouts: 12.4 us -> 5.02 us
  transfers between devices with their start and end apart: 8 -> 38, of which waited for: 4 -> 13; matrix products, arithmetic and copies ran while one was open for 1% -> 3% of each run, Pallas kernels for 6% -> 20%
where the time goes in v1:
time: 247 us; the launch traced here: 246 us
  Pallas kernels  84.8 us (34%)
  waiting for transfers between devices  82.4 us (33%)
  starting transfers between devices  40.1 us (16%)
  between operations  22.8 us (9%)
  local copies, waits for them, and re-layouts  8.35 us (3%)
  other arithmetic  7.68 us (3%)
    ppermute x37, waiting for transfers between devices, flip(): lax.ppermute(a, axis, [(i, i ^ bit) for i in range(lax.axis_size(axis))])  82.3 us
    pallas_call x6, Pallas kernels, call(): pl.pallas_call(kernel, grid_spec=pltpu.PrefetchScalarGridSpec(num_scalar_...  57.6 us
    ppermute x37, starting transfers between devices, flip(): lax.ppermute(a, axis, [(i, i ^ bit) for i in range(lax.axis_size(axis))])  40.1 us
    pallas_call x7, Pallas kernels, project(): pl.pallas_call(functools.partial(project_kernel, depth), grid_spec=pltpu....  27.3 us
    unnamed x22, local copies, waits for them, and re-layouts  5.02 us
  transfers between devices with their start and end apart: 38, of which 13 were waited for; matrix products, arithmetic and copies ran while one was open for 3% of the time, Pallas kernels for 20%

profile of v1, /device:TPU:0, one launch (start us, length us, event | category | flops | bytes accessed | tf_op | source)
XLA Modules:
  0.0 246.1 jit_solution(14645266711904296649)
XLA Ops:
  8.5 5.5 %key_states.1 = (f32[4,4,128,128]{3,2,1,0:T(8,128)}, f32[4,128,128]{2,1,0:T(8,128)}) custom-call(s32[4]{0:T(128)} %pad_add_fusion.info, bf16[2048,512]{1,0:T(8,128)(2,1)} %k_ref.7, bf16[2048,512]{1,0:T(8,128)(2,1)} %v_ref.7), custom_call_target="tpu_custom_call" | custom-call | flops 268435456 | bytes 5505024 | tf_op jit(solution)/shard_map/key_states/key_states/pallas_call | solution.py:352
  14.0 3.0 %collective-permute-start = (bf16[256,4096]{1,0:T(8,128)(2,1)S(1)}, bf16[256,4096]{1,0:T(8,128)(2,1)}, u32[]{:S(2)}, u32[]{:S(2)}) collective-permute-start(bf16[256,4096]{1,0:T(8,128)(2,1)S(1)} %copy-done), channel_id=1, source_target_pairs={{0,1},{1,0},{2,3},{3,2},{4,5},{5,4},{6,7},{7,6},{8,9},{9,8},{10,11... | collective-permute-start | bytes 6291464 | tf_op jit(solution)/shard_map/ppermute | solution.py:373
  23.3 20.4 %collective-permute-done.2.refs_0_ = bf16[256,1024]{1,0:T(8,128)(2,1)} collective-permute-done((bf16[256,1024]{1,0:T(8,128)(2,1)S(1)}, bf16[256,1024]{1,0:T(8,128)(2,1)}, u32[]{:S(2)}, u32[]{:S(2)}) %collective-permute-start.2) | collective-permute-done | bytes 524320 | tf_op jit(solution)/shard_map/ppermute | solution.py:373
  56.7 4.3 %collective-permute-done.4.refs_2_ = bf16[256,1024]{1,0:T(8,128)(2,1)} collective-permute-done((bf16[256,1024]{1,0:T(8,128)(2,1)S(1)}, bf16[256,1024]{1,0:T(8,128)(2,1)}, u32[]{:S(2)}, u32[]{:S(2)}) %collective-permute-start.4) | collective-permute-done | bytes 524320 | tf_op jit(solution)/shard_map/ppermute | solution.py:373
  62.9 11.8 %attention.1 = (f32[2048,512]{1,0:T(8,128)}, f32[1,2048]{1,0:T(1,128)}, bf16[4,4,128,128]{3,2,1,0:T(8,128)(2,1)}) custom-call(s32[4]{0:T(128)} %pad_add_fusion.info, bf16[2048,512]{1,0:T(8,128)(2,1)} %q_ref.5, bf16[2048,512]{1,0:T(8,128)(2,1)} %k_ref.7, bf16[2048,512]{1,0:T(8,128)(2,1)} %v_ref.7, f32[4,4,128,128]{3,2,1,0:T(8,128)} %get-tuple-element.25.before_ref, ...), custom_call_target="tpu_custom_call" | custom-call | flops 2147483648 | bytes 12328960 | tf_op jit(solution)/shard_map/attention/attention/pallas_call | solution.py:352
  78.9 11.0 %collective-permute-done.14.refs_2_ = bf16[256,1024]{1,0:T(8,128)(2,1)} collective-permute-done((bf16[256,1024]{1,0:T(8,128)(2,1)}, bf16[256,1024]{1,0:T(8,128)(2,1)}, u32[]{:S(2)}, u32[]{:S(2)}) %collective-permute-start.14) | collective-permute-done | bytes 524320 | tf_op jit(solution)/shard_map/ppermute | solution.py:373
  89.9 10.9 %collective-permute-done.18.refs_2_ = bf16[256,1024]{1,0:T(8,128)(2,1)} collective-permute-done((bf16[256,1024]{1,0:T(8,128)(2,1)S(1)}, bf16[256,1024]{1,0:T(8,128)(2,1)}, u32[]{:S(2)}, u32[]{:S(2)}) %collective-permute-start.18) | collective-permute-done | bytes 524320 | tf_op jit(solution)/shard_map/ppermute | solution.py:373
  104.5 4.5 %project.7 = bf16[512,512]{1,0:T(8,128)(2,1)S(1)} custom-call(s32[2]{0:T(128)S(1)} %pad_add_fusion.1.info, bf16[256,4096]{1,0:T(8,128)(2,1)S(1)} %copy-done, bf16[256,4096]{1,0:T(8,128)(2,1)} %collective-permute-done.pair_ref, bf16[512,4096]{1,0:T(8,128)(2,1)S(1)} %copy-done.1), custom_call_target="tpu_custom_call" | custom-call | flops 2147483648 | bytes 8912896 | tf_op jit(solution)/shard_map/project/pallas_call | solution.py:256
  111.1 3.8 %project.8 = bf16[512,256]{1,0:T(8,128)(2,1)S(1)} custom-call(s32[2]{0:T(128)S(1)} %pad_add_fusion.1.info, bf16[256,4096]{1,0:T(8,128)(2,1)S(1)} %copy-done, bf16[256,4096]{1,0:T(8,128)(2,1)} %collective-permute-done.pair_ref, bf16[256,1024]{1,0:T(8,128)(2,1)S(1)} %copy-done.3, bf16[256,1024]{1,0:T(8,128)(2,1)} %collective-permute-done.3.refs_1_, ...), custom_call_target="tpu_custom_call" | custom-call | flops 1073741824 | bytes 6553600 | tf_op jit(solution)/shard_map/project/pallas_call | solution.py:256
  116.3 4.0 %project.9 = bf16[512,256]{1,0:T(8,128)(2,1)S(1)} custom-call(s32[2]{0:T(128)S(1)} %pad_add_fusion.1.info, bf16[256,4096]{1,0:T(8,128)(2,1)S(1)} %copy-done, bf16[256,4096]{1,0:T(8,128)(2,1)} %collective-permute-done.pair_ref, bf16[256,1024]{1,0:T(8,128)(2,1)} %collective-permute-done.2.refs_0_, bf16[256,1024]{1,0:T(8,128)(2,1)} %collective-permute-done.7.refs_1_, ...), custom_call_target="tpu_custom_call" | custom-call | flops 1073741824 | bytes 6553600 | tf_op jit(solution)/shard_map/project/pallas_call | solution.py:256
  122.8 7.4 %collective-permute-done.6 = bf16[512,256]{1,0:T(8,128)(2,1)S(1)} collective-permute-done((bf16[512,256]{1,0:T(8,128)(2,1)S(1)}, bf16[512,256]{1,0:T(8,128)(2,1)S(1)}, u32[]{:S(2)}, u32[]{:S(2)}) %collective-permute-start.6) | collective-permute-done | bytes 262176 | tf_op jit(solution)/shard_map/ppermute | solution.py:373
  130.9 4.2 %collective-permute-done.10 = bf16[512,256]{1,0:T(8,128)(2,1)} collective-permute-done((bf16[512,256]{1,0:T(8,128)(2,1)S(1)}, bf16[512,256]{1,0:T(8,128)(2,1)}, u32[]{:S(2)}, u32[]{:S(2)}) %collective-permute-start.10) | collective-permute-done | bytes 262176 | tf_op jit(solution)/shard_map/ppermute | solution.py:373
  137.5 4.0 %project.10 = bf16[512,256]{1,0:T(8,128)(2,1)S(1)} custom-call(s32[2]{0:T(128)S(1)} %pad_add_fusion.1.info, bf16[256,4096]{1,0:T(8,128)(2,1)S(1)} %copy-done, bf16[256,4096]{1,0:T(8,128)(2,1)} %collective-permute-done.pair_ref, bf16[256,1024]{1,0:T(8,128)(2,1)} %collective-permute-done.11.refs_0_, bf16[256,1024]{1,0:T(8,128)(2,1)} %collective-permute-done.13.refs_1_, ...), custom_call_target="tpu_custom_call" | custom-call | flops 1073741824 | bytes 6553600 | tf_op jit(solution)/shard_map/project/pallas_call | solution.py:256
  141.6 3.7 %project.11 = bf16[512,256]{1,0:T(8,128)(2,1)S(1)} custom-call(s32[2]{0:T(128)S(1)} %pad_add_fusion.1.info, bf16[256,4096]{1,0:T(8,128)(2,1)S(1)} %copy-done, bf16[256,4096]{1,0:T(8,128)(2,1)} %collective-permute-done.pair_ref, bf16[256,1024]{1,0:T(8,128)(2,1)S(1)} %collective-permute-done.12.refs_0_, bf16[256,1024]{1,0:T(8,128)(2,1)S(1)} %copy-done.5, ...), custom_call_target="tpu_custom_call" | custom-call | flops 1073741824 | bytes 6553600 | tf_op jit(solution)/shard_map/project/pallas_call | solution.py:256
  147.1 3.7 %project.12 = bf16[512,256]{1,0:T(8,128)(2,1)S(1)} custom-call(s32[2]{0:T(128)S(1)} %pad_add_fusion.1.info, bf16[256,4096]{1,0:T(8,128)(2,1)S(1)} %copy-done, bf16[256,4096]{1,0:T(8,128)(2,1)} %collective-permute-done.pair_ref, bf16[256,1024]{1,0:T(8,128)(2,1)} %collective-permute-done.21.refs_0_, bf16[256,1024]{1,0:T(8,128)(2,1)S(1)} %collective-permute-done.23.refs_1_, ...), custom_call_target="tpu_custom_call" | custom-call | flops 1073741824 | bytes 6553600 | tf_op jit(solution)/shard_map/project/pallas_call | solution.py:256
  152.5 3.7 %project.13 = bf16[512,256]{1,0:T(8,128)(2,1)S(1)} custom-call(s32[2]{0:T(128)S(1)} %pad_add_fusion.1.info, bf16[256,4096]{1,0:T(8,128)(2,1)S(1)} %copy-done, bf16[256,4096]{1,0:T(8,128)(2,1)} %collective-permute-done.pair_ref, bf16[256,1024]{1,0:T(8,128)(2,1)} %collective-permute-done.22.refs_0_, bf16[256,1024]{1,0:T(8,128)(2,1)S(1)} %collective-permute-done.27.refs_1_, ...), custom_call_target="tpu_custom_call" | custom-call | flops 1073741824 | bytes 6553600 | tf_op jit(solution)/shard_map/project/pallas_call | solution.py:256
  157.8 4.0 %collective-permute-done.16 = bf16[512,256]{1,0:T(8,128)(2,1)S(1)} collective-permute-done((bf16[512,256]{1,0:T(8,128)(2,1)S(1)}, bf16[512,256]{1,0:T(8,128)(2,1)S(1)}, u32[]{:S(2)}, u32[]{:S(2)}) %collective-permute-start.16) | collective-permute-done | bytes 262176 | tf_op jit(solution)/shard_map/ppermute | solution.py:373
  161.9 10.2 %collective-permute-done.26 = bf16[512,256]{1,0:T(8,128)(2,1)S(1)} collective-permute-done((bf16[512,256]{1,0:T(8,128)(2,1)S(1)}, bf16[512,256]{1,0:T(8,128)(2,1)S(1)}, u32[]{:S(2)}, u32[]{:S(2)}) %collective-permute-start.26) | collective-permute-done | bytes 262176 | tf_op jit(solution)/shard_map/ppermute | solution.py:373
  173.5 5.7 %cross.1 = f32[1,2048]{1,0:T(1,128)} custom-call(s32[4]{0:T(128)} %pad_add_fusion.info, bf16[2048,512]{1,0:T(8,128)(2,1)} %copy-done.6, bf16[2048,512]{1,0:T(8,128)(2,1)} %gate_ref.1, f32[2048,512]{1,0:T(8,128)} %get-tuple-element.38.refs_2_.attn_ref), custom_call_target="tpu_custom_call" | custom-call | bytes 8396800 | tf_op jit(solution)/shard_map/cross/cross/pallas_call | solution.py:352
  180.5 3.2 %collective-permute-done.31 = f32[2,2048]{1,0:T(2,128)S(1)} collective-permute-done((f32[2,2048]{1,0:T(2,128)S(1)}, f32[2,2048]{1,0:T(2,128)S(1)}, u32[]{:S(2)}, u32[]{:S(2)}) %collective-permute-start.31) | collective-permute-done | bytes 16416 | tf_op jit(solution)/shard_map/ppermute | solution.py:373
  184.5 6.2 %collective-permute-start.32 = (f32[2,2048]{1,0:T(2,128)S(1)}, f32[2,2048]{1,0:T(2,128)S(1)}, u32[]{:S(2)}, u32[]{:S(2)}) collective-permute-start(f32[2,2048]{1,0:T(2,128)S(1)} %fusion.12), channel_id=1, source_target_pairs={{0,2},{1,3},{2,0},{3,1},{4,6},{5,7},{6,4},{7,5},{8,10},{9,11},{10,... | collective-permute-start | bytes 49160 | tf_op jit(solution)/shard_map/ppermute | solution.py:373
  198.5 8.6 %grad_attn.1 = (bf16[2048,512]{1,0:T(8,128)(2,1)}, bf16[2048,512]{1,0:T(8,128)(2,1)}, f32[4,4,128,128]{3,2,1,0:T(8,128)}, f32[4,128,128]{2,1,0:T(8,128)}) custom-call(s32[4]{0:T(128)} %pad_add_fusion.info, bf16[2048,512]{1,0:T(8,128)(2,1)} %copy-done.6, bf16[2048,512]{1,0:T(8,128)(2,1)} %gate_ref.1, f32[2048,512]{1,0:T(8,128)} %get-tuple-element.38.refs_2_.attn_ref, ...), custom_call_target="tpu_custom_call" | custom-call | flops 268435456 | bytes 16007168 | tf_op jit(solution)/shard_map/grad_attn/grad_attn/pallas_call | solution.py:352
  212.6 10.8 %grad_queries.1 = bf16[2048,512]{1,0:T(8,128)(2,1)} custom-call(s32[4]{0:T(128)} %pad_add_fusion.info, bf16[2048,512]{1,0:T(8,128)(2,1)} %get-tuple-element.39.grad_ref, bf16[2048,512]{1,0:T(8,128)(2,1)} %k_ref.7, bf16[2048,512]{1,0:T(8,128)(2,1)} %v_ref.7, bf16[4,4,128,128]{3,2,1,0:T(8,128)(2,1)} %get-tuple-element.40.low_ref), custom_call_target="tpu_custom_call" | custom-call | flops 2147483648 | bytes 8912896 | tf_op jit(solution)/shard_map/grad_queries/grad_queries/pallas_call | solution.py:352
  224.2 15.1 %grad_keys_values.1 = (bf16[2048,512]{1,0:T(8,128)(2,1)}, bf16[2048,512]{1,0:T(8,128)(2,1)}) custom-call(s32[4]{0:T(128)} %pad_add_fusion.info, bf16[2048,512]{1,0:T(8,128)(2,1)} %get-tuple-element.39.grad_ref, bf16[2048,512]{1,0:T(8,128)(2,1)} %q_ref.5, bf16[2048,512]{1,0:T(8,128)(2,1)} %k_ref.7, bf16[2048,512]{1,0:T(8,128)(2,1)} %v_ref.7, ...), custom_call_target="tpu_custom_call" | custom-call | flops 4294967296 | bytes 13893632 | tf_op jit(solution)/shard_map/grad_keys_values/grad_keys_values/pallas_call | solution.py:352
  (106 shorter events, 53.7 us)
Async XLA Ops:
  7.2 53.8 %all-gather.3.cloned.1.call-start = ((), (), s32[]{:S(2)}) async-start(), calls=%async_computation | async-start | bytes 1310720 | tf_op jit(solution)/shard_map/all_gather | solution.py:419
  14.0 64.9 %collective-permute-start = (bf16[256,4096]{1,0:T(8,128)(2,1)S(1)}, bf16[256,4096]{1,0:T(8,128)(2,1)}, u32[]{:S(2)}, u32[]{:S(2)}) collective-permute-start(bf16[256,4096]{1,0:T(8,128)(2,1)S(1)} %copy-done), channel_id=1, source_target_pairs={{0,1},{1,0},{2,3},{3,2},{4,5},{5,4},{6,7},{7,6},{8,9},{9,8},{10,11... | collective-permute-start | bytes 6291464 | tf_op jit(solution)/shard_map/ppermute | solution.py:373
  19.1 24.6 %collective-permute-start.2 = (bf16[256,1024]{1,0:T(8,128)(2,1)S(1)}, bf16[256,1024]{1,0:T(8,128)(2,1)}, u32[]{:S(2)}, u32[]{:S(2)}) collective-permute-start(bf16[256,1024]{1,0:T(8,128)(2,1)S(1)} %get-tuple-element.56), channel_id=1, source_target_pairs={{0,2},{1,3},{2,0},{3,1},{4,6},{5,7},{6,4},{7,5},{8,10},{9,11},{10,... | collective-permute-start | bytes 1572872 | tf_op jit(solution)/shard_map/ppermute | solution.py:373
  20.7 25.3 %collective-permute-start.1 = (bf16[256,1024]{1,0:T(8,128)(2,1)S(1)}, bf16[256,1024]{1,0:T(8,128)(2,1)S(1)}, u32[]{:S(2)}, u32[]{:S(2)}) collective-permute-start(bf16[256,1024]{1,0:T(8,128)(2,1)S(1)} %get-tuple-element.56), channel_id=1, source_target_pairs={{0,4},{1,5},{2,6},{3,7},{4,0},{5,1},{6,2},{7,3},{8,12},{9,13},{10,... | collective-permute-start | bytes 1572872 | tf_op jit(solution)/shard_map/ppermute | solution.py:373
  47.5 27.3 %collective-permute-start.8 = (bf16[256,1024]{1,0:T(8,128)(2,1)}, bf16[256,1024]{1,0:T(8,128)(2,1)}, u32[]{:S(2)}, u32[]{:S(2)}) collective-permute-start(bf16[256,1024]{1,0:T(8,128)(2,1)} %collective-permute-done.2.refs_0_), channel_id=1, source_target_pairs={{0,16},{8,24},{16,0},{24,8},{1,17},{9,25},{17,1},{25,9},{2,18},{10... | collective-permute-start | bytes 1572872 | tf_op jit(solution)/shard_map/ppermute | solution.py:373
  48.0 26.8 %collective-permute-start.11 = (bf16[256,1024]{1,0:T(8,128)(2,1)}, bf16[256,1024]{1,0:T(8,128)(2,1)}, u32[]{:S(2)}, u32[]{:S(2)}) collective-permute-start(bf16[256,1024]{1,0:T(8,128)(2,1)} %get-tuple-element.34), channel_id=1, source_target_pairs={{0,4},{1,5},{2,6},{3,7},{4,0},{5,1},{6,2},{7,3},{8,12},{9,13},{10,... | collective-permute-start | bytes 1572872 | tf_op jit(solution)/shard_map/ppermute | solution.py:373
  48.3 26.4 %collective-permute-start.12 = (bf16[256,1024]{1,0:T(8,128)(2,1)S(1)}, bf16[256,1024]{1,0:T(8,128)(2,1)S(1)}, u32[]{:S(2)}, u32[]{:S(2)}) collective-permute-start(bf16[256,1024]{1,0:T(8,128)(2,1)S(1)} %collective-permute-done.1.refs_0_), channel_id=1, source_target_pairs={{0,2},{1,3},{2,0},{3,1},{4,6},{5,7},{6,4},{7,5},{8,10},{9,11},{10,... | collective-permute-start | bytes 1572872 | tf_op jit(solution)/shard_map/ppermute | solution.py:373
  60.9 16.4 %collective-permute-start.3 = (bf16[256,1024]{1,0:T(8,128)(2,1)S(1)}, bf16[256,1024]{1,0:T(8,128)(2,1)}, u32[]{:S(2)}, u32[]{:S(2)}) collective-permute-start(bf16[256,1024]{1,0:T(8,128)(2,1)S(1)} %collective-permute-done.1.refs_0_), channel_id=1, source_target_pairs={{0,8},{8,0},{16,24},{24,16},{1,9},{9,1},{17,25},{25,17},{2,10},{10... | collective-permute-start | bytes 1572872 | tf_op jit(solution)/shard_map/ppermute | solution.py:373
  76.4 24.4 %collective-permute-start.18 = (bf16[256,1024]{1,0:T(8,128)(2,1)S(1)}, bf16[256,1024]{1,0:T(8,128)(2,1)}, u32[]{:S(2)}, u32[]{:S(2)}) collective-permute-start(bf16[256,1024]{1,0:T(8,128)(2,1)S(1)} %collective-permute-done.12.refs_0_), channel_id=1, source_target_pairs={{0,16},{8,24},{16,0},{24,8},{1,17},{9,25},{17,1},{25,9},{2,18},{10... | collective-permute-start | bytes 1572872 | tf_op jit(solution)/shard_map/ppermute | solution.py:373
  76.9 23.9 %collective-permute-start.21 = (bf16[256,1024]{1,0:T(8,128)(2,1)}, bf16[256,1024]{1,0:T(8,128)(2,1)}, u32[]{:S(2)}, u32[]{:S(2)}) collective-permute-start(bf16[256,1024]{1,0:T(8,128)(2,1)} %get-tuple-element.34), channel_id=1, source_target_pairs={{0,2},{1,3},{2,0},{3,1},{4,6},{5,7},{6,4},{7,5},{8,10},{9,11},{10,... | collective-permute-start | bytes 1572872 | tf_op jit(solution)/shard_map/ppermute | solution.py:373
  77.3 24.9 %collective-permute-start.22 = (bf16[256,1024]{1,0:T(8,128)(2,1)}, bf16[256,1024]{1,0:T(8,128)(2,1)}, u32[]{:S(2)}, u32[]{:S(2)}) collective-permute-start(bf16[256,1024]{1,0:T(8,128)(2,1)} %collective-permute-done.11.refs_0_), channel_id=1, source_target_pairs={{0,2},{1,3},{2,0},{3,1},{4,6},{5,7},{6,4},{7,5},{8,10},{9,11},{10,... | collective-permute-start | bytes 1572872 | tf_op jit(solution)/shard_map/ppermute | solution.py:373
  78.9 30.1 %collective-permute-start.7 = (bf16[256,1024]{1,0:T(8,128)(2,1)}, bf16[256,1024]{1,0:T(8,128)(2,1)}, u32[]{:S(2)}, u32[]{:S(2)}) collective-permute-start(bf16[256,1024]{1,0:T(8,128)(2,1)} %collective-permute-done.2.refs_0_), channel_id=1, source_target_pairs={{0,8},{8,0},{16,24},{24,16},{1,9},{9,1},{17,25},{25,17},{2,10},{10... | collective-permute-start | bytes 1572872 | tf_op jit(solution)/shard_map/ppermute | solution.py:373
  89.9 20.7 %collective-permute-start.5 = (bf16[256,1024]{1,0:T(8,128)(2,1)}, bf16[256,1024]{1,0:T(8,128)(2,1)}, u32[]{:S(2)}, u32[]{:S(2)}) collective-permute-start(bf16[256,1024]{1,0:T(8,128)(2,1)} %collective-permute-done.4.refs_2_), channel_id=1, source_target_pairs={{0,8},{8,0},{16,24},{24,16},{1,9},{9,1},{17,25},{25,17},{2,10},{10... | collective-permute-start | bytes 1572872 | tf_op jit(solution)/shard_map/ppermute | solution.py:373
  102.2 18.1 %collective-permute-start.17 = (bf16[256,1024]{1,0:T(8,128)(2,1)S(1)}, bf16[256,1024]{1,0:T(8,128)(2,1)S(1)}, u32[]{:S(2)}, u32[]{:S(2)}) collective-permute-start(bf16[256,1024]{1,0:T(8,128)(2,1)S(1)} %collective-permute-done.12.refs_0_), channel_id=1, source_target_pairs={{0,8},{8,0},{16,24},{24,16},{1,9},{9,1},{17,25},{25,17},{2,10},{10... | collective-permute-start | bytes 1572872 | tf_op jit(solution)/shard_map/ppermute | solution.py:373
  109.0 26.2 %collective-permute-start.24 = (bf16[256,1024]{1,0:T(8,128)(2,1)}, bf16[256,1024]{1,0:T(8,128)(2,1)}, u32[]{:S(2)}, u32[]{:S(2)}) collective-permute-start(bf16[256,1024]{1,0:T(8,128)(2,1)} %collective-permute-done.21.refs_0_), channel_id=1, source_target_pairs={{0,16},{8,24},{16,0},{24,8},{1,17},{9,25},{17,1},{25,9},{2,18},{10... | collective-permute-start | bytes 1572872 | tf_op jit(solution)/shard_map/ppermute | solution.py:373
  110.6 25.4 %collective-permute-start.28 = (bf16[256,1024]{1,0:T(8,128)(2,1)}, bf16[256,1024]{1,0:T(8,128)(2,1)}, u32[]{:S(2)}, u32[]{:S(2)}) collective-permute-start(bf16[256,1024]{1,0:T(8,128)(2,1)} %collective-permute-done.22.refs_0_), channel_id=1, source_target_pairs={{0,16},{8,24},{16,0},{24,8},{1,17},{9,25},{17,1},{25,9},{2,18},{10... | collective-permute-start | bytes 1572872 | tf_op jit(solution)/shard_map/ppermute | solution.py:373
  111.1 24.8 %collective-permute-start.15 = (bf16[256,1024]{1,0:T(8,128)(2,1)}, bf16[256,1024]{1,0:T(8,128)(2,1)}, u32[]{:S(2)}, u32[]{:S(2)}) collective-permute-start(bf16[256,1024]{1,0:T(8,128)(2,1)} %collective-permute-done.14.refs_2_), channel_id=1, source_target_pairs={{0,8},{8,0},{16,24},{24,16},{1,9},{9,1},{17,25},{25,17},{2,10},{10... | collective-permute-start | bytes 1572872 | tf_op jit(solution)/shard_map/ppermute | solution.py:373
  135.9 16.6 %collective-permute-start.27 = (bf16[256,1024]{1,0:T(8,128)(2,1)}, bf16[256,1024]{1,0:T(8,128)(2,1)S(1)}, u32[]{:S(2)}, u32[]{:S(2)}) collective-permute-start(bf16[256,1024]{1,0:T(8,128)(2,1)} %collective-permute-done.22.refs_0_), channel_id=1, source_target_pairs={{0,8},{8,0},{16,24},{24,16},{1,9},{9,1},{17,25},{25,17},{2,10},{10... | collective-permute-start | bytes 1572872 | tf_op jit(solution)/shard_map/ppermute | solution.py:373
  136.0 16.6 %collective-permute-start.29 = (bf16[256,1024]{1,0:T(8,128)(2,1)}, bf16[256,1024]{1,0:T(8,128)(2,1)S(1)}, u32[]{:S(2)}, u32[]{:S(2)}) collective-permute-start(bf16[256,1024]{1,0:T(8,128)(2,1)} %collective-permute-done.28.refs_2_), channel_id=1, source_target_pairs={{0,8},{8,0},{16,24},{24,16},{1,9},{9,1},{17,25},{25,17},{2,10},{10... | collective-permute-start | bytes 1572872 | tf_op jit(solution)/shard_map/ppermute | solution.py:373
  141.5 20.3 %collective-permute-start.16 = (bf16[512,256]{1,0:T(8,128)(2,1)S(1)}, bf16[512,256]{1,0:T(8,128)(2,1)S(1)}, u32[]{:S(2)}, u32[]{:S(2)}) collective-permute-start(bf16[512,256]{1,0:T(8,128)(2,1)S(1)} %project.10), channel_id=1, source_target_pairs={{0,4},{1,5},{2,6},{3,7},{4,0},{5,1},{6,2},{7,3},{8,12},{9,13},{10,... | collective-permute-start | bytes 786440 | tf_op jit(solution)/shard_map/ppermute | solution.py:373
  145.3 16.6 %collective-permute-start.20 = (bf16[512,256]{1,0:T(8,128)(2,1)S(1)}, bf16[512,256]{1,0:T(8,128)(2,1)S(1)}, u32[]{:S(2)}, u32[]{:S(2)}) collective-permute-start(bf16[512,256]{1,0:T(8,128)(2,1)S(1)} %project.11), channel_id=1, source_target_pairs={{0,6},{1,7},{2,4},{3,5},{4,2},{5,3},{6,0},{7,1},{8,14},{9,15},{10,... | collective-permute-start | bytes 786440 | tf_op jit(solution)/shard_map/ppermute | solution.py:373
  150.8 21.3 %collective-permute-start.26 = (bf16[512,256]{1,0:T(8,128)(2,1)S(1)}, bf16[512,256]{1,0:T(8,128)(2,1)S(1)}, u32[]{:S(2)}, u32[]{:S(2)}) collective-permute-start(bf16[512,256]{1,0:T(8,128)(2,1)S(1)} %project.12), channel_id=1, source_target_pairs={{0,2},{1,3},{2,0},{3,1},{4,6},{5,7},{6,4},{7,5},{8,10},{9,11},{10,... | collective-permute-start | bytes 786440 | tf_op jit(solution)/shard_map/ppermute | solution.py:373
  207.0 16.3 %collective-permute-start.36 = (f32[4,128,128]{2,1,0:T(8,128)}, f32[4,128,128]{2,1,0:T(8,128)S(1)}, u32[]{:S(2)}, u32[]{:S(2)}) collective-permute-start(f32[4,128,128]{2,1,0:T(8,128)} %get-tuple-element.42), channel_id=1, source_target_pairs={{0,24},{8,16},{16,8},{24,0},{1,25},{9,17},{17,9},{25,1},{2,26},{10... | collective-permute-start | bytes 786440 | tf_op jit(solution)/shard_map/ppermute | solution.py:373
  207.1 16.3 %collective-permute-start.35 = (f32[4,128,128]{2,1,0:T(8,128)}, f32[4,128,128]{2,1,0:T(8,128)S(1)}, u32[]{:S(2)}, u32[]{:S(2)}) collective-permute-start(f32[4,128,128]{2,1,0:T(8,128)} %get-tuple-element.42), channel_id=1, source_target_pairs={{0,16},{8,24},{16,0},{24,8},{1,17},{9,25},{17,1},{25,9},{2,18},{10... | collective-permute-start | bytes 786440 | tf_op jit(solution)/shard_map/ppermute | solution.py:373
  (25 other events, 261.9 us)
Sparse Core Ops, SparseCore 0:
  14.2 19.4 all-gather.2

commit v2 on v1

v2 whole, which is shorter than its diff:
```python
import functools

import jax
import jax.numpy as jnp
from jax import lax
from jax.experimental import pallas as pl
from jax.experimental.pallas import tpu as pltpu
from jax.sharding import PartitionSpec as P

HEAD_DIM = 128
BLK = 512
CHUNK = 256
EPS = 1e-06
F32 = jnp.float32
BF16 = jnp.bfloat16
VMEM_LIMIT = 16 * 1024 * 1024
PROJECT_VMEM = 24 * 1024 * 1024
PIECES = 2
COST_SCALE = 1.15e9


def dot(a, b):
    return lax.dot_general(a, b, (((1,), (0,)), ((), ())), preferred_element_type=F32)


def dot_nt(a, b):
    return lax.dot_general(a, b, (((1,), (1,)), ((), ())), preferred_element_type=F32)


def dot_tn(a, b):
    return lax.dot_general(a, b, (((0,), (0,)), ((), ())), preferred_element_type=F32)


def doc_of(info, count, pos):
    total = jnp.zeros_like(pos)
    for i in range(count):
        total = total + jnp.where(info[i] <= pos, 1, 0)
    return total


def same(a, b):
    return jnp.where(a == b, F32(1.0), F32(0.0))


def column_docs(info, count, start, size):
    return doc_of(info, count, start + lax.broadcasted_iota(jnp.int32, (size, 1), 0))


def row_docs(info, count, start, size):
    return doc_of(info, count, start + lax.broadcasted_iota(jnp.int32, (1, size), 1))


def causal_mask(info, count, start, transposed):
    down = lax.broadcasted_iota(jnp.int32, (CHUNK, CHUNK), 0)
    over = lax.broadcasted_iota(jnp.int32, (CHUNK, CHUNK), 1)
    equal = column_docs(info, count, start, CHUNK) == row_docs(info, count, start, CHUNK)
    return equal & ((down <= over) if transposed else (over <= down))


def chunk_rows(r):
    return slice(r * CHUNK, (r + 1) * CHUNK)


def lane_sums(x):
    return jnp.sum(x.T, axis=0, keepdims=True)


def to_columns(row):
    return jnp.broadcast_to(row, (HEAD_DIM, row.shape[1])).T


def head_slice(h):
    return slice(h * HEAD_DIM, (h + 1) * HEAD_DIM)


def key_state_kernel(count, heads, info, k_ref, v_ref, before_ref, total_ref, state):
    b = pl.program_id(0)

    @pl.when(b == 0)
    def _():
        state[...] = jnp.zeros_like(state)

    for r in range(BLK // CHUNK):
        rows = chunk_rows(r)
        start = info[count] + b * BLK + r * CHUNK
        last_doc = doc_of(info, count, start + CHUNK - 1)
        keep_out = same(column_docs(info, count, start, CHUNK), last_doc).astype(BF16)
        carry = same(doc_of(info, count, start - 1), last_doc)
        for h in range(heads):
            at = head_slice(h)
            before_ref[r, h] = state[h]
            state[h] = dot_tn(k_ref[rows, at] * keep_out, v_ref[rows, at]) + carry * state[h]
    total_ref[...] = state[...]


def attention_kernel(
    count, heads, info, q_ref, k_ref, v_ref, before_ref, into_ref, attn_ref, square_ref, low_ref
):
    first = info[count]
    for r in range(BLK // CHUNK):
        rows = chunk_rows(r)
        start = first + pl.program_id(0) * BLK + r * CHUNK
        prior = doc_of(info, count, start - 1)
        carry = same(prior, doc_of(info, count, first - 1))
        mask = causal_mask(info, count, start, False)
        keep_in = same(column_docs(info, count, start, CHUNK), prior)
        squares = jnp.zeros((CHUNK, HEAD_DIM), F32)
        for h in range(heads):
            at = head_slice(h)
            low = (before_ref[r, h] + carry * into_ref[h]).astype(BF16)
            low_ref[r, h] = low
            q = q_ref[rows, at]
            probs = jnp.where(mask, dot_nt(q, k_ref[rows, at]), 0.0).astype(BF16)
            out = keep_in * dot(q, low) + dot(probs, v_ref[rows, at])
            attn_ref[rows, at] = out
            squares = squares + out * out
        square_ref[:, rows] = lane_sums(squares)


def mix_heads(heads, info, near_ref, far_ref):
    core = info[info.shape[0] - 1]
    half = heads // 2
    for index, ref in enumerate((near_ref, far_ref)):
        for i in range(half):
            h = (core ^ index) * half + i
            at = pl.ds(pl.multiple_of(h * HEAD_DIM, HEAD_DIM), HEAD_DIM)
            yield ref.at[:, head_slice(i)], at


def cross_kernel(heads, info, near_ref, far_ref, gate_ref, attn_ref, cross_ref):
    total = jnp.zeros((BLK, HEAD_DIM), F32)
    for mix, at in mix_heads(heads, info, near_ref, far_ref):
        total = total + mix[...].astype(F32) * gate_ref[:, at].astype(F32) * attn_ref[:, at]
    cross_ref[...] = lane_sums(total)


def grad_attn_kernel(
    count,
    heads,
    width,
    info,
    near_ref,
    far_ref,
    gate_ref,
    attn_ref,
    q_ref,
    sums_ref,
    grad_ref,
    gate_grad_ref,
    after_ref,
    total_ref,
    state,
):
    @pl.when(pl.program_id(0) == 0)
    def _():
        state[...] = jnp.zeros_like(state)

    b = pl.num_programs(0) - 1 - pl.program_id(0)
    rms = jnp.sqrt(sums_ref[0:1, :] / width + EPS)
    inverse = to_columns(1.0 / rms)
    pull = to_columns(sums_ref[1:2, :] / (width * (rms * rms * rms)))
    for r in reversed(range(BLK // CHUNK)):
        rows = chunk_rows(r)
        start = info[count] + b * BLK + r * CHUNK
        prior = doc_of(info, count, start - 1)
        keep_in = same(column_docs(info, count, start, CHUNK), prior).astype(BF16)
        carry = same(doc_of(info, count, start + CHUNK - 1), prior)
        half = heads // 2
        for i, (mix, at) in enumerate(mix_heads(heads, info, near_ref, far_ref)):
            h = (info[count + 1] ^ (i // half)) * half + i % half
            scaled = mix[rows].astype(F32) * inverse[rows]
            attn = attn_ref[rows, at]
            gate_grad_ref[rows, at] = (scaled * attn).astype(BF16)
            grad = (scaled * gate_ref[rows, at].astype(F32) - attn * pull[rows]).astype(BF16)
            grad_ref[rows, at] = grad
            after_ref[r, h] = state[h]
            state[h] = dot_tn(q_ref[rows, at] * keep_in, grad) + carry * state[h]
    total_ref[...] = state[...]


def grad_query_kernel(count, heads, info, grad_ref, k_ref, v_ref, low_ref, out_ref):
    for r in range(BLK // CHUNK):
        rows = chunk_rows(r)
        start = info[count] + pl.program_id(0) * BLK + r * CHUNK
        prior = doc_of(info, count, start - 1)
        mask = causal_mask(info, count, start, False)
        keep_in = same(column_docs(info, count, start, CHUNK), prior)
        for h in range(heads):
            at = head_slice(h)
            grad = grad_ref[rows, at]
            dprob = jnp.where(mask, dot_nt(grad, v_ref[rows, at]), 0.0).astype(BF16)
            out = keep_in * dot_nt(grad, low_ref[r, h]) + dot(dprob, k_ref[rows, at])
            out_ref[rows, at] = out.astype(BF16)


def grad_key_value_kernel(
    count, heads, length, info, grad_ref, q_ref, k_ref, v_ref, after_ref, into_ref, dk_ref, dv_ref
):
    first = info[count]
    for r in range(BLK // CHUNK):
        rows = chunk_rows(r)
        start = first + pl.program_id(0) * BLK + r * CHUNK
        last_doc = doc_of(info, count, start + CHUNK - 1)
        carry = same(last_doc, doc_of(info, count, first + length - 1))
        mask = causal_mask(info, count, start, True)
        keep_out = same(column_docs(info, count, start, CHUNK), last_doc)
        for h in range(heads):
            at = head_slice(h)
            low = (after_ref[r, h] + carry * into_ref[h]).astype(BF16)
            k, v, q, grad = k_ref[rows, at], v_ref[rows, at], q_ref[rows, at], grad_ref[rows, at]
            dprob = jnp.where(mask, dot_nt(v, grad), 0.0).astype(BF16)
            probs = jnp.where(mask, dot_nt(k, q), 0.0).astype(BF16)
            dk_ref[rows, at] = (keep_out * dot_nt(v, low) + dot(dprob, q)).astype(BF16)
            dv_ref[rows, at] = (keep_out * dot(k, low) + dot(probs, grad)).astype(BF16)


def neighbour_states(total, doc_starts, length, reverse):
    def doc_at(pos):
        return jnp.sum((doc_starts <= pos).astype(jnp.int32))

    place = lax.axis_index("seq")
    mine = doc_at((place + 1) * length - 1 if reverse else place * length - 1)
    into = jnp.zeros_like(total)
    if reverse and lax.axis_size("seq") <= 4:
        for step in range(1, lax.axis_size("seq")):
            source = place ^ step
            edge = doc_at(source * length - 1 + (0 if reverse else length))
            outer = (source > place) if reverse else (source < place)
            sent = total if step == 1 else total.astype(BF16)
            into = into + jnp.where(outer & (edge == mine), flip(sent, "seq", step), 0.0)
        return into
    size = 1
    while size < lax.axis_size("seq"):
        other = flip(total if size == 1 else total.astype(BF16), "seq", size).astype(F32)
        group = place // size
        other_edge = doc_at((group ^ 1) * size * length - 1 + (0 if reverse else size * length))
        my_edge = doc_at(group * size * length - 1 + (0 if reverse else size * length))
        outer = (group % 2 == 0) if reverse else (group % 2 == 1)
        into = into + jnp.where(outer & (other_edge == mine), other, 0.0)
        joined = other_edge == my_edge
        total = jnp.where(
            outer,
            total + jnp.where(joined, other, 0.0),
            other + jnp.where(joined, total, 0.0),
        )
        size *= 2
    return into


def project_kernel(split, info, *refs):
    sets = refs[:4]
    shards = refs[4 : len(refs) - (len(refs) - 4) // (split + 1)]
    outs = refs[4 + len(shards) :]
    rows, depth = sets[0].shape
    part = depth // split
    slot = info[1]
    weights = [
        jnp.concatenate([shards[i * split + j][...] for i in range(len(outs))], axis=0)
        for j in range(split)
    ]
    for index, ref in enumerate(sets):
        total = None
        for j in range(split):
            if split == 1:
                left = ref[...]
            else:
                left = ref[:, pl.ds(pl.multiple_of((slot ^ j) * part, part), part)]
            term = dot_nt(left, weights[j])
            total = term if total is None else total + term
        place = 2 * (info[2] ^ (index // 2)) + (info[0] ^ (index % 2))
        at = pl.ds(pl.multiple_of(place * rows, rows), rows)
        width = total.shape[1] // len(outs)
        for i, out in enumerate(outs):
            out[at, :] = total[:, i * width : (i + 1) * width].astype(BF16)


def project(info, sets, shards):
    split = len(shards[0])
    features = shards[0][0].shape[0]
    rows, depth = sets[0].shape
    args = [*sets, *(part for parts in shards for part in parts)]
    outs = [jax.ShapeDtypeStruct((4 * rows, features), BF16)] * len(shards)
    return pl.pallas_call(
        functools.partial(project_kernel, split),
        grid_spec=pltpu.PrefetchScalarGridSpec(
            num_scalar_prefetch=1,
            grid=(1,),
            in_specs=[pl.BlockSpec(memory_space=pltpu.VMEM) for a in args],
            out_specs=[pl.BlockSpec(memory_space=pltpu.VMEM) for o in outs],
        ),
        out_shape=outs,
        name="project",
        cost_estimate=cost(5.0),
        compiler_params=pltpu.CompilerParams(vmem_limit_bytes=PROJECT_VMEM),
    )(info, *args)


def cost(micros):
    return pl.CostEstimate(
        flops=int(micros * COST_SCALE), bytes_accessed=0, transcendentals=0
    )


def grad_mixture(out_grad, out_weight, length, early, late):
    n_head = lax.axis_size("head")
    n_pairs = n_head // 2
    rows, depth = out_grad.shape
    width = out_weight.shape[0]
    half = width // 2
    piece_size = half // PIECES
    part_depth = depth // 2
    me = lax.axis_index("head")
    side, pair = me % 2, me // 2
    core = lax.axis_index("seq") % 2
    slot = (lax.axis_index("seq") // 2) % 2
    info = jnp.stack([side, slot, core]).astype(jnp.int32)
    hops = sorted(range(1, n_pairs), key=lambda k: (bin(k).count("1"), -k))
    order = [(0, hop) for hop in hops if hop & (hop - 1) == 0]
    order += [(1, hop) for hop in hops[:1]]
    order += [(0, hop) for hop in hops if hop & (hop - 1) != 0]
    order += [(1, hop) for hop in hops[1:]]
    waves = [order[i : i + 2] for i in range(0, len(order), 2)]

    fetched = {
        (piece, 0): lax.dynamic_slice(
            out_weight,
            (core * half + piece * piece_size, slot * part_depth),
            (piece_size, part_depth),
        )
        for piece in range(PIECES)
    }
    sets = [out_grad, flip(out_grad, "head", 1), None, None]
    across = {}
    arrived = {}
    for step in range(len(waves) + 2):
        wave = waves[step] if step < len(waves) else []
        landed = waves[step - 1] if 0 < step <= len(waves) else []
        spread = waves[step - 2] if 1 < step else []
        for piece, hop in wave:
            low = hop & -hop
            fetched[piece, hop] = flip(fetched[piece, hop ^ low], "head", 2 * low)
        for key in landed:
            across[key] = flip(fetched[key], "seq", 2)
        made = []
        if step == 1:
            sets[2] = flip(out_grad, "seq", 1)
            made += [sets[1], early()]
        if step == 2:
            sets[3] = flip(sets[1], "seq", 1)
        if spread:
            shards = [[fetched[key], across[key]] for key in spread]
            products = project(info, sets, shards)
            made += products
            for key, product in zip(spread, products):
                arrived[key] = flip(product, "head", 2 * key[1])
        if step == 2:
            made.append(late(products[0]))
        if step == 3:
            mine = lax.dynamic_slice(out_weight, (core * half, 0), (half, depth))
            arrived[0, 0] = project(info, sets, [[mine]])[0]
            made.append(arrived[0, 0])
        if step < len(waves) + 1:
            names = [key for key in fetched if key not in wave]
            keep, new, far, made = lax.optimization_barrier(
                (
                    [fetched[key] for key in names],
                    [fetched[key] for key in wave],
                    [across[key] for key in landed],
                    made,
                )
            )
            if step == 1:
                sets[1] = made[0]
            fetched.update(zip(names, keep))
            fetched.update(zip(wave, new))
            across.update(zip(landed, far))
    mixes = []
    for source in (None, 1):
        mix = jnp.zeros((length, half), BF16)
        for (piece, hop), product in arrived.items():
            which = core if source is None else 1 - core
            product = lax.dynamic_slice(
                product, (which * 2 * rows, 0), (2 * rows, product.shape[1])
            )
            mix = lax.dynamic_update_slice(
                mix, product, ((pair ^ hop) * 2 * rows, piece * piece_size)
            )
        mixes.append(mix)
    return mixes[0], flip(mixes[1], "seq", 1)


def call(kernel, name, info, args, in_specs, outs, out_specs, scratch=(), micros=3.0):
    nblocks = max(a.shape[0] for a in args if a.ndim == 2) // BLK
    return pl.pallas_call(
        kernel,
        grid_spec=pltpu.PrefetchScalarGridSpec(
            num_scalar_prefetch=1,
            grid=(nblocks,),
            in_specs=in_specs,
            out_specs=out_specs,
            scratch_shapes=list(scratch),
        ),
        out_shape=outs,
        name=name,
        cost_estimate=cost(micros),
        compiler_params=pltpu.CompilerParams(vmem_limit_bytes=VMEM_LIMIT),
    )(info, *args)


def shaped(shape, dtype):
    return jax.ShapeDtypeStruct(shape, dtype)


def flip(a, axis, bit):
    return lax.ppermute(a, axis, [(i, i ^ bit) for i in range(lax.axis_size(axis))])


def subsets(items):
    found = [[]]
    for item in items:
        found += [[*one, item] for one in found]
    return found[1:]


def head_sum(sums):
    bits = [1 << i for i in range(lax.axis_size("head").bit_length() - 1)]
    for group in (bits[1:3], bits[:1], bits[3:]):
        spans = [sum(chosen) for chosen in subsets(group)]
        sums = sums + sum(flip(sums, "head", span) for span in spans) if spans else sums
    return sums


def body(out_grad, out_weight, queries, key_rows, value_rows, gate_out, doc_starts):
    length, width = queries.shape
    heads = width // HEAD_DIM
    nblocks = length // BLK
    count = doc_starts.shape[0]
    full_width = width * lax.axis_size("head")
    place = lax.axis_index("seq")
    first = place * length
    info = jnp.concatenate([doc_starts, jnp.stack([first, place % 2]).astype(jnp.int32)])

    block = pl.BlockSpec((BLK, width), lambda b, s: (b, 0))
    half_block = pl.BlockSpec((BLK, width // 2), lambda b, s: (b, 0))
    line = pl.BlockSpec((1, BLK), lambda b, s: (0, b))
    states = pl.BlockSpec((BLK // CHUNK, heads, HEAD_DIM, HEAD_DIM), lambda b, s: (b, 0, 0, 0))
    state = pl.BlockSpec((heads, HEAD_DIM, HEAD_DIM), lambda b, s: (0, 0, 0))
    one_state = shaped((heads, HEAD_DIM, HEAD_DIM), F32)
    all_states = shaped((length // CHUNK, heads, HEAD_DIM, HEAD_DIM), F32)
    low_states = shaped((length // CHUNK, heads, HEAD_DIM, HEAD_DIM), BF16)
    tokens16 = shaped((length, width), BF16)
    tokens32 = shaped((length, width), F32)
    row = shaped((1, length), F32)
    scratch = [pltpu.VMEM((heads, HEAD_DIM, HEAD_DIM), F32)]

    kept = {}

    def early():
        with jax.named_scope("key_states"):
            before, key_total = call(
                functools.partial(key_state_kernel, count, heads),
                "key_states",
                info,
                [key_rows, value_rows],
                [block, block],
                [all_states, one_state],
                [states, state],
                scratch,
            )
        kept["before"] = before
        kept["into"] = neighbour_states(key_total, doc_starts, length, False)
        return kept["into"]

    def late(product):
        tokens, _ = lax.optimization_barrier((queries, product))
        with jax.named_scope("attention"):
            kept["attn"], kept["square"], kept["low"] = call(
                functools.partial(attention_kernel, count, heads),
                "attention",
                info,
                [tokens, key_rows, value_rows, kept["before"], kept["into"]],
                [block, block, block, states, state],
                [tokens32, row, low_states],
                [block, line, states],
            )
        return kept["square"]

    near, far = grad_mixture(out_grad, out_weight, length, early, late)
    attn, square, low = kept["attn"], kept["square"], kept["low"]

    with jax.named_scope("cross"):
        cross = call(
            functools.partial(cross_kernel, heads),
            "cross",
            info,
            [near, far, gate_out, attn],
            [half_block, half_block, block, block],
            [row],
            [line],
        )[0]

    sums = head_sum(jnp.concatenate([square, cross], axis=0))

    back = lambda spec_shape, f: pl.BlockSpec(spec_shape, lambda b, s: f(nblocks - 1 - b))
    block_r = back((BLK, width), lambda b: (b, 0))
    half_r = back((BLK, width // 2), lambda b: (b, 0))
    line_r = back((2, BLK), lambda b: (0, b))
    states_r = back((BLK // CHUNK, heads, HEAD_DIM, HEAD_DIM), lambda b: (b, 0, 0, 0))
    with jax.named_scope("grad_attn"):
        grad, grad_gate, after, query_total = call(
            functools.partial(grad_attn_kernel, count, heads, full_width),
            "grad_attn",
            info,
            [near, far, gate_out, attn, queries, sums],
            [half_r, half_r, block_r, block_r, block_r, line_r],
            [tokens16, tokens16, all_states, one_state],
            [block_r, block_r, states_r, state],
            scratch,
        )
    out_of = neighbour_states(query_total, doc_starts, length, True)
    with jax.named_scope("grad_queries"):
        grad_queries = call(
            functools.partial(grad_query_kernel, count, heads),
            "grad_queries",
            info,
            [grad, key_rows, value_rows, low],
            [block, block, block, states],
            [tokens16],
            [block],
            (),
            8.0,
        )[0]
    with jax.named_scope("grad_keys_values"):
        grad_keys, grad_values = call(
            functools.partial(grad_key_value_kernel, count, heads, length),
            "grad_keys_values",
            info,
            [grad, queries, key_rows, value_rows, after, out_of],
            [block, block, block, block, states, state],
            [tokens16, tokens16],
            [block, block],
            (),
            8.0,
        )
    return (grad_queries, grad_keys, grad_values, grad_gate)


def solution(mesh):
    return jax.shard_map(
        body,
        mesh=mesh,
        in_specs=(
            P(("seq", "head"), None),
            P("head", None),
            P("seq", "head"),
            P("seq", "head"),
            P("seq", "head"),
            P("seq", "head"),
            P(),
        ),
        out_specs=(P("seq", "head"), P("seq", "head"), P("seq", "head"), P("seq", "head")),
        check_vma=False,
    )
```

time: 247 us -> 193 us (0.78)
  Pallas kernels: 84.8 us -> 53.5 us
  between operations: 22.8 us -> 8.38 us
  local copies, waits for them, and re-layouts: 8.35 us -> 15.4 us
  other arithmetic: 7.68 us -> 1.82 us
  starting transfers between devices: 40.1 us -> 34.5 us
  waiting for transfers between devices: 82.4 us -> 78.6 us
    pallas_call x6, Pallas kernels: 57.6 us -> 29.8 us  [call(): pl.pallas_call(kernel, grid_spec=pltpu.PrefetchScalarGridSpec(num_scalar_...]
    ppermute x37 -> x31, starting transfers between devices: 40.1 us -> 34.5 us  [flip(): lax.ppermute(a, axis, [(i, i ^ bit) for i in range(lax.axis_size(axis))])]
    unnamed x22 -> x42, local copies, waits for them, and re-layouts: 5.02 us -> 10.5 us
    add x5 -> x4, other arithmetic: 4.77 us -> 0.14 us  [the longest x1 0.06 us: neighbour_states(): into + jnp.where(outer & (edge == mine), flip(sent, 'seq', step), 0.0)]
    ppermute x37 -> x31, waiting for transfers between devices: 82.3 us -> 78.6 us  [flip(): lax.ppermute(a, axis, [(i, i ^ bit) for i in range(lax.axis_size(axis))])]
    pallas_call x7 -> x4, Pallas kernels: 27.3 us -> 23.7 us  [project(): pl.pallas_call(functools.partial(project_kernel, split), grid_spec=pltpu....]
  transfers between devices with their start and end apart: 38 -> 31, of which waited for: 13 -> 11; matrix products, arithmetic and copies ran while one was open for 3% -> 3% of each run, Pallas kernels for 20% -> 19%
where the time goes in v2:
time: 193 us; the launch traced here: 192 us
  waiting for transfers between devices  78.6 us (41%)
  Pallas kernels  53.5 us (28%)
  starting transfers between devices  34.5 us (18%)
  local copies, waits for them, and re-layouts  15.4 us (8%)
  between operations  8.38 us (4%)
    ppermute x31, waiting for transfers between devices, flip(): lax.ppermute(a, axis, [(i, i ^ bit) for i in range(lax.axis_size(axis))])  78.6 us
    ppermute x31, starting transfers between devices, flip(): lax.ppermute(a, axis, [(i, i ^ bit) for i in range(lax.axis_size(axis))])  34.5 us
    pallas_call x6, Pallas kernels, call(): pl.pallas_call(kernel, grid_spec=pltpu.PrefetchScalarGridSpec(num_scalar_...  29.8 us
    pallas_call x4, Pallas kernels, project(): pl.pallas_call(functools.partial(project_kernel, split), grid_spec=pltpu....  23.7 us
    unnamed x42, local copies, waits for them, and re-layouts  10.5 us
  transfers between devices with their start and end apart: 31, of which 11 were waited for; matrix products, arithmetic and copies ran while one was open for 3% of the time, Pallas kernels for 19%

profile of v2, /device:TPU:0, one launch (start us, length us, event | category | flops | bytes accessed | tf_op | source)
XLA Modules:
  0.0 192.1 jit_solution(13307924273650964003)
XLA Ops:
  0.6 3.0 %collective-permute-start.6 = (bf16[256,4096]{1,0:T(8,128)(2,1)}, bf16[256,4096]{1,0:T(8,128)(2,1)}, u32[]{:S(2)}, u32[]{:S(2)}) collective-permute-start(bf16[256,4096]{1,0:T(8,128)(2,1)} %refs_0_.7), channel_id=1, source_target_pairs={{0,1},{1,0},{2,3},{3,2},{4,5},{5,4},{6,7},{7,6},{8,9},{9,8},{10,11... | collective-permute-start | bytes 6291464 | tf_op jit(solution)/shard_map/ppermute | solution.py:415
  7.5 2.3 %key_states.1 = (f32[8,4,128,128]{3,2,1,0:T(8,128)S(1)}, f32[4,128,128]{2,1,0:T(8,128)S(1)}) custom-call(s32[5]{0:T(128)S(1)} %pad_add_fusion.info, bf16[2048,512]{1,0:T(8,128)(2,1)S(1)} %copy-done.5, bf16[2048,512]{1,0:T(8,128)(2,1)S(1)} %copy-done.8), custom_call_target="tpu_custom_call" | custom-call | flops 3449999872 | tf_op jit(solution)/shard_map/key_states/key_states/pallas_call | solution.py:394
  11.1 2.4 %fusion.8 = (bf16[128,2048]{1,0:T(8,128)(2,1)}, bf16[128,2048]{1,0:T(8,128)(2,1)}) fusion(bf16[512,4096]{1,0:T(8,128)(2,1)} %param.8, s32[]{:T(128)S(6)} %select_n.139, s32[]{:T(128)S(6)} %select_n.138, s32[]{:T(128)S(6)} %select_n.137), kind=kLoop, calls=%fused_computation.38 | loop fusion | bytes 2097164 | tf_op jit(solution)/shard_map/dynamic_slice | solution.py:325
  13.6 2.6 %collective-permute-start = (bf16[128,2048]{1,0:T(8,128)(2,1)}, bf16[128,2048]{1,0:T(8,128)(2,1)S(1)}, u32[]{:S(2)}, u32[]{:S(2)}) collective-permute-start(bf16[128,2048]{1,0:T(8,128)(2,1)} %get-tuple-element.91), channel_id=1, source_target_pairs={{0,4},{1,5},{2,6},{3,7},{4,0},{5,1},{6,2},{7,3},{8,12},{9,13},{10,... | collective-permute-start | bytes 1572872 | tf_op jit(solution)/shard_map/ppermute | solution.py:415
  21.4 18.8 %collective-permute-done.refs_4_ = bf16[128,2048]{1,0:T(8,128)(2,1)S(1)} collective-permute-done((bf16[128,2048]{1,0:T(8,128)(2,1)}, bf16[128,2048]{1,0:T(8,128)(2,1)S(1)}, u32[]{:S(2)}, u32[]{:S(2)}) %collective-permute-start) | collective-permute-done | bytes 524320 | tf_op jit(solution)/shard_map/ppermute | solution.py:415
  41.8 2.3 %collective-permute-start.3 = (bf16[128,2048]{1,0:T(8,128)(2,1)S(1)}, bf16[128,2048]{1,0:T(8,128)(2,1)}, u32[]{:S(2)}, u32[]{:S(2)}) collective-permute-start(bf16[128,2048]{1,0:T(8,128)(2,1)S(1)} %collective-permute-done.refs_4_), channel_id=1, source_target_pairs={{0,2},{1,3},{2,0},{3,1},{4,6},{5,7},{6,4},{7,5},{8,10},{9,11},{10,... | collective-permute-start | bytes 1572872 | tf_op jit(solution)/shard_map/ppermute | solution.py:415
  48.7 17.3 %collective-permute-done.2.refs_4_ = bf16[128,2048]{1,0:T(8,128)(2,1)} collective-permute-done((bf16[128,2048]{1,0:T(8,128)(2,1)}, bf16[128,2048]{1,0:T(8,128)(2,1)}, u32[]{:S(2)}, u32[]{:S(2)}) %collective-permute-start.2) | collective-permute-done | bytes 524320 | tf_op jit(solution)/shard_map/ppermute | solution.py:415
  66.0 2.8 %collective-permute-done.5.refs_7_ = bf16[128,2048]{1,0:T(8,128)(2,1)} collective-permute-done((bf16[128,2048]{1,0:T(8,128)(2,1)}, bf16[128,2048]{1,0:T(8,128)(2,1)}, u32[]{:S(2)}, u32[]{:S(2)}) %collective-permute-start.5) | collective-permute-done | bytes 524320 | tf_op jit(solution)/shard_map/ppermute | solution.py:415
  74.9 6.1 %project.4 = (bf16[1024,128]{1,0:T(8,128)(2,1)S(1)}, bf16[1024,128]{1,0:T(8,128)(2,1)S(1)}) custom-call(s32[3]{0:T(128)S(1)} %pad_add_fusion.1.info, bf16[256,4096]{1,0:T(8,128)(2,1)S(1)} %copy-done, bf16[256,4096]{1,0:T(8,128)(2,1)} %collective-permute-done.6.refs_1_, bf16[256,4096]{1,0:T(8,128)(2,1)} %collective-permute-done.9.refs_2_, ...), custom_call_target="tpu_custom_call" | custom-call | flops 5750000128 | tf_op jit(solution)/shard_map/project/pallas_call | solution.py:283
  81.4 5.5 %attention.1 = (f32[2048,512]{1,0:T(8,128)S(1)}, f32[1,2048]{1,0:T(1,128)S(1)}, bf16[8,4,128,128]{3,2,1,0:T(8,128)(2,1)S(1)}) custom-call(s32[5]{0:T(128)S(1)} %pad_add_fusion.info, bf16[2048,512]{1,0:T(8,128)(2,1)S(1)} %copy-done.2, bf16[2048,512]{1,0:T(8,128)(2,1)S(1)} %copy-done.6, bf16[2048,512]{1,0:T(8,128)(2,1)S(1)} %copy-done.9, ...), custom_call_target="tpu_custom_call" | custom-call | flops 3449999872 | tf_op jit(solution)/shard_map/attention/attention/pallas_call | solution.py:394
  87.9 14.4 %collective-permute-done.13.refs_4_ = bf16[128,2048]{1,0:T(8,128)(2,1)S(1)} collective-permute-done((bf16[128,2048]{1,0:T(8,128)(2,1)S(1)}, bf16[128,2048]{1,0:T(8,128)(2,1)S(1)}, u32[]{:S(2)}, u32[]{:S(2)}) %collective-permute-start.13) | collective-permute-done | bytes 524320 | tf_op jit(solution)/shard_map/ppermute | solution.py:415
  104.3 6.0 %project.5 = (bf16[1024,128]{1,0:T(8,128)(2,1)S(1)}, bf16[1024,128]{1,0:T(8,128)(2,1)S(1)}) custom-call(s32[3]{0:T(128)S(1)} %pad_add_fusion.1.info, bf16[256,4096]{1,0:T(8,128)(2,1)S(1)} %copy-done, bf16[256,4096]{1,0:T(8,128)(2,1)} %collective-permute-done.6.refs_1_, bf16[256,4096]{1,0:T(8,128)(2,1)} %collective-permute-done.9.refs_2_, ...), custom_call_target="tpu_custom_call" | custom-call | flops 5750000128 | tf_op jit(solution)/shard_map/project/pallas_call | solution.py:283
  111.0 5.8 %project.6 = bf16[1024,256]{1,0:T(8,128)(2,1)S(1)} custom-call(s32[3]{0:T(128)S(1)} %pad_add_fusion.1.info, bf16[256,4096]{1,0:T(8,128)(2,1)S(1)} %copy-done, bf16[256,4096]{1,0:T(8,128)(2,1)} %collective-permute-done.6.refs_1_, bf16[256,4096]{1,0:T(8,128)(2,1)} %collective-permute-done.9.refs_2_, bf16[256,4096]{1,0:T(8,128)(2,1)} %collective-permute-done.10.refs_3_, ...), custom_call_target="tpu_custom_call" | custom-call | flops 5750000128 | tf_op jit(solution)/shard_map/project/pallas_call | solution.py:283
  116.8 3.8 %collective-permute-start.18 = (bf16[1024,128]{1,0:T(8,128)(2,1)S(1)}, bf16[1024,128]{1,0:T(8,128)(2,1)S(1)}, u32[]{:S(2)}, u32[]{:S(2)}) collective-permute-start(bf16[1024,128]{1,0:T(8,128)(2,1)S(1)} %get-tuple-element.65), channel_id=1, source_target_pairs={{0,6},{1,7},{2,4},{3,5},{4,2},{5,3},{6,0},{7,1},{8,14},{9,15},{10,... | collective-permute-start | bytes 786440 | tf_op jit(solution)/shard_map/ppermute | solution.py:415
  121.0 6.1 %collective-permute-done.20.refs_7_ = bf16[128,2048]{1,0:T(8,128)(2,1)S(1)} collective-permute-done((bf16[128,2048]{1,0:T(8,128)(2,1)S(1)}, bf16[128,2048]{1,0:T(8,128)(2,1)S(1)}, u32[]{:S(2)}, u32[]{:S(2)}) %collective-permute-start.20) | collective-permute-done | bytes 524320 | tf_op jit(solution)/shard_map/ppermute | solution.py:415
  127.1 5.8 %project.7 = (bf16[1024,128]{1,0:T(8,128)(2,1)S(1)}, bf16[1024,128]{1,0:T(8,128)(2,1)S(1)}) custom-call(s32[3]{0:T(128)S(1)} %pad_add_fusion.1.info, bf16[256,4096]{1,0:T(8,128)(2,1)S(1)} %copy-done, bf16[256,4096]{1,0:T(8,128)(2,1)} %collective-permute-done.6.refs_1_, bf16[256,4096]{1,0:T(8,128)(2,1)} %collective-permute-done.9.refs_2_, ...), custom_call_target="tpu_custom_call" | custom-call | flops 5750000128 | tf_op jit(solution)/shard_map/project/pallas_call | solution.py:283
  135.0 10.6 %collective-permute-done.21 = bf16[1024,128]{1,0:T(8,128)(2,1)S(1)} collective-permute-done((bf16[1024,128]{1,0:T(8,128)(2,1)S(1)}, bf16[1024,128]{1,0:T(8,128)(2,1)S(1)}, u32[]{:S(2)}, u32[]{:S(2)}) %collective-permute-start.21) | collective-permute-done | bytes 262176 | tf_op jit(solution)/shard_map/ppermute | solution.py:415
  145.9 2.6 %collective-permute-done.23.far_ref = bf16[2048,256]{1,0:T(8,128)(2,1)S(1)} collective-permute-done((bf16[2048,256]{1,0:T(8,128)(2,1)S(1)}, bf16[2048,256]{1,0:T(8,128)(2,1)S(1)}, u32[]{:S(2)}, u32[]{:S(2)}) %collective-permute-start.23) | collective-permute-done | bytes 1048608 | tf_op jit(solution)/shard_map/ppermute | solution.py:415
  155.0 2.0 %collective-permute-done.25 = f32[2,2048]{1,0:T(2,128)S(1)} collective-permute-done((f32[2,2048]{1,0:T(2,128)S(1)}, f32[2,2048]{1,0:T(2,128)S(1)}, u32[]{:S(2)}, u32[]{:S(2)}) %collective-permute-start.25) | collective-permute-done | bytes 16416 | tf_op jit(solution)/shard_map/ppermute | solution.py:415
  157.1 2.8 %collective-permute-done.26 = f32[2,2048]{1,0:T(2,128)S(1)} collective-permute-done((f32[2,2048]{1,0:T(2,128)S(1)}, f32[2,2048]{1,0:T(2,128)S(1)}, u32[]{:S(2)}, u32[]{:S(2)}) %collective-permute-start.26) | collective-permute-done | bytes 16416 | tf_op jit(solution)/shard_map/ppermute | solution.py:415
  167.1 2.2 %copy-done.14 = f32[2048,512]{1,0:T(8,128)S(1)} copy-done((f32[2048,512]{1,0:T(8,128)S(1)}, f32[2048,512]{1,0:T(8,128)}, u32[]{:S(2)}) %copy-start.14) | copy-done | bytes 4194328
  169.3 5.6 %grad_attn.1 = (bf16[2048,512]{1,0:T(8,128)(2,1)S(1)}, bf16[2048,512]{1,0:T(8,128)(2,1)}, f32[8,4,128,128]{3,2,1,0:T(8,128)S(1)}, f32[4,128,128]{2,1,0:T(8,128)S(1)}) custom-call(s32[5]{0:T(128)S(1)} %pad_add_fusion.info, bf16[2048,256]{1,0:T(8,128)(2,1)S(1)} %get-tuple-element.95.near_ref, bf16[2048,256]{1,0:T(8,128)(2,1)S(1)} %copy-done.12, ...), custom_call_target="tpu_custom_call" | custom-call | flops 3449999872 | tf_op jit(solution)/shard_map/grad_attn/grad_attn/pallas_call | solution.py:394
  176.8 5.7 %grad_queries.1 = bf16[2048,512]{1,0:T(8,128)(2,1)} custom-call(s32[5]{0:T(128)S(1)} %pad_add_fusion.info, bf16[2048,512]{1,0:T(8,128)(2,1)S(1)} %get-tuple-element.75.grad_ref, bf16[2048,512]{1,0:T(8,128)(2,1)S(1)} %copy-done.7, bf16[2048,512]{1,0:T(8,128)(2,1)S(1)} %copy-done.10, bf16[8,4,128,128]{3,2,1,0:T(8,128)(2,1)S(1)} %copy-done.18), custom_call_target="tpu_custom_call" | custom-call | flops 9200000000 | tf_op jit(solution)/shard_map/grad_queries/grad_queries/pallas_call | solution.py:394
  183.4 8.8 %grad_keys_values.1 = (bf16[2048,512]{1,0:T(8,128)(2,1)}, bf16[2048,512]{1,0:T(8,128)(2,1)}) custom-call(s32[5]{0:T(128)S(1)} %pad_add_fusion.info, bf16[2048,512]{1,0:T(8,128)(2,1)S(1)} %get-tuple-element.75.grad_ref, bf16[2048,512]{1,0:T(8,128)(2,1)S(1)} %copy-done.4, bf16[2048,512]{1,0:T(8,128)(2,1)S(1)} %copy-done.7, bf16[2048,512]{1,0:T(8,128)(2,1)S(1)} %copy-done.10, ...), custom_call_target="tpu_custom_call" | custom-call | flops 9200000000 | tf_op jit(solution)/shard_map/grad_keys_values/grad_keys_values/pallas_call | solution.py:394
  (112 shorter events, 38.3 us)
Async XLA Ops:
  0.6 68.2 %collective-permute-start.6 = (bf16[256,4096]{1,0:T(8,128)(2,1)}, bf16[256,4096]{1,0:T(8,128)(2,1)}, u32[]{:S(2)}, u32[]{:S(2)}) collective-permute-start(bf16[256,4096]{1,0:T(8,128)(2,1)} %refs_0_.7), channel_id=1, source_target_pairs={{0,1},{1,0},{2,3},{3,2},{4,5},{5,4},{6,7},{7,6},{8,9},{9,8},{10,11... | collective-permute-start | bytes 6291464 | tf_op jit(solution)/shard_map/ppermute | solution.py:415
  11.1 8.6 %collective-permute-start.7 = (f32[4,128,128]{2,1,0:T(8,128)S(1)}, f32[4,128,128]{2,1,0:T(8,128)S(1)}, u32[]{:S(2)}, u32[]{:S(2)}) collective-permute-start(f32[4,128,128]{2,1,0:T(8,128)S(1)} %get-tuple-element.46), channel_id=1, source_target_pairs={{0,8},{8,0},{16,24},{24,16},{1,9},{9,1},{17,25},{25,17},{2,10},{10... | collective-permute-start | bytes 786440 | tf_op jit(solution)/shard_map/ppermute | solution.py:415
  13.6 26.6 %collective-permute-start = (bf16[128,2048]{1,0:T(8,128)(2,1)}, bf16[128,2048]{1,0:T(8,128)(2,1)S(1)}, u32[]{:S(2)}, u32[]{:S(2)}) collective-permute-start(bf16[128,2048]{1,0:T(8,128)(2,1)} %get-tuple-element.91), channel_id=1, source_target_pairs={{0,4},{1,5},{2,6},{3,7},{4,0},{5,1},{6,2},{7,3},{8,12},{9,13},{10,... | collective-permute-start | bytes 1572872 | tf_op jit(solution)/shard_map/ppermute | solution.py:415
  16.2 24.3 %collective-permute-start.1 = (bf16[128,2048]{1,0:T(8,128)(2,1)}, bf16[128,2048]{1,0:T(8,128)(2,1)}, u32[]{:S(2)}, u32[]{:S(2)}) collective-permute-start(bf16[128,2048]{1,0:T(8,128)(2,1)} %get-tuple-element.91), channel_id=1, source_target_pairs={{0,2},{1,3},{2,0},{3,1},{4,6},{5,7},{6,4},{7,5},{8,10},{9,11},{10,... | collective-permute-start | bytes 1572872 | tf_op jit(solution)/shard_map/ppermute | solution.py:415
  19.8 25.9 %collective-permute-start.8 = (bf16[4,128,128]{2,1,0:T(8,128)(2,1)S(1)}, bf16[4,128,128]{2,1,0:T(8,128)(2,1)S(1)}, u32[]{:S(2)}, u32[]{:S(2)}) collective-permute-start(bf16[4,128,128]{2,1,0:T(8,128)(2,1)S(1)} %select_convert_fusion), channel_id=1, source_target_pairs={{0,16},{8,24},{16,0},{24,8},{1,17},{9,25},{17,1},{25,9},{2,18},{10... | collective-permute-start | bytes 393224 | tf_op jit(solution)/shard_map/ppermute | solution.py:415
  40.5 25.5 %collective-permute-start.2 = (bf16[128,2048]{1,0:T(8,128)(2,1)}, bf16[128,2048]{1,0:T(8,128)(2,1)}, u32[]{:S(2)}, u32[]{:S(2)}) collective-permute-start(bf16[128,2048]{1,0:T(8,128)(2,1)} %get-tuple-element.54), channel_id=1, source_target_pairs={{0,4},{1,5},{2,6},{3,7},{4,0},{5,1},{6,2},{7,3},{8,12},{9,13},{10,... | collective-permute-start | bytes 1572872 | tf_op jit(solution)/shard_map/ppermute | solution.py:415
  41.8 24.2 %collective-permute-start.3 = (bf16[128,2048]{1,0:T(8,128)(2,1)S(1)}, bf16[128,2048]{1,0:T(8,128)(2,1)}, u32[]{:S(2)}, u32[]{:S(2)}) collective-permute-start(bf16[128,2048]{1,0:T(8,128)(2,1)S(1)} %collective-permute-done.refs_4_), channel_id=1, source_target_pairs={{0,2},{1,3},{2,0},{3,1},{4,6},{5,7},{6,4},{7,5},{8,10},{9,11},{10,... | collective-permute-start | bytes 1572872 | tf_op jit(solution)/shard_map/ppermute | solution.py:415
  44.2 21.8 %collective-permute-start.4 = (bf16[128,2048]{1,0:T(8,128)(2,1)S(1)}, bf16[128,2048]{1,0:T(8,128)(2,1)}, u32[]{:S(2)}, u32[]{:S(2)}) collective-permute-start(bf16[128,2048]{1,0:T(8,128)(2,1)S(1)} %collective-permute-done.refs_4_), channel_id=1, source_target_pairs={{0,16},{8,24},{16,0},{24,8},{1,17},{9,25},{17,1},{25,9},{2,18},{10... | collective-permute-start | bytes 1572872 | tf_op jit(solution)/shard_map/ppermute | solution.py:415
  45.7 23.1 %collective-permute-start.5 = (bf16[128,2048]{1,0:T(8,128)(2,1)}, bf16[128,2048]{1,0:T(8,128)(2,1)}, u32[]{:S(2)}, u32[]{:S(2)}) collective-permute-start(bf16[128,2048]{1,0:T(8,128)(2,1)} %collective-permute-done.1.refs_6_), channel_id=1, source_target_pairs={{0,16},{8,24},{16,0},{24,8},{1,17},{9,25},{17,1},{25,9},{2,18},{10... | collective-permute-start | bytes 1572872 | tf_op jit(solution)/shard_map/ppermute | solution.py:415
  66.0 8.4 %collective-permute-start.9 = (bf16[256,4096]{1,0:T(8,128)(2,1)S(1)}, bf16[256,4096]{1,0:T(8,128)(2,1)}, u32[]{:S(2)}, u32[]{:S(2)}) collective-permute-start(bf16[256,4096]{1,0:T(8,128)(2,1)S(1)} %copy-done), channel_id=1, source_target_pairs={{0,8},{8,0},{16,24},{24,16},{1,9},{9,1},{17,25},{25,17},{2,10},{10... | collective-permute-start | bytes 6291464 | tf_op jit(solution)/shard_map/ppermute | solution.py:415
  70.8 31.5 %collective-permute-start.14 = (bf16[128,2048]{1,0:T(8,128)(2,1)}, bf16[128,2048]{1,0:T(8,128)(2,1)S(1)}, u32[]{:S(2)}, u32[]{:S(2)}) collective-permute-start(bf16[128,2048]{1,0:T(8,128)(2,1)} %collective-permute-done.2.refs_4_), channel_id=1, source_target_pairs={{0,2},{1,3},{2,0},{3,1},{4,6},{5,7},{6,4},{7,5},{8,10},{9,11},{10,... | collective-permute-start | bytes 1572872 | tf_op jit(solution)/shard_map/ppermute | solution.py:415
  71.1 31.1 %collective-permute-start.15 = (bf16[128,2048]{1,0:T(8,128)(2,1)}, bf16[128,2048]{1,0:T(8,128)(2,1)S(1)}, u32[]{:S(2)}, u32[]{:S(2)}) collective-permute-start(bf16[128,2048]{1,0:T(8,128)(2,1)} %collective-permute-done.2.refs_4_), channel_id=1, source_target_pairs={{0,16},{8,24},{16,0},{24,8},{1,17},{9,25},{17,1},{25,9},{2,18},{10... | collective-permute-start | bytes 1572872 | tf_op jit(solution)/shard_map/ppermute | solution.py:415
  72.6 29.6 %collective-permute-start.13 = (bf16[128,2048]{1,0:T(8,128)(2,1)S(1)}, bf16[128,2048]{1,0:T(8,128)(2,1)S(1)}, u32[]{:S(2)}, u32[]{:S(2)}) collective-permute-start(bf16[128,2048]{1,0:T(8,128)(2,1)S(1)} %copy-done.19), channel_id=1, source_target_pairs={{0,2},{1,3},{2,0},{3,1},{4,6},{5,7},{6,4},{7,5},{8,10},{9,11},{10,... | collective-permute-start | bytes 1572872 | tf_op jit(solution)/shard_map/ppermute | solution.py:415
  74.4 27.9 %collective-permute-start.16 = (bf16[128,2048]{1,0:T(8,128)(2,1)}, bf16[128,2048]{1,0:T(8,128)(2,1)S(1)}, u32[]{:S(2)}, u32[]{:S(2)}) collective-permute-start(bf16[128,2048]{1,0:T(8,128)(2,1)} %collective-permute-done.3.refs_6_), channel_id=1, source_target_pairs={{0,16},{8,24},{16,0},{24,8},{1,17},{9,25},{17,1},{25,9},{2,18},{10... | collective-permute-start | bytes 1572872 | tf_op jit(solution)/shard_map/ppermute | solution.py:415
  81.0 35.8 %collective-permute-start.11 = (bf16[1024,128]{1,0:T(8,128)(2,1)S(1)}, bf16[1024,128]{1,0:T(8,128)(2,1)S(1)}, u32[]{:S(2)}, u32[]{:S(2)}) collective-permute-start(bf16[1024,128]{1,0:T(8,128)(2,1)S(1)} %get-tuple-element.52), channel_id=1, source_target_pairs={{0,4},{1,5},{2,6},{3,7},{4,0},{5,1},{6,2},{7,3},{8,12},{9,13},{10,... | collective-permute-start | bytes 786440 | tf_op jit(solution)/shard_map/ppermute | solution.py:415
  102.2 18.7 %collective-permute-start.12 = (bf16[1024,128]{1,0:T(8,128)(2,1)S(1)}, bf16[1024,128]{1,0:T(8,128)(2,1)S(1)}, u32[]{:S(2)}, u32[]{:S(2)}) collective-permute-start(bf16[1024,128]{1,0:T(8,128)(2,1)S(1)} %get-tuple-element.53), channel_id=1, source_target_pairs={{0,2},{1,3},{2,0},{3,1},{4,6},{5,7},{6,4},{7,5},{8,10},{9,11},{10,... | collective-permute-start | bytes 786440 | tf_op jit(solution)/shard_map/ppermute | solution.py:415
  102.2 18.7 %collective-permute-start.19 = (bf16[128,2048]{1,0:T(8,128)(2,1)S(1)}, bf16[128,2048]{1,0:T(8,128)(2,1)S(1)}, u32[]{:S(2)}, u32[]{:S(2)}) collective-permute-start(bf16[128,2048]{1,0:T(8,128)(2,1)S(1)} %collective-permute-done.13.refs_4_), channel_id=1, source_target_pairs={{0,16},{8,24},{16,0},{24,8},{1,17},{9,25},{17,1},{25,9},{2,18},{10... | collective-permute-start | bytes 1572872 | tf_op jit(solution)/shard_map/ppermute | solution.py:415
  103.8 23.3 %collective-permute-start.20 = (bf16[128,2048]{1,0:T(8,128)(2,1)S(1)}, bf16[128,2048]{1,0:T(8,128)(2,1)S(1)}, u32[]{:S(2)}, u32[]{:S(2)}) collective-permute-start(bf16[128,2048]{1,0:T(8,128)(2,1)S(1)} %collective-permute-done.14.refs_6_), channel_id=1, source_target_pairs={{0,16},{8,24},{16,0},{24,8},{1,17},{9,25},{17,1},{25,9},{2,18},{10... | collective-permute-start | bytes 1572872 | tf_op jit(solution)/shard_map/ppermute | solution.py:415
  110.3 24.4 %collective-permute-start.17 = (bf16[1024,128]{1,0:T(8,128)(2,1)S(1)}, bf16[1024,128]{1,0:T(8,128)(2,1)S(1)}, u32[]{:S(2)}, u32[]{:S(2)}) collective-permute-start(bf16[1024,128]{1,0:T(8,128)(2,1)S(1)} %get-tuple-element.64), channel_id=1, source_target_pairs={{0,4},{1,5},{2,6},{3,7},{4,0},{5,1},{6,2},{7,3},{8,12},{9,13},{10,... | collective-permute-start | bytes 786440 | tf_op jit(solution)/shard_map/ppermute | solution.py:415
  116.8 18.1 %collective-permute-start.18 = (bf16[1024,128]{1,0:T(8,128)(2,1)S(1)}, bf16[1024,128]{1,0:T(8,128)(2,1)S(1)}, u32[]{:S(2)}, u32[]{:S(2)}) collective-permute-start(bf16[1024,128]{1,0:T(8,128)(2,1)S(1)} %get-tuple-element.65), channel_id=1, source_target_pairs={{0,6},{1,7},{2,4},{3,5},{4,2},{5,3},{6,0},{7,1},{8,14},{9,15},{10,... | collective-permute-start | bytes 786440 | tf_op jit(solution)/shard_map/ppermute | solution.py:415
  132.9 12.7 %collective-permute-start.21 = (bf16[1024,128]{1,0:T(8,128)(2,1)S(1)}, bf16[1024,128]{1,0:T(8,128)(2,1)S(1)}, u32[]{:S(2)}, u32[]{:S(2)}) collective-permute-start(bf16[1024,128]{1,0:T(8,128)(2,1)S(1)} %get-tuple-element.72), channel_id=1, source_target_pairs={{0,2},{1,3},{2,0},{3,1},{4,6},{5,7},{6,4},{7,5},{8,10},{9,11},{10,... | collective-permute-start | bytes 786440 | tf_op jit(solution)/shard_map/ppermute | solution.py:415
  134.8 10.9 %collective-permute-start.22 = (bf16[1024,128]{1,0:T(8,128)(2,1)S(1)}, bf16[1024,128]{1,0:T(8,128)(2,1)S(1)}, u32[]{:S(2)}, u32[]{:S(2)}) collective-permute-start(bf16[1024,128]{1,0:T(8,128)(2,1)S(1)} %get-tuple-element.73), channel_id=1, source_target_pairs={{0,6},{1,7},{2,4},{3,5},{4,2},{5,3},{6,0},{7,1},{8,14},{9,15},{10,... | collective-permute-start | bytes 786440 | tf_op jit(solution)/shard_map/ppermute | solution.py:415
  174.8 8.4 %collective-permute-start.28 = (f32[4,128,128]{2,1,0:T(8,128)S(1)}, f32[4,128,128]{2,1,0:T(8,128)S(1)}, u32[]{:S(2)}, u32[]{:S(2)}) collective-permute-start(f32[4,128,128]{2,1,0:T(8,128)S(1)} %get-tuple-element.78), channel_id=1, source_target_pairs={{0,8},{8,0},{16,24},{24,16},{1,9},{9,1},{17,25},{25,17},{2,10},{10... | collective-permute-start | bytes 786440 | tf_op jit(solution)/shard_map/ppermute | solution.py:415
  174.9 7.7 %collective-permute-start.29 = (bf16[4,128,128]{2,1,0:T(8,128)(2,1)S(1)}, bf16[4,128,128]{2,1,0:T(8,128)(2,1)S(1)}, u32[]{:S(2)}, u32[]{:S(2)}) collective-permute-start(bf16[4,128,128]{2,1,0:T(8,128)(2,1)S(1)} %convert_element_type.52), channel_id=1, source_target_pairs={{0,16},{8,24},{16,0},{24,8},{1,17},{9,25},{17,1},{25,9},{2,18},{10... | collective-permute-start | bytes 393224 | tf_op jit(solution)/shard_map/ppermute | solution.py:415
  (28 other events, 260.3 us)

commit v3 on v2

--- a/solution.py
+++ b/solution.py
@@ -14,7 +14,7 @@
 F32 = jnp.float32
 BF16 = jnp.bfloat16
 VMEM_LIMIT = 16 * 1024 * 1024
-PROJECT_VMEM = 24 * 1024 * 1024
+PROJECT_VMEM = 16 * 1024 * 1024
 PIECES = 2
 COST_SCALE = 1.15e9
 
@@ -127,11 +127,12 @@
             yield ref.at[:, head_slice(i)], at
 
 
-def cross_kernel(heads, info, near_ref, far_ref, gate_ref, attn_ref, cross_ref):
+def cross_kernel(heads, info, near_ref, far_ref, gate_ref, attn_ref, square_ref, sums_ref):
     total = jnp.zeros((BLK, HEAD_DIM), F32)
     for mix, at in mix_heads(heads, info, near_ref, far_ref):
         total = total + mix[...].astype(F32) * gate_ref[:, at].astype(F32) * attn_ref[:, at]
-    cross_ref[...] = lane_sums(total)
+    sums_ref[0:1, :] = square_ref[...]
+    sums_ref[1:2, :] = lane_sums(total)
 
 
 def grad_attn_kernel(
@@ -149,6 +150,7 @@
     gate_grad_ref,
     after_ref,
     total_ref,
+    low_ref,
     state,
 ):
     @pl.when(pl.program_id(0) == 0)
@@ -176,6 +178,7 @@
             after_ref[r, h] = state[h]
             state[h] = dot_tn(q_ref[rows, at] * keep_in, grad) + carry * state[h]
     total_ref[...] = state[...]
+    low_ref[...] = state[...].astype(BF16)
 
 
 def grad_query_kernel(count, heads, info, grad_ref, k_ref, v_ref, low_ref, out_ref):
@@ -194,9 +197,24 @@
 
 
 def grad_key_value_kernel(
-    count, heads, length, info, grad_ref, q_ref, k_ref, v_ref, after_ref, into_ref, dk_ref, dv_ref
+    count, heads, length, info, grad_ref, q_ref, k_ref, v_ref, after_ref, *refs
 ):
+    *landed, dk_ref, dv_ref, into_ref = refs
     first = info[count]
+
+    @pl.when(pl.program_id(0) == 0)
+    def _():
+        place = lax.div(first, length)
+        last_doc = doc_of(info, count, first + length - 1)
+        total = None
+        for index, ref in enumerate(landed):
+            source = place ^ (index + 1)
+            takes = jnp.where(source > place, F32(1.0), F32(0.0))
+            takes = takes * same(doc_of(info, count, source * length - 1), last_doc)
+            term = ref[...].astype(F32) * takes
+            total = term if total is None else total + term
+        into_ref[...] = total
+
     for r in range(BLK // CHUNK):
         rows = chunk_rows(r)
         start = first + pl.program_id(0) * BLK + r * CHUNK
@@ -214,74 +232,96 @@
             dv_ref[rows, at] = (keep_out * dot(k, low) + dot(probs, grad)).astype(BF16)
 
 
-def neighbour_states(total, doc_starts, length, reverse):
-    def doc_at(pos):
-        return jnp.sum((doc_starts <= pos).astype(jnp.int32))
-
-    place = lax.axis_index("seq")
-    mine = doc_at((place + 1) * length - 1 if reverse else place * length - 1)
-    into = jnp.zeros_like(total)
-    if reverse and lax.axis_size("seq") <= 4:
-        for step in range(1, lax.axis_size("seq")):
-            source = place ^ step
-            edge = doc_at(source * length - 1 + (0 if reverse else length))
-            outer = (source > place) if reverse else (source < place)
-            sent = total if step == 1 else total.astype(BF16)
-            into = into + jnp.where(outer & (edge == mine), flip(sent, "seq", step), 0.0)
-        return into
-    size = 1
-    while size < lax.axis_size("seq"):
-        other = flip(total if size == 1 else total.astype(BF16), "seq", size).astype(F32)
-        group = place // size
-        other_edge = doc_at((group ^ 1) * size * length - 1 + (0 if reverse else size * length))
-        my_edge = doc_at(group * size * length - 1 + (0 if reverse else size * length))
-        outer = (group % 2 == 0) if reverse else (group % 2 == 1)
-        into = into + jnp.where(outer & (other_edge == mine), other, 0.0)
-        joined = other_edge == my_edge
-        total = jnp.where(
-            outer,
-            total + jnp.where(joined, other, 0.0),
-            other + jnp.where(joined, total, 0.0),
-        )
-        size *= 2
-    return into
-
-
-def project_kernel(split, info, *refs):
-    sets = refs[:4]
-    shards = refs[4 : len(refs) - (len(refs) - 4) // (split + 1)]
-    outs = refs[4 + len(shards) :]
-    rows, depth = sets[0].shape
-    part = depth // split
-    slot = info[1]
-    weights = [
-        jnp.concatenate([shards[i * split + j][...] for i in range(len(outs))], axis=0)
-        for j in range(split)
-    ]
+def combine_kernel(count, length, size, info, total_ref, other_ref, into_ref, *outs):
+    first = info[count]
+    place = lax.div(first, length)
+    group = lax.div(place, size)
+    other_doc = doc_of(info, count, ((group ^ 1) + 1) * (size * length) - 1)
+    my_doc = doc_of(info, count, (group + 1) * (size * length) - 1)
+    later = same(group & 1, 1)
+    reaches = later * same(other_doc, doc_of(info, count, first - 1))
+    joined = same(other_doc, my_doc)
+    total_share = later + (1.0 - later) * joined
+    other_share = later * joined + (1.0 - later)
+    other = other_ref[...].astype(F32)
+    total = total_ref[...].astype(F32) * total_share + other * other_share
+    outs[0][...] = total.astype(BF16)
+    outs[1][...] = into_ref[...] + other * reaches
+
+
+def combine(info, count, length, size, total, other, into):
+    whole = pl.BlockSpec(total.shape, lambda i, s: (0, 0, 0))
+    return pl.pallas_call(
+        functools.partial(combine_kernel, count, length, size),
+        grid_spec=pltpu.PrefetchScalarGridSpec(
+            num_scalar_prefetch=1, grid=(1,), in_specs=[whole] * 3, out_specs=[whole] * 2
+        ),
+        out_shape=[
+            jax.ShapeDtypeStruct(total.shape, BF16),
+            jax.ShapeDtypeStruct(total.shape, F32),
+        ],
+        name="combine",
+        cost_estimate=cost(1.0),
+        compiler_params=pltpu.CompilerParams(vmem_limit_bytes=VMEM_LIMIT),
+    )(info, total, other, into)
+
+
+def gather_kernel(info, *refs):
+    sets, out, arrived = refs[:4], refs[4], refs[5]
+    rows = sets[0].shape[0]
+    copies = []
     for index, ref in enumerate(sets):
-        total = None
-        for j in range(split):
-            if split == 1:
-                left = ref[...]
-            else:
-                left = ref[:, pl.ds(pl.multiple_of((slot ^ j) * part, part), part)]
-            term = dot_nt(left, weights[j])
-            total = term if total is None else total + term
         place = 2 * (info[2] ^ (index // 2)) + (info[0] ^ (index % 2))
         at = pl.ds(pl.multiple_of(place * rows, rows), rows)
-        width = total.shape[1] // len(outs)
-        for i, out in enumerate(outs):
-            out[at, :] = total[:, i * width : (i + 1) * width].astype(BF16)
-
-
-def project(info, sets, shards):
-    split = len(shards[0])
-    features = shards[0][0].shape[0]
+        copies.append(pltpu.make_async_copy(ref, out.at[at, :], arrived.at[index]))
+    for copy in copies:
+        copy.start()
+    for copy in copies:
+        copy.wait()
+
+
+def gather_rows(info, sets):
     rows, depth = sets[0].shape
-    args = [*sets, *(part for parts in shards for part in parts)]
-    outs = [jax.ShapeDtypeStruct((4 * rows, features), BF16)] * len(shards)
     return pl.pallas_call(
-        functools.partial(project_kernel, split),
+        gather_kernel,
+        grid_spec=pltpu.PrefetchScalarGridSpec(
+            num_scalar_prefetch=1,
+            grid=(1,),
+            in_specs=[pl.BlockSpec(memory_space=pl.ANY)] * 4,
+            out_specs=pl.BlockSpec(memory_space=pltpu.VMEM),
+            scratch_shapes=[pltpu.SemaphoreType.DMA((4,))],
+        ),
+        out_shape=jax.ShapeDtypeStruct((4 * rows, depth), BF16),
+        name="gather_rows",
+        cost_estimate=cost(3.0),
+        compiler_params=pltpu.CompilerParams(vmem_limit_bytes=PROJECT_VMEM),
+    )(info, *sets)
+
+
+def project_kernel(split, info, rows_ref, *refs):
+    count = len(refs) // (split + 1)
+    shards, outs = refs[: count * split], refs[count * split :]
+    part = rows_ref.shape[1] // split
+    total = None
+    for j in range(split):
+        if split == 1:
+            left = rows_ref[...]
+        else:
+            left = rows_ref[:, pl.ds(pl.multiple_of((info[1] ^ j) * part, part), part)]
+        weights = [shards[i * split + j][...] for i in range(count)]
+        weights = weights[0] if count == 1 else jnp.concatenate(weights, axis=0)
+        term = dot_nt(left, weights)
+        total = term if total is None else total + term
+    width = total.shape[1] // count
+    for i, out in enumerate(outs):
+        out[...] = total[:, i * width : (i + 1) * width].astype(BF16)
+
+
+def project(info, rows, shards):
+    args = [rows, *(part for parts in shards for part in parts)]
+    outs = [jax.ShapeDtypeStruct((rows.shape[0], shards[0][0].shape[0]), BF16)] * len(shards)
+    return pl.pallas_call(
+        functools.partial(project_kernel, len(shards[0])),
         grid_spec=pltpu.PrefetchScalarGridSpec(
             num_scalar_prefetch=1,
             grid=(1,),
@@ -290,9 +330,28 @@
         ),
         out_shape=outs,
         name="project",
-        cost_estimate=cost(5.0),
+        cost_estimate=cost(3.0),
         compiler_params=pltpu.CompilerParams(vmem_limit_bytes=PROJECT_VMEM),
     )(info, *args)
+
+
+def add_kernel(*refs):
+    total = refs[0][...]
+    for ref in refs[1:-1]:
+        total = total + ref[...]
+    refs[-1][...] = total
+
+
+def add_all(arrays):
+    return pl.pallas_call(
+        add_kernel,
+        in_specs=[pl.BlockSpec(memory_space=pltpu.VMEM)] * len(arrays),
+        out_specs=pl.BlockSpec(memory_space=pltpu.VMEM),
+        out_shape=jax.ShapeDtypeStruct(arrays[0].shape, arrays[0].dtype),
+        name="add_all",
+        cost_estimate=cost(0.7),
+        compiler_params=pltpu.CompilerParams(vmem_limit_bytes=2 * 1024 * 1024),
+    )(*arrays)
 
 
 def cost(micros):
@@ -301,7 +360,7 @@
     )
 
 
-def grad_mixture(out_grad, out_weight, length, early, late):
+def grad_mixture(out_grad, out_weight, length, early, middle, late):
     n_head = lax.axis_size("head")
     n_pairs = n_head // 2
     rows, depth = out_grad.shape
@@ -314,6 +373,8 @@
     core = lax.axis_index("seq") % 2
     slot = (lax.axis_index("seq") // 2) % 2
     info = jnp.stack([side, slot, core]).astype(jnp.int32)
+    pair, core, slot = (value.astype(jnp.uint32) for value in (pair, core, slot))
+    nothing = jnp.uint32(0)
     hops = sorted(range(1, n_pairs), key=lambda k: (bin(k).count("1"), -k))
     order = [(0, hop) for hop in hops if hop & (hop - 1) == 0]
     order += [(1, hop) for hop in hops[:1]]
@@ -324,12 +385,13 @@
     fetched = {
         (piece, 0): lax.dynamic_slice(
             out_weight,
-            (core * half + piece * piece_size, slot * part_depth),
+            (core * half + jnp.uint32(piece * piece_size), slot * part_depth),
             (piece_size, part_depth),
         )
         for piece in range(PIECES)
     }
-    sets = [out_grad, flip(out_grad, "head", 1), None, None]
+    rows_after, _ = lax.optimization_barrier((out_grad, fetched[0, 0]))
+    sets = [out_grad, flip(rows_after, "head", 1), None, None]
     across = {}
     arrived = {}
     for step in range(len(waves) + 2):
@@ -342,48 +404,69 @@
         for key in landed:
             across[key] = flip(fetched[key], "seq", 2)
         made = []
+        if step == 0:
+            sets[2] = flip(rows_after, "seq", 1)
+            made.append(sets[2])
         if step == 1:
-            sets[2] = flip(out_grad, "seq", 1)
-            made += [sets[1], early()]
+            weight, _ = lax.optimization_barrier((out_weight, fetched[waves[0][0]]))
+            mine = lax.dynamic_slice(weight, (core * half, nothing), (half, depth))
+            made += [mine, sets[1], early(fetched[waves[0][0]])]
         if step == 2:
             sets[3] = flip(sets[1], "seq", 1)
+            all_rows = gather_rows(info, sets)
         if spread:
             shards = [[fetched[key], across[key]] for key in spread]
-            products = project(info, sets, shards)
+            products = project(info, all_rows, shards)
             made += products
             for key, product in zip(spread, products):
                 arrived[key] = flip(product, "head", 2 * key[1])
-        if step == 2:
-            made.append(late(products[0]))
+        if step >= 2 and size < lax.axis_size("seq"):
+            total, _ = lax.optimization_barrier((total, products[0]))
+            total, into = middle(total, into, size)
+            size *= 2
+        if step == len(waves) + 1:
+            while size < lax.axis_size("seq"):
+                total, into = middle(total, into, size)
+                size *= 2
+            attended = late(products[0], into)
         if step == 3:
-            mine = lax.dynamic_slice(out_weight, (core * half, 0), (half, depth))
-            arrived[0, 0] = project(info, sets, [[mine]])[0]
+            arrived[0, 0] = project(info, all_rows, [[mine]])[0]
             made.append(arrived[0, 0])
         if step < len(waves) + 1:
             names = [key for key in fetched if key not in wave]
-            keep, new, far, made = lax.optimization_barrier(
+            carried = (total, into) if step > 1 else ()
+            keep, new, far, made, carried = lax.optimization_barrier(
                 (
                     [fetched[key] for key in names],
                     [fetched[key] for key in wave],
                     [across[key] for key in landed],
                     made,
+                    carried,
                 )
             )
+            if step == 0:
+                sets[2] = made[0]
             if step == 1:
-                sets[1] = made[0]
+                mine, sets[1], total = made
+                into, size = jnp.zeros_like(total), 1
+            elif step > 1:
+                total, into = carried
             fetched.update(zip(names, keep))
             fetched.update(zip(wave, new))
             across.update(zip(landed, far))
+    last = [arrived[key] for key in spread]
+    last, _ = lax.optimization_barrier((last, attended))
+    arrived.update(zip(spread, last))
     mixes = []
     for source in (None, 1):
         mix = jnp.zeros((length, half), BF16)
         for (piece, hop), product in arrived.items():
-            which = core if source is None else 1 - core
+            which = core if source is None else jnp.uint32(1) - core
             product = lax.dynamic_slice(
-                product, (which * 2 * rows, 0), (2 * rows, product.shape[1])
+                product, (which * (2 * rows), nothing), (2 * rows, product.shape[1])
             )
             mix = lax.dynamic_update_slice(
-                mix, product, ((pair ^ hop) * 2 * rows, piece * piece_size)
+                mix, product, ((pair ^ jnp.uint32(hop)) * (2 * rows), jnp.uint32(piece * piece_size))
             )
         mixes.append(mix)
     return mixes[0], flip(mixes[1], "seq", 1)
@@ -426,7 +509,8 @@
     bits = [1 << i for i in range(lax.axis_size("head").bit_length() - 1)]
     for group in (bits[1:3], bits[:1], bits[3:]):
         spans = [sum(chosen) for chosen in subsets(group)]
-        sums = sums + sum(flip(sums, "head", span) for span in spans) if spans else sums
+        if spans:
+            sums = add_all([sums, *(flip(sums, "head", span) for span in spans)])
     return sums
 
 
@@ -446,6 +530,7 @@
     states = pl.BlockSpec((BLK // CHUNK, heads, HEAD_DIM, HEAD_DIM), lambda b, s: (b, 0, 0, 0))
     state = pl.BlockSpec((heads, HEAD_DIM, HEAD_DIM), lambda b, s: (0, 0, 0))
     one_state = shaped((heads, HEAD_DIM, HEAD_DIM), F32)
+    low_state = shaped((heads, HEAD_DIM, HEAD_DIM), BF16)
     all_states = shaped((length // CHUNK, heads, HEAD_DIM, HEAD_DIM), F32)
     low_states = shaped((length // CHUNK, heads, HEAD_DIM, HEAD_DIM), BF16)
     tokens16 = shaped((length, width), BF16)
@@ -455,23 +540,27 @@
 
     kept = {}
 
-    def early():
+    def early(landed):
+        keys, values, _ = lax.optimization_barrier((key_rows, value_rows, landed))
         with jax.named_scope("key_states"):
             before, key_total = call(
                 functools.partial(key_state_kernel, count, heads),
                 "key_states",
                 info,
-                [key_rows, value_rows],
+                [keys, values],
                 [block, block],
                 [all_states, one_state],
                 [states, state],
                 scratch,
             )
         kept["before"] = before
-        kept["into"] = neighbour_states(key_total, doc_starts, length, False)
-        return kept["into"]
-
-    def late(product):
+        return key_total
+
+    def middle(total, into, size):
+        return combine(info, count, length, size, total, flip(total, "seq", size), into)
+
+    def late(product, into):
+        kept["into"] = into
         tokens, _ = lax.optimization_barrier((queries, product))
         with jax.named_scope("attention"):
             kept["attn"], kept["square"], kept["low"] = call(
@@ -485,21 +574,21 @@
             )
         return kept["square"]
 
-    near, far = grad_mixture(out_grad, out_weight, length, early, late)
+    near, far = grad_mixture(out_grad, out_weight, length, early, middle, late)
     attn, square, low = kept["attn"], kept["square"], kept["low"]
 
     with jax.named_scope("cross"):
-        cross = call(
+        sums = call(
             functools.partial(cross_kernel, heads),
             "cross",
             info,
-            [near, far, gate_out, attn],
-            [half_block, half_block, block, block],
-            [row],
-            [line],
+            [near, far, gate_out, attn, square],
+            [half_block, half_block, block, block, line],
+            [shaped((2, length), F32)],
+            [pl.BlockSpec((2, BLK), lambda b, s: (0, b))],
         )[0]
 
-    sums = head_sum(jnp.concatenate([square, cross], axis=0))
+    sums = head_sum(sums)
 
     back = lambda spec_shape, f: pl.BlockSpec(spec_shape, lambda b, s: f(nblocks - 1 - b))
     block_r = back((BLK, width), lambda b: (b, 0))
@@ -507,17 +596,21 @@
     line_r = back((2, BLK), lambda b: (0, b))
     states_r = back((BLK // CHUNK, heads, HEAD_DIM, HEAD_DIM), lambda b: (b, 0, 0, 0))
     with jax.named_scope("grad_attn"):
-        grad, grad_gate, after, query_total = call(
+        grad, grad_gate, after, query_total, query_low = call(
             functools.partial(grad_attn_kernel, count, heads, full_width),
             "grad_attn",
             info,
             [near, far, gate_out, attn, queries, sums],
             [half_r, half_r, block_r, block_r, block_r, line_r],
-            [tokens16, tokens16, all_states, one_state],
-            [block_r, block_r, states_r, state],
+            [tokens16, tokens16, all_states, one_state, low_state],
+            [block_r, block_r, states_r, state, state],
             scratch,
+            4.0,
         )
-    out_of = neighbour_states(query_total, doc_starts, length, True)
+    landed = [
+        flip(query_total if step == 1 else query_low, "seq", step)
+        for step in range(1, lax.axis_size("seq"))
+    ]
     with jax.named_scope("grad_queries"):
         grad_queries = call(
             functools.partial(grad_query_kernel, count, heads),
@@ -535,11 +628,11 @@
             functools.partial(grad_key_value_kernel, count, heads, length),
             "grad_keys_values",
             info,
-            [grad, queries, key_rows, value_rows, after, out_of],
-            [block, block, block, block, states, state],
+            [grad, queries, key_rows, value_rows, after, *landed],
+            [block, block, block, block, states] + [state] * len(landed),
             [tokens16, tokens16],
             [block, block],
-            (),
+            scratch,
             8.0,
         )
     return (grad_queries, grad_keys, grad_values, grad_gate)

time: 193 us -> 182 us (0.943)
  waiting for transfers between devices: 78.6 us -> 87.8 us
  between operations: 8.38 us -> 0.97 us
  Pallas kernels: 53.5 us -> 47.9 us
  local copies, waits for them, and re-layouts: 15.4 us -> 11.3 us
    ppermute x31, waiting for transfers between devices: 78.6 us -> 87.8 us  [flip(): lax.ppermute(a, axis, [(i, i ^ bit) for i in range(lax.axis_size(axis))])]
    pallas_call x4 -> x9, Pallas kernels: 23.7 us -> 18.2 us  [the longest x4 12.7 us: project(): pl.pallas_call(functools.partial(project_kernel, len(shards[0])), grid_sp...]
    unnamed x42 -> x36, local copies, waits for them, and re-layouts: 10.5 us -> 7 us
  transfers between devices with their start and end apart: 31 -> 31, of which waited for: 11 -> 16; matrix products, arithmetic and copies ran while one was open for 3% -> 1% of each run, Pallas kernels for 19% -> 16%
where the time goes in v3:
time: 182 us
  waiting for transfers between devices  87.8 us (48%)
  Pallas kernels  47.9 us (26%)
  starting transfers between devices  34 us (19%)
  local copies, waits for them, and re-layouts  11.3 us (6%)
    ppermute x31, waiting for transfers between devices, flip(): lax.ppermute(a, axis, [(i, i ^ bit) for i in range(lax.axis_size(axis))])  87.8 us
    ppermute x31, starting transfers between devices, flip(): lax.ppermute(a, axis, [(i, i ^ bit) for i in range(lax.axis_size(axis))])  34 us
    pallas_call x6, Pallas kernels, call(): pl.pallas_call(kernel, grid_spec=pltpu.PrefetchScalarGridSpec(num_scalar_...  29.7 us
    pallas_call x4, Pallas kernels, project(): pl.pallas_call(functools.partial(project_kernel, len(shards[0])), grid_sp...  12.7 us
    unnamed x36, local copies, waits for them, and re-layouts  7 us
  transfers between devices with their start and end apart: 31, of which 16 were waited for; matrix products, arithmetic and copies ran while one was open for 1% of the time, Pallas kernels for 16%

profile of v3, /device:TPU:0, one launch (start us, length us, event | category | flops | bytes accessed | tf_op | source)
XLA Modules:
  0.0 182.1 jit_solution(8347367529686321277)
XLA Ops:
  0.7 2.2 %fusion = (bf16[128,2048]{1,0:T(8,128)(2,1)}, bf16[128,2048]{1,0:T(8,128)(2,1)S(1)}) fusion(bf16[512,4096]{1,0:T(8,128)(2,1)} %param.8, u32[]{:T(128)S(6)} %add.19, u32[]{:T(128)S(6)} %mul.20, u32[]{:T(128)S(6)} %mul.19), kind=kLoop, calls=%fused_computation.17 | loop fusion | bytes 2097164 | tf_op jit(solution)/shard_map/dynamic_slice | solution.py:386
  3.4 2.5 %collective-permute-start.7 = (bf16[256,4096]{1,0:T(8,128)(2,1)S(1)}, bf16[256,4096]{1,0:T(8,128)(2,1)}, u32[]{:S(2)}, u32[]{:S(2)}) collective-permute-start(bf16[256,4096]{1,0:T(8,128)(2,1)S(1)} %copy-done), channel_id=1, source_target_pairs={{0,1},{1,0},{2,3},{3,2},{4,5},{5,4},{6,7},{7,6},{8,9},{9,8},{10,11... | collective-permute-start | bytes 6291464 | tf_op jit(solution)/shard_map/ppermute | solution.py:498
  5.9 2.6 %collective-permute-start = (bf16[128,2048]{1,0:T(8,128)(2,1)S(1)}, bf16[128,2048]{1,0:T(8,128)(2,1)}, u32[]{:S(2)}, u32[]{:S(2)}) collective-permute-start(bf16[128,2048]{1,0:T(8,128)(2,1)S(1)} %get-tuple-element.119), channel_id=1, source_target_pairs={{0,4},{1,5},{2,6},{3,7},{4,0},{5,1},{6,2},{7,3},{8,12},{9,13},{10,... | collective-permute-start | bytes 1572872 | tf_op jit(solution)/shard_map/ppermute | solution.py:498
  10.1 22.2 %collective-permute-done.refs_0_ = bf16[128,2048]{1,0:T(8,128)(2,1)} collective-permute-done((bf16[128,2048]{1,0:T(8,128)(2,1)S(1)}, bf16[128,2048]{1,0:T(8,128)(2,1)}, u32[]{:S(2)}, u32[]{:S(2)}) %collective-permute-start) | collective-permute-done | bytes 524320 | tf_op jit(solution)/shard_map/ppermute | solution.py:498
  36.1 2.4 %collective-permute-start.3 = (bf16[128,2048]{1,0:T(8,128)(2,1)}, bf16[128,2048]{1,0:T(8,128)(2,1)S(1)}, u32[]{:S(2)}, u32[]{:S(2)}) collective-permute-start(bf16[128,2048]{1,0:T(8,128)(2,1)} %get-tuple-element.77), channel_id=1, source_target_pairs={{0,4},{1,5},{2,6},{3,7},{4,0},{5,1},{6,2},{7,3},{8,12},{9,13},{10,... | collective-permute-start | bytes 1572872 | tf_op jit(solution)/shard_map/ppermute | solution.py:498
  42.3 2.3 %key_states.1 = (f32[8,4,128,128]{3,2,1,0:T(8,128)S(1)}, f32[4,128,128]{2,1,0:T(8,128)S(1)}) custom-call(s32[5]{0:T(128)S(1)} %pad_add_fusion.info, bf16[2048,512]{1,0:T(8,128)(2,1)S(1)} %copy-done.4, bf16[2048,512]{1,0:T(8,128)(2,1)S(1)} %copy-done.6), custom_call_target="tpu_custom_call" | custom-call | flops 3449999872 | tf_op jit(solution)/shard_map/key_states/key_states/pallas_call | solution.py:477
  47.3 5.0 %collective-permute-done.7.refs_1_ = bf16[256,4096]{1,0:T(8,128)(2,1)} collective-permute-done((bf16[256,4096]{1,0:T(8,128)(2,1)S(1)}, bf16[256,4096]{1,0:T(8,128)(2,1)}, u32[]{:S(2)}, u32[]{:S(2)}) %collective-permute-start.7) | collective-permute-done | bytes 2097184 | tf_op jit(solution)/shard_map/ppermute | solution.py:498
  52.3 9.4 %collective-permute-done.3.refs_0_ = bf16[128,2048]{1,0:T(8,128)(2,1)S(1)} collective-permute-done((bf16[128,2048]{1,0:T(8,128)(2,1)}, bf16[128,2048]{1,0:T(8,128)(2,1)S(1)}, u32[]{:S(2)}, u32[]{:S(2)}) %collective-permute-start.3) | collective-permute-done | bytes 524320 | tf_op jit(solution)/shard_map/ppermute | solution.py:498
  67.8 3.6 %gather_rows.1.rows_ref = bf16[1024,4096]{1,0:T(8,128)(2,1)S(1)} custom-call(s32[3]{0:T(128)S(1)} %pad_add_fusion.1.info, bf16[256,4096]{1,0:T(8,128)(2,1)S(1)} %copy-done, bf16[256,4096]{1,0:T(8,128)(2,1)} %collective-permute-done.7.refs_1_, bf16[256,4096]{1,0:T(8,128)(2,1)} %collective-permute-done.2.refs_2_, bf16[256,4096]{1,0:T(8,128)(2,1)} %collective-permute-done.8.refs_3_), custom_call_target="tpu_custom_call" | custom-call | flops 3449999872 | tf_op jit(solution)/shard_map/gather_rows/pallas_call | solution.py:285
  71.4 4.0 %project.4 = (bf16[1024,128]{1,0:T(8,128)(2,1)S(1)}, bf16[1024,128]{1,0:T(8,128)(2,1)S(1)}) custom-call(s32[3]{0:T(128)S(1)} %pad_add_fusion.1.info, bf16[1024,4096]{1,0:T(8,128)(2,1)S(1)} %gather_rows.1.rows_ref, bf16[128,2048]{1,0:T(8,128)(2,1)} %collective-permute-done.refs_0_, bf16[128,2048]{1,0:T(8,128)(2,1)S(1)} %copy-done.11, ...), custom_call_target="tpu_custom_call" | custom-call | flops 3449999872 | tf_op jit(solution)/shard_map/project/pallas_call | solution.py:323
  75.6 2.9 %project.6 = bf16[1024,256]{1,0:T(8,128)(2,1)S(1)} custom-call(s32[3]{0:T(128)S(1)} %pad_add_fusion.1.info, bf16[1024,4096]{1,0:T(8,128)(2,1)S(1)} %gather_rows.1.rows_ref, bf16[256,4096]{1,0:T(8,128)(2,1)S(1)} %copy-done.1), custom_call_target="tpu_custom_call" | custom-call | flops 3449999872 | tf_op jit(solution)/shard_map/project/pallas_call | solution.py:323
  79.8 14.8 %collective-permute-done.11.refs_0_ = bf16[128,2048]{1,0:T(8,128)(2,1)S(1)} collective-permute-done((bf16[128,2048]{1,0:T(8,128)(2,1)}, bf16[128,2048]{1,0:T(8,128)(2,1)S(1)}, u32[]{:S(2)}, u32[]{:S(2)}) %collective-permute-start.11) | collective-permute-done | bytes 524320 | tf_op jit(solution)/shard_map/ppermute | solution.py:498
  94.6 2.9 %project.5 = (bf16[1024,128]{1,0:T(8,128)(2,1)S(1)}, bf16[1024,128]{1,0:T(8,128)(2,1)S(1)}) custom-call(s32[3]{0:T(128)S(1)} %pad_add_fusion.1.info, bf16[1024,4096]{1,0:T(8,128)(2,1)S(1)} %gather_rows.1.rows_ref, bf16[128,2048]{1,0:T(8,128)(2,1)S(1)} %collective-permute-done.3.refs_0_, bf16[128,2048]{1,0:T(8,128)(2,1)S(1)} %collective-permute-done.13.refs_1_, ...), custom_call_target="tpu_custom_call" | custom-call | flops 3449999872 | tf_op jit(solution)/shard_map/project/pallas_call | solution.py:323
  97.5 3.0 %collective-permute-start.16 = (bf16[1024,128]{1,0:T(8,128)(2,1)S(1)}, bf16[1024,128]{1,0:T(8,128)(2,1)S(1)}, u32[]{:S(2)}, u32[]{:S(2)}) collective-permute-start(bf16[1024,128]{1,0:T(8,128)(2,1)S(1)} %get-tuple-element.88), channel_id=1, source_target_pairs={{0,4},{1,5},{2,6},{3,7},{4,0},{5,1},{6,2},{7,3},{8,12},{9,13},{10,... | collective-permute-start | bytes 786440 | tf_op jit(solution)/shard_map/ppermute | solution.py:498
  108.2 10.7 %collective-permute-done.16 = bf16[1024,128]{1,0:T(8,128)(2,1)S(1)} collective-permute-done((bf16[1024,128]{1,0:T(8,128)(2,1)S(1)}, bf16[1024,128]{1,0:T(8,128)(2,1)S(1)}, u32[]{:S(2)}, u32[]{:S(2)}) %collective-permute-start.16) | collective-permute-done | bytes 262176 | tf_op jit(solution)/shard_map/ppermute | solution.py:498
  119.2 8.4 %collective-permute-done.19.refs_3_ = bf16[128,2048]{1,0:T(8,128)(2,1)S(1)} collective-permute-done((bf16[128,2048]{1,0:T(8,128)(2,1)S(1)}, bf16[128,2048]{1,0:T(8,128)(2,1)S(1)}, u32[]{:S(2)}, u32[]{:S(2)}) %collective-permute-start.19) | collective-permute-done | bytes 524320 | tf_op jit(solution)/shard_map/ppermute | solution.py:498
  127.6 2.9 %project.7 = (bf16[1024,128]{1,0:T(8,128)(2,1)S(1)}, bf16[1024,128]{1,0:T(8,128)(2,1)S(1)}) custom-call(s32[3]{0:T(128)S(1)} %pad_add_fusion.1.info, bf16[1024,4096]{1,0:T(8,128)(2,1)S(1)} %gather_rows.1.rows_ref, bf16[128,2048]{1,0:T(8,128)(2,1)S(1)} %collective-permute-done.11.refs_0_, bf16[128,2048]{1,0:T(8,128)(2,1)S(1)} %collective-permute-done.18.refs_1_, ...), custom_call_target="tpu_custom_call" | custom-call | flops 3449999872 | tf_op jit(solution)/shard_map/project/pallas_call | solution.py:323
  132.4 5.4 %attention.1 = (f32[2048,512]{1,0:T(8,128)S(1)}, f32[1,2048]{1,0:T(1,128)S(1)}, bf16[8,4,128,128]{3,2,1,0:T(8,128)(2,1)S(1)}) custom-call(s32[5]{0:T(128)S(1)} %pad_add_fusion.info, bf16[2048,512]{1,0:T(8,128)(2,1)S(1)} %copy-done.3, bf16[2048,512]{1,0:T(8,128)(2,1)S(1)} %copy-done.5, bf16[2048,512]{1,0:T(8,128)(2,1)S(1)} %copy-done.7, ...), custom_call_target="tpu_custom_call" | custom-call | flops 3449999872 | tf_op jit(solution)/shard_map/attention/attention/pallas_call | solution.py:477
  139.4 3.4 %collective-permute-done.22 = bf16[1024,128]{1,0:T(8,128)(2,1)S(1)} collective-permute-done((bf16[1024,128]{1,0:T(8,128)(2,1)S(1)}, bf16[1024,128]{1,0:T(8,128)(2,1)S(1)}, u32[]{:S(2)}, u32[]{:S(2)}) %collective-permute-start.22) | collective-permute-done | bytes 262176 | tf_op jit(solution)/shard_map/ppermute | solution.py:498
  143.0 2.6 %collective-permute-done.23.far_ref = bf16[2048,256]{1,0:T(8,128)(2,1)S(1)} collective-permute-done((bf16[2048,256]{1,0:T(8,128)(2,1)S(1)}, bf16[2048,256]{1,0:T(8,128)(2,1)S(1)}, u32[]{:S(2)}, u32[]{:S(2)}) %collective-permute-start.23) | collective-permute-done | bytes 1048608 | tf_op jit(solution)/shard_map/ppermute | solution.py:498
  156.5 3.2 %collective-permute-done.27.refs_1_ = f32[2,2048]{1,0:T(2,128)S(1)} collective-permute-done((f32[2,2048]{1,0:T(2,128)S(1)}, f32[2,2048]{1,0:T(2,128)S(1)}, u32[]{:S(2)}, u32[]{:S(2)}) %collective-permute-start.27) | collective-permute-done | bytes 16416 | tf_op jit(solution)/shard_map/ppermute | solution.py:498
  159.7 5.8 %grad_attn.1 = (bf16[2048,512]{1,0:T(8,128)(2,1)S(1)}, bf16[2048,512]{1,0:T(8,128)(2,1)}, f32[8,4,128,128]{3,2,1,0:T(8,128)S(1)}, f32[4,128,128]{2,1,0:T(8,128)S(1)}, bf16[4,128,128]{2,1,0:T(8,128)(2,1)S(1)}) custom-call(s32[5]{0:T(128)S(1)} %pad_add_fusion.info, bf16[2048,256]{1,0:T(8,128)(2,1)S(1)} %get-tuple-element.123.near_ref, ...), custom_call_target="tpu_custom_call" | custom-call | flops 4600000000 | tf_op jit(solution)/shard_map/grad_attn/grad_attn/pallas_call | solution.py:477
  167.6 5.7 %grad_queries.1 = bf16[2048,512]{1,0:T(8,128)(2,1)} custom-call(s32[5]{0:T(128)S(1)} %pad_add_fusion.info, bf16[2048,512]{1,0:T(8,128)(2,1)S(1)} %get-tuple-element.110.grad_ref, bf16[2048,512]{1,0:T(8,128)(2,1)S(1)} %copy-done.5, bf16[2048,512]{1,0:T(8,128)(2,1)S(1)} %copy-done.7, bf16[8,4,128,128]{3,2,1,0:T(8,128)(2,1)S(1)} %get-tuple-element.111.low_ref), custom_call_target="tpu_custom_call" | custom-call | flops 9200000000 | tf_op jit(solution)/shard_map/grad_queries/grad_queries/pallas_call | solution.py:477
  173.4 8.7 %grad_keys_values.1 = (bf16[2048,512]{1,0:T(8,128)(2,1)}, bf16[2048,512]{1,0:T(8,128)(2,1)}) custom-call(s32[5]{0:T(128)S(1)} %pad_add_fusion.info, bf16[2048,512]{1,0:T(8,128)(2,1)S(1)} %get-tuple-element.110.grad_ref, bf16[2048,512]{1,0:T(8,128)(2,1)S(1)} %copy-done.3, bf16[2048,512]{1,0:T(8,128)(2,1)S(1)} %copy-done.5, bf16[2048,512]{1,0:T(8,128)(2,1)S(1)} %copy-done.7, ...), custom_call_target="tpu_custom_call" | custom-call | flops 9200000000 | tf_op jit(solution)/shard_map/grad_keys_values/grad_keys_values/pallas_call | solution.py:477
  (104 shorter events, 44.6 us)
Async XLA Ops:
  2.9 29.4 %collective-permute-start.2 = (bf16[256,4096]{1,0:T(8,128)(2,1)S(1)}, bf16[256,4096]{1,0:T(8,128)(2,1)}, u32[]{:S(2)}, u32[]{:S(2)}) collective-permute-start(bf16[256,4096]{1,0:T(8,128)(2,1)S(1)} %copy-done), channel_id=1, source_target_pairs={{0,8},{8,0},{16,24},{24,16},{1,9},{9,1},{17,25},{25,17},{2,10},{10... | collective-permute-start | bytes 6291464 | tf_op jit(solution)/shard_map/ppermute | solution.py:498
  3.4 48.9 %collective-permute-start.7 = (bf16[256,4096]{1,0:T(8,128)(2,1)S(1)}, bf16[256,4096]{1,0:T(8,128)(2,1)}, u32[]{:S(2)}, u32[]{:S(2)}) collective-permute-start(bf16[256,4096]{1,0:T(8,128)(2,1)S(1)} %copy-done), channel_id=1, source_target_pairs={{0,1},{1,0},{2,3},{3,2},{4,5},{5,4},{6,7},{7,6},{8,9},{9,8},{10,11... | collective-permute-start | bytes 6291464 | tf_op jit(solution)/shard_map/ppermute | solution.py:498
  5.9 26.4 %collective-permute-start = (bf16[128,2048]{1,0:T(8,128)(2,1)S(1)}, bf16[128,2048]{1,0:T(8,128)(2,1)}, u32[]{:S(2)}, u32[]{:S(2)}) collective-permute-start(bf16[128,2048]{1,0:T(8,128)(2,1)S(1)} %get-tuple-element.119), channel_id=1, source_target_pairs={{0,4},{1,5},{2,6},{3,7},{4,0},{5,1},{6,2},{7,3},{8,12},{9,13},{10,... | collective-permute-start | bytes 1572872 | tf_op jit(solution)/shard_map/ppermute | solution.py:498
  8.5 23.9 %collective-permute-start.1 = (bf16[128,2048]{1,0:T(8,128)(2,1)S(1)}, bf16[128,2048]{1,0:T(8,128)(2,1)S(1)}, u32[]{:S(2)}, u32[]{:S(2)}) collective-permute-start(bf16[128,2048]{1,0:T(8,128)(2,1)S(1)} %get-tuple-element.119), channel_id=1, source_target_pairs={{0,2},{1,3},{2,0},{3,1},{4,6},{5,7},{6,4},{7,5},{8,10},{9,11},{10,... | collective-permute-start | bytes 1572872 | tf_op jit(solution)/shard_map/ppermute | solution.py:498
  33.2 28.4 %collective-permute-start.4 = (bf16[128,2048]{1,0:T(8,128)(2,1)}, bf16[128,2048]{1,0:T(8,128)(2,1)S(1)}, u32[]{:S(2)}, u32[]{:S(2)}) collective-permute-start(bf16[128,2048]{1,0:T(8,128)(2,1)} %collective-permute-done.refs_0_), channel_id=1, source_target_pairs={{0,2},{1,3},{2,0},{3,1},{4,6},{5,7},{6,4},{7,5},{8,10},{9,11},{10,... | collective-permute-start | bytes 1572872 | tf_op jit(solution)/shard_map/ppermute | solution.py:498
  34.6 27.0 %collective-permute-start.5 = (bf16[128,2048]{1,0:T(8,128)(2,1)}, bf16[128,2048]{1,0:T(8,128)(2,1)S(1)}, u32[]{:S(2)}, u32[]{:S(2)}) collective-permute-start(bf16[128,2048]{1,0:T(8,128)(2,1)} %collective-permute-done.refs_0_), channel_id=1, source_target_pairs={{0,16},{8,24},{16,0},{24,8},{1,17},{9,25},{17,1},{25,9},{2,18},{10... | collective-permute-start | bytes 1572872 | tf_op jit(solution)/shard_map/ppermute | solution.py:498
  36.1 25.5 %collective-permute-start.3 = (bf16[128,2048]{1,0:T(8,128)(2,1)}, bf16[128,2048]{1,0:T(8,128)(2,1)S(1)}, u32[]{:S(2)}, u32[]{:S(2)}) collective-permute-start(bf16[128,2048]{1,0:T(8,128)(2,1)} %get-tuple-element.77), channel_id=1, source_target_pairs={{0,4},{1,5},{2,6},{3,7},{4,0},{5,1},{6,2},{7,3},{8,12},{9,13},{10,... | collective-permute-start | bytes 1572872 | tf_op jit(solution)/shard_map/ppermute | solution.py:498
  38.6 23.9 %collective-permute-start.6 = (bf16[128,2048]{1,0:T(8,128)(2,1)}, bf16[128,2048]{1,0:T(8,128)(2,1)S(1)}, u32[]{:S(2)}, u32[]{:S(2)}) collective-permute-start(bf16[128,2048]{1,0:T(8,128)(2,1)} %copy-done.8), channel_id=1, source_target_pairs={{0,16},{8,24},{16,0},{24,8},{1,17},{9,25},{17,1},{25,9},{2,18},{10... | collective-permute-start | bytes 1572872 | tf_op jit(solution)/shard_map/ppermute | solution.py:498
  63.4 31.2 %collective-permute-start.12 = (bf16[128,2048]{1,0:T(8,128)(2,1)S(1)}, bf16[128,2048]{1,0:T(8,128)(2,1)S(1)}, u32[]{:S(2)}, u32[]{:S(2)}) collective-permute-start(bf16[128,2048]{1,0:T(8,128)(2,1)S(1)} %collective-permute-done.3.refs_0_), channel_id=1, source_target_pairs={{0,2},{1,3},{2,0},{3,1},{4,6},{5,7},{6,4},{7,5},{8,10},{9,11},{10,... | collective-permute-start | bytes 1572872 | tf_op jit(solution)/shard_map/ppermute | solution.py:498
  63.4 31.2 %collective-permute-start.13 = (bf16[128,2048]{1,0:T(8,128)(2,1)S(1)}, bf16[128,2048]{1,0:T(8,128)(2,1)S(1)}, u32[]{:S(2)}, u32[]{:S(2)}) collective-permute-start(bf16[128,2048]{1,0:T(8,128)(2,1)S(1)} %collective-permute-done.3.refs_0_), channel_id=1, source_target_pairs={{0,16},{8,24},{16,0},{24,8},{1,17},{9,25},{17,1},{25,9},{2,18},{10... | collective-permute-start | bytes 1572872 | tf_op jit(solution)/shard_map/ppermute | solution.py:498
  64.0 30.6 %collective-permute-start.11 = (bf16[128,2048]{1,0:T(8,128)(2,1)}, bf16[128,2048]{1,0:T(8,128)(2,1)S(1)}, u32[]{:S(2)}, u32[]{:S(2)}) collective-permute-start(bf16[128,2048]{1,0:T(8,128)(2,1)} %get-tuple-element.77), channel_id=1, source_target_pairs={{0,2},{1,3},{2,0},{3,1},{4,6},{5,7},{6,4},{7,5},{8,10},{9,11},{10,... | collective-permute-start | bytes 1572872 | tf_op jit(solution)/shard_map/ppermute | solution.py:498
  65.9 28.7 %collective-permute-start.14 = (bf16[128,2048]{1,0:T(8,128)(2,1)S(1)}, bf16[128,2048]{1,0:T(8,128)(2,1)S(1)}, u32[]{:S(2)}, u32[]{:S(2)}) collective-permute-start(bf16[128,2048]{1,0:T(8,128)(2,1)S(1)} %collective-permute-done.4.refs_2_), channel_id=1, source_target_pairs={{0,16},{8,24},{16,0},{24,8},{1,17},{9,25},{17,1},{25,9},{2,18},{10... | collective-permute-start | bytes 1572872 | tf_op jit(solution)/shard_map/ppermute | solution.py:498
  78.6 24.0 %collective-permute-start.9 = (bf16[1024,128]{1,0:T(8,128)(2,1)S(1)}, bf16[1024,128]{1,0:T(8,128)(2,1)S(1)}, u32[]{:S(2)}, u32[]{:S(2)}) collective-permute-start(bf16[1024,128]{1,0:T(8,128)(2,1)S(1)} %get-tuple-element.75), channel_id=1, source_target_pairs={{0,4},{1,5},{2,6},{3,7},{4,0},{5,1},{6,2},{7,3},{8,12},{9,13},{10,... | collective-permute-start | bytes 786440 | tf_op jit(solution)/shard_map/ppermute | solution.py:498
  94.6 10.3 %collective-permute-start.10 = (bf16[1024,128]{1,0:T(8,128)(2,1)S(1)}, bf16[1024,128]{1,0:T(8,128)(2,1)S(1)}, u32[]{:S(2)}, u32[]{:S(2)}) collective-permute-start(bf16[1024,128]{1,0:T(8,128)(2,1)S(1)} %get-tuple-element.76), channel_id=1, source_target_pairs={{0,2},{1,3},{2,0},{3,1},{4,6},{5,7},{6,4},{7,5},{8,10},{9,11},{10,... | collective-permute-start | bytes 786440 | tf_op jit(solution)/shard_map/ppermute | solution.py:498
  97.5 21.4 %collective-permute-start.16 = (bf16[1024,128]{1,0:T(8,128)(2,1)S(1)}, bf16[1024,128]{1,0:T(8,128)(2,1)S(1)}, u32[]{:S(2)}, u32[]{:S(2)}) collective-permute-start(bf16[1024,128]{1,0:T(8,128)(2,1)S(1)} %get-tuple-element.88), channel_id=1, source_target_pairs={{0,4},{1,5},{2,6},{3,7},{4,0},{5,1},{6,2},{7,3},{8,12},{9,13},{10,... | collective-permute-start | bytes 786440 | tf_op jit(solution)/shard_map/ppermute | solution.py:498
  100.5 6.4 %collective-permute-start.20 = (bf16[4,128,128]{2,1,0:T(8,128)(2,1)S(1)}, bf16[4,128,128]{2,1,0:T(8,128)(2,1)S(1)}, u32[]{:S(2)}, u32[]{:S(2)}) collective-permute-start(bf16[4,128,128]{2,1,0:T(8,128)(2,1)S(1)} %get-tuple-element.94.total_ref), channel_id=1, source_target_pairs={{0,16},{8,24},{16,0},{24,8},{1,17},{9,25},{17,1},{25,9},{2,18},{10... | collective-permute-start | bytes 393224 | tf_op jit(solution)/shard_map/ppermute | solution.py:498
  101.0 18.1 %collective-permute-start.18 = (bf16[128,2048]{1,0:T(8,128)(2,1)S(1)}, bf16[128,2048]{1,0:T(8,128)(2,1)S(1)}, u32[]{:S(2)}, u32[]{:S(2)}) collective-permute-start(bf16[128,2048]{1,0:T(8,128)(2,1)S(1)} %collective-permute-done.11.refs_0_), channel_id=1, source_target_pairs={{0,16},{8,24},{16,0},{24,8},{1,17},{9,25},{17,1},{25,9},{2,18},{10... | collective-permute-start | bytes 1572872 | tf_op jit(solution)/shard_map/ppermute | solution.py:498
  102.5 25.0 %collective-permute-start.19 = (bf16[128,2048]{1,0:T(8,128)(2,1)S(1)}, bf16[128,2048]{1,0:T(8,128)(2,1)S(1)}, u32[]{:S(2)}, u32[]{:S(2)}) collective-permute-start(bf16[128,2048]{1,0:T(8,128)(2,1)S(1)} %collective-permute-done.12.refs_2_), channel_id=1, source_target_pairs={{0,16},{8,24},{16,0},{24,8},{1,17},{9,25},{17,1},{25,9},{2,18},{10... | collective-permute-start | bytes 1572872 | tf_op jit(solution)/shard_map/ppermute | solution.py:498
  104.9 14.1 %collective-permute-start.17 = (bf16[1024,128]{1,0:T(8,128)(2,1)S(1)}, bf16[1024,128]{1,0:T(8,128)(2,1)S(1)}, u32[]{:S(2)}, u32[]{:S(2)}) collective-permute-start(bf16[1024,128]{1,0:T(8,128)(2,1)S(1)} %get-tuple-element.89), channel_id=1, source_target_pairs={{0,6},{1,7},{2,4},{3,5},{4,2},{5,3},{6,0},{7,1},{8,14},{9,15},{10,... | collective-permute-start | bytes 786440 | tf_op jit(solution)/shard_map/ppermute | solution.py:498
  130.5 8.9 %collective-permute-start.21 = (bf16[1024,128]{1,0:T(8,128)(2,1)S(1)}, bf16[1024,128]{1,0:T(8,128)(2,1)S(1)}, u32[]{:S(2)}, u32[]{:S(2)}) collective-permute-start(bf16[1024,128]{1,0:T(8,128)(2,1)S(1)} %get-tuple-element.101), channel_id=1, source_target_pairs={{0,2},{1,3},{2,0},{3,1},{4,6},{5,7},{6,4},{7,5},{8,10},{9,11},{10,... | collective-permute-start | bytes 786440 | tf_op jit(solution)/shard_map/ppermute | solution.py:498
  130.8 12.0 %collective-permute-start.22 = (bf16[1024,128]{1,0:T(8,128)(2,1)S(1)}, bf16[1024,128]{1,0:T(8,128)(2,1)S(1)}, u32[]{:S(2)}, u32[]{:S(2)}) collective-permute-start(bf16[1024,128]{1,0:T(8,128)(2,1)S(1)} %get-tuple-element.102), channel_id=1, source_target_pairs={{0,6},{1,7},{2,4},{3,5},{4,2},{5,3},{6,0},{7,1},{8,14},{9,15},{10,... | collective-permute-start | bytes 786440 | tf_op jit(solution)/shard_map/ppermute | solution.py:498
  165.5 7.9 %collective-permute-start.29 = (bf16[4,128,128]{2,1,0:T(8,128)(2,1)S(1)}, bf16[4,128,128]{2,1,0:T(8,128)(2,1)S(1)}, u32[]{:S(2)}, u32[]{:S(2)}) collective-permute-start(bf16[4,128,128]{2,1,0:T(8,128)(2,1)S(1)} %get-tuple-element.114), channel_id=1, source_target_pairs={{0,16},{8,24},{16,0},{24,8},{1,17},{9,25},{17,1},{25,9},{2,18},{10... | collective-permute-start | bytes 393224 | tf_op jit(solution)/shard_map/ppermute | solution.py:498
  166.0 7.4 %collective-permute-start.30 = (bf16[4,128,128]{2,1,0:T(8,128)(2,1)S(1)}, bf16[4,128,128]{2,1,0:T(8,128)(2,1)S(1)}, u32[]{:S(2)}, u32[]{:S(2)}) collective-permute-start(bf16[4,128,128]{2,1,0:T(8,128)(2,1)S(1)} %get-tuple-element.114), channel_id=1, source_target_pairs={{0,24},{8,16},{16,8},{24,0},{1,25},{9,17},{17,9},{25,1},{2,26},{10... | collective-permute-start | bytes 393224 | tf_op jit(solution)/shard_map/ppermute | solution.py:498
  166.0 7.4 %collective-permute-start.28 = (f32[4,128,128]{2,1,0:T(8,128)S(1)}, f32[4,128,128]{2,1,0:T(8,128)S(1)}, u32[]{:S(2)}, u32[]{:S(2)}) collective-permute-start(f32[4,128,128]{2,1,0:T(8,128)S(1)} %get-tuple-element.113), channel_id=1, source_target_pairs={{0,8},{8,0},{16,24},{24,16},{1,9},{9,1},{17,25},{25,17},{2,10},{10... | collective-permute-start | bytes 786440 | tf_op jit(solution)/shard_map/ppermute | solution.py:498
  (25 other events, 111.9 us)

commit v4 on v3

--- a/solution.py
+++ b/solution.py
@@ -9,6 +9,7 @@
 
 HEAD_DIM = 128
 BLK = 512
+LARGE = 1024
 CHUNK = 256
 EPS = 1e-06
 F32 = jnp.float32
@@ -97,21 +98,26 @@
     count, heads, info, q_ref, k_ref, v_ref, before_ref, into_ref, attn_ref, square_ref, low_ref
 ):
     first = info[count]
-    for r in range(BLK // CHUNK):
+    size = q_ref.shape[0]
+    for r in range(size // CHUNK):
         rows = chunk_rows(r)
-        start = first + pl.program_id(0) * BLK + r * CHUNK
+        start = first + pl.program_id(0) * size + r * CHUNK
         prior = doc_of(info, count, start - 1)
         carry = same(prior, doc_of(info, count, first - 1))
         mask = causal_mask(info, count, start, False)
         keep_in = same(column_docs(info, count, start, CHUNK), prior)
-        squares = jnp.zeros((CHUNK, HEAD_DIM), F32)
+        probs, carried = [], []
         for h in range(heads):
             at = head_slice(h)
             low = (before_ref[r, h] + carry * into_ref[h]).astype(BF16)
             low_ref[r, h] = low
             q = q_ref[rows, at]
-            probs = jnp.where(mask, dot_nt(q, k_ref[rows, at]), 0.0).astype(BF16)
-            out = keep_in * dot(q, low) + dot(probs, v_ref[rows, at])
+            probs.append(jnp.where(mask, dot_nt(q, k_ref[rows, at]), 0.0).astype(BF16))
+            carried.append(keep_in * dot(q, low))
+        squares = jnp.zeros((CHUNK, HEAD_DIM), F32)
+        for h in range(heads):
+            at = head_slice(h)
+            out = carried[h] + dot(probs[h], v_ref[rows, at])
             attn_ref[rows, at] = out
             squares = squares + out * out
         square_ref[:, rows] = lane_sums(squares)
@@ -182,18 +188,22 @@
 
 
 def grad_query_kernel(count, heads, info, grad_ref, k_ref, v_ref, low_ref, out_ref):
-    for r in range(BLK // CHUNK):
+    size = grad_ref.shape[0]
+    for r in range(size // CHUNK):
         rows = chunk_rows(r)
-        start = info[count] + pl.program_id(0) * BLK + r * CHUNK
+        start = info[count] + pl.program_id(0) * size + r * CHUNK
         prior = doc_of(info, count, start - 1)
         mask = causal_mask(info, count, start, False)
         keep_in = same(column_docs(info, count, start, CHUNK), prior)
+        dprobs, carried = [], []
         for h in range(heads):
             at = head_slice(h)
             grad = grad_ref[rows, at]
-            dprob = jnp.where(mask, dot_nt(grad, v_ref[rows, at]), 0.0).astype(BF16)
-            out = keep_in * dot_nt(grad, low_ref[r, h]) + dot(dprob, k_ref[rows, at])
-            out_ref[rows, at] = out.astype(BF16)
+            dprobs.append(jnp.where(mask, dot_nt(grad, v_ref[rows, at]), 0.0).astype(BF16))
+            carried.append(keep_in * dot_nt(grad, low_ref[r, h]))
+        for h in range(heads):
+            at = head_slice(h)
+            out_ref[rows, at] = (carried[h] + dot(dprobs[h], k_ref[rows, at])).astype(BF16)
 
 
 def grad_key_value_kernel(
@@ -201,6 +211,7 @@
 ):
     *landed, dk_ref, dv_ref, into_ref = refs
     first = info[count]
+    size = grad_ref.shape[0]
 
     @pl.when(pl.program_id(0) == 0)
     def _():
@@ -215,21 +226,27 @@
             total = term if total is None else total + term
         into_ref[...] = total
 
-    for r in range(BLK // CHUNK):
+    for r in range(size // CHUNK):
         rows = chunk_rows(r)
-        start = first + pl.program_id(0) * BLK + r * CHUNK
+        start = first + pl.program_id(0) * size + r * CHUNK
         last_doc = doc_of(info, count, start + CHUNK - 1)
         carry = same(last_doc, doc_of(info, count, first + length - 1))
         mask = causal_mask(info, count, start, True)
         keep_out = same(column_docs(info, count, start, CHUNK), last_doc)
-        for h in range(heads):
-            at = head_slice(h)
-            low = (after_ref[r, h] + carry * into_ref[h]).astype(BF16)
-            k, v, q, grad = k_ref[rows, at], v_ref[rows, at], q_ref[rows, at], grad_ref[rows, at]
-            dprob = jnp.where(mask, dot_nt(v, grad), 0.0).astype(BF16)
-            probs = jnp.where(mask, dot_nt(k, q), 0.0).astype(BF16)
-            dk_ref[rows, at] = (keep_out * dot_nt(v, low) + dot(dprob, q)).astype(BF16)
-            dv_ref[rows, at] = (keep_out * dot(k, low) + dot(probs, grad)).astype(BF16)
+        for pair in range(0, heads, 2):
+            parts = []
+            for h in range(pair, min(pair + 2, heads)):
+                at = head_slice(h)
+                low = (after_ref[r, h] + carry * into_ref[h]).astype(BF16)
+                k, v = k_ref[rows, at], v_ref[rows, at]
+                dprob = jnp.where(mask, dot_nt(v, grad_ref[rows, at]), 0.0).astype(BF16)
+                probs = jnp.where(mask, dot_nt(k, q_ref[rows, at]), 0.0).astype(BF16)
+                parts.append(
+                    (at, dprob, probs, keep_out * dot_nt(v, low), keep_out * dot(k, low))
+                )
+            for at, dprob, probs, from_v, from_k in parts:
+                dk_ref[rows, at] = (from_v + dot(dprob, q_ref[rows, at])).astype(BF16)
+                dv_ref[rows, at] = (from_k + dot(probs, grad_ref[rows, at])).astype(BF16)
 
 
 def combine_kernel(count, length, size, info, total_ref, other_ref, into_ref, *outs):
@@ -325,7 +342,8 @@
         grid_spec=pltpu.PrefetchScalarGridSpec(
             num_scalar_prefetch=1,
             grid=(1,),
-            in_specs=[pl.BlockSpec(memory_space=pltpu.VMEM) for a in args],
+            in_specs=[pl.BlockSpec(memory_space=pltpu.VMEM)]
+            * len(args),
             out_specs=[pl.BlockSpec(memory_space=pltpu.VMEM) for o in outs],
         ),
         out_shape=outs,
@@ -380,6 +398,7 @@
     order += [(1, hop) for hop in hops[:1]]
     order += [(0, hop) for hop in hops if hop & (hop - 1) != 0]
     order += [(1, hop) for hop in hops[1:]]
+    order[-2], order[-1] = order[-1], order[-2]
     waves = [order[i : i + 2] for i in range(0, len(order), 2)]
 
     fetched = {
@@ -414,19 +433,20 @@
         if step == 2:
             sets[3] = flip(sets[1], "seq", 1)
             all_rows = gather_rows(info, sets)
+        last_step = step == len(waves) + 1
         if spread:
             shards = [[fetched[key], across[key]] for key in spread]
             products = project(info, all_rows, shards)
             made += products
             for key, product in zip(spread, products):
                 arrived[key] = flip(product, "head", 2 * key[1])
-        if step >= 2 and size < lax.axis_size("seq"):
+        if step >= 2 and size < lax.axis_size("seq") and (step >= 4 or size == 1):
             total, _ = lax.optimization_barrier((total, products[0]))
-            total, into = middle(total, into, size)
+            total, into = middle(total, flip(total, "seq", size), into, size)
             size *= 2
-        if step == len(waves) + 1:
+        if last_step:
             while size < lax.axis_size("seq"):
-                total, into = middle(total, into, size)
+                total, into = middle(total, flip(total, "seq", size), into, size)
                 size *= 2
             attended = late(products[0], into)
         if step == 3:
@@ -438,7 +458,7 @@
             keep, new, far, made, carried = lax.optimization_barrier(
                 (
                     [fetched[key] for key in names],
-                    [fetched[key] for key in wave],
+                    [fetched[key] for key in wave] if step > 0 else [],
                     [across[key] for key in landed],
                     made,
                     carried,
@@ -452,7 +472,8 @@
             elif step > 1:
                 total, into = carried
             fetched.update(zip(names, keep))
-            fetched.update(zip(wave, new))
+            if step > 0:
+                fetched.update(zip(wave, new))
             across.update(zip(landed, far))
     last = [arrived[key] for key in spread]
     last, _ = lax.optimization_barrier((last, attended))
@@ -472,8 +493,8 @@
     return mixes[0], flip(mixes[1], "seq", 1)
 
 
-def call(kernel, name, info, args, in_specs, outs, out_specs, scratch=(), micros=3.0):
-    nblocks = max(a.shape[0] for a in args if a.ndim == 2) // BLK
+def call(kernel, name, info, args, in_specs, outs, out_specs, scratch=(), micros=3.0, size=BLK):
+    nblocks = max(a.shape[0] for a in args if a.ndim == 2) // size
     return pl.pallas_call(
         kernel,
         grid_spec=pltpu.PrefetchScalarGridSpec(
@@ -552,12 +573,13 @@
                 [all_states, one_state],
                 [states, state],
                 scratch,
+                3.0,
             )
         kept["before"] = before
         return key_total
 
-    def middle(total, into, size):
-        return combine(info, count, length, size, total, flip(total, "seq", size), into)
+    def middle(total, other, into, size):
+        return combine(info, count, length, size, total, other, into)
 
     def late(product, into):
         kept["into"] = into
@@ -571,6 +593,8 @@
                 [block, block, block, states, state],
                 [tokens32, row, low_states],
                 [block, line, states],
+                (),
+                8.0,
             )
         return kept["square"]
 
@@ -611,17 +635,22 @@
         flip(query_total if step == 1 else query_low, "seq", step)
         for step in range(1, lax.axis_size("seq"))
     ]
+    big = pl.BlockSpec((LARGE, width), lambda b, s: (b, 0))
+    big_states = pl.BlockSpec(
+        (LARGE // CHUNK, heads, HEAD_DIM, HEAD_DIM), lambda b, s: (b, 0, 0, 0)
+    )
     with jax.named_scope("grad_queries"):
         grad_queries = call(
             functools.partial(grad_query_kernel, count, heads),
             "grad_queries",
             info,
             [grad, key_rows, value_rows, low],
-            [block, block, block, states],
+            [big, big, big, big_states],
             [tokens16],
-            [block],
+            [big],
             (),
             8.0,
+            LARGE,
         )[0]
     with jax.named_scope("grad_keys_values"):
         grad_keys, grad_values = call(
@@ -629,11 +658,12 @@
             "grad_keys_values",
             info,
             [grad, queries, key_rows, value_rows, after, *landed],
-            [block, block, block, block, states] + [state] * len(landed),
+            [big, big, big, big, big_states] + [state] * len(landed),
             [tokens16, tokens16],
-            [block, block],
+            [big, big],
             scratch,
             8.0,
+            LARGE,
         )
     return (grad_queries, grad_keys, grad_values, grad_gate)
 

time: 182 us -> 174 us (0.956)
  waiting for transfers between devices: 87.8 us -> 80.5 us
  Pallas kernels: 47.9 us -> 45.6 us
  starting transfers between devices: 34 us -> 36.2 us
    ppermute x31, waiting for transfers between devices: 87.8 us -> 80.5 us  [flip(): lax.ppermute(a, axis, [(i, i ^ bit) for i in range(lax.axis_size(axis))])]
    pallas_call x6, Pallas kernels: 29.7 us -> 27.2 us  [call(): pl.pallas_call(kernel, grid_spec=pltpu.PrefetchScalarGridSpec(num_scalar_...]
    ppermute x31, starting transfers between devices: 34 us -> 36.2 us  [flip(): lax.ppermute(a, axis, [(i, i ^ bit) for i in range(lax.axis_size(axis))])]
    unnamed x36 -> x32, local copies, waits for them, and re-layouts: 7 us -> 6.23 us
  transfers between devices with their start and end apart: 31 -> 31, of which waited for: 16 -> 15; matrix products, arithmetic and copies ran while one was open for 1% -> 1% of each run, Pallas kernels for 16% -> 17%
where the time goes in v4:
time: 174 us
  waiting for transfers between devices  80.5 us (46%)
  Pallas kernels  45.6 us (26%)
  starting transfers between devices  36.2 us (21%)
  local copies, waits for them, and re-layouts  10.5 us (6%)
    ppermute x31, waiting for transfers between devices, flip(): lax.ppermute(a, axis, [(i, i ^ bit) for i in range(lax.axis_size(axis))])  80.5 us
    ppermute x31, starting transfers between devices, flip(): lax.ppermute(a, axis, [(i, i ^ bit) for i in range(lax.axis_size(axis))])  36.2 us
    pallas_call x6, Pallas kernels, call(): pl.pallas_call(kernel, grid_spec=pltpu.PrefetchScalarGridSpec(num_scalar_...  27.2 us
    pallas_call x4, Pallas kernels, project(): pl.pallas_call(functools.partial(project_kernel, len(shards[0])), grid_sp...  12.9 us
    unnamed x32, local copies, waits for them, and re-layouts  6.23 us
    pallas_call x1, Pallas kernels, gather_rows(): pl.pallas_call(gather_kernel, grid_spec=pltpu.PrefetchScalarGridSpec(num_...  3.58 us
  transfers between devices with their start and end apart: 31, of which 15 were waited for; matrix products, arithmetic and copies ran while one was open for 1% of the time, Pallas kernels for 17%

profile of v4, /device:TPU:0, one launch (start us, length us, event | category | flops | bytes accessed | tf_op | source)
XLA Modules:
  0.0 173.9 jit_solution(6775164551434715113)
XLA Ops:
  3.4 2.5 %collective-permute-start.7 = (bf16[256,4096]{1,0:T(8,128)(2,1)S(1)}, bf16[256,4096]{1,0:T(8,128)(2,1)}, u32[]{:S(2)}, u32[]{:S(2)}) collective-permute-start(bf16[256,4096]{1,0:T(8,128)(2,1)S(1)} %copy-done), channel_id=1, source_target_pairs={{0,1},{1,0},{2,3},{3,2},{4,5},{5,4},{6,7},{7,6},{8,9},{9,8},{10,11... | collective-permute-start | bytes 6291464 | tf_op jit(solution)/shard_map/ppermute | solution.py:519
  5.9 2.6 %collective-permute-start.1 = (bf16[128,2048]{1,0:T(8,128)(2,1)S(1)}, bf16[128,2048]{1,0:T(8,128)(2,1)}, u32[]{:S(2)}, u32[]{:S(2)}) collective-permute-start(bf16[128,2048]{1,0:T(8,128)(2,1)S(1)} %get-tuple-element.117), channel_id=1, source_target_pairs={{0,4},{1,5},{2,6},{3,7},{4,0},{5,1},{6,2},{7,3},{8,12},{9,13},{10,... | collective-permute-start | bytes 1572872 | tf_op jit(solution)/shard_map/ppermute | solution.py:519
  10.1 22.2 %collective-permute-done.1.refs_0_ = bf16[128,2048]{1,0:T(8,128)(2,1)} collective-permute-done((bf16[128,2048]{1,0:T(8,128)(2,1)S(1)}, bf16[128,2048]{1,0:T(8,128)(2,1)}, u32[]{:S(2)}, u32[]{:S(2)}) %collective-permute-start.1) | collective-permute-done | bytes 524320 | tf_op jit(solution)/shard_map/ppermute | solution.py:519
  34.8 3.5 %collective-permute-start.3 = (bf16[128,2048]{1,0:T(8,128)(2,1)}, bf16[128,2048]{1,0:T(8,128)(2,1)S(1)}, u32[]{:S(2)}, u32[]{:S(2)}) collective-permute-start(bf16[128,2048]{1,0:T(8,128)(2,1)} %get-tuple-element.74), channel_id=1, source_target_pairs={{0,4},{1,5},{2,6},{3,7},{4,0},{5,1},{6,2},{7,3},{8,12},{9,13},{10,... | collective-permute-start | bytes 1572872 | tf_op jit(solution)/shard_map/ppermute | solution.py:519
  41.4 2.3 %key_states.1 = (f32[8,4,128,128]{3,2,1,0:T(8,128)S(1)}, f32[4,128,128]{2,1,0:T(8,128)S(1)}) custom-call(s32[5]{0:T(128)S(1)} %pad_add_fusion.info, bf16[2048,512]{1,0:T(8,128)(2,1)S(1)} %copy-done.4, bf16[2048,512]{1,0:T(8,128)(2,1)S(1)} %copy-done.6), custom_call_target="tpu_custom_call" | custom-call | flops 3449999872 | tf_op jit(solution)/shard_map/key_states/key_states/pallas_call | solution.py:498
  46.5 8.7 %collective-permute-done.4.refs_2_ = bf16[128,2048]{1,0:T(8,128)(2,1)S(1)} collective-permute-done((bf16[128,2048]{1,0:T(8,128)(2,1)}, bf16[128,2048]{1,0:T(8,128)(2,1)S(1)}, u32[]{:S(2)}, u32[]{:S(2)}) %collective-permute-start.4) | collective-permute-done | bytes 524320 | tf_op jit(solution)/shard_map/ppermute | solution.py:519
  58.6 2.4 %collective-permute-done.3.refs_0_ = bf16[128,2048]{1,0:T(8,128)(2,1)S(1)} collective-permute-done((bf16[128,2048]{1,0:T(8,128)(2,1)}, bf16[128,2048]{1,0:T(8,128)(2,1)S(1)}, u32[]{:S(2)}, u32[]{:S(2)}) %collective-permute-start.3) | collective-permute-done | bytes 524320 | tf_op jit(solution)/shard_map/ppermute | solution.py:519
  65.5 3.6 %gather_rows.1.rows_ref = bf16[1024,4096]{1,0:T(8,128)(2,1)S(1)} custom-call(s32[3]{0:T(128)S(1)} %pad_add_fusion.1.info, bf16[256,4096]{1,0:T(8,128)(2,1)S(1)} %copy-done, bf16[256,4096]{1,0:T(8,128)(2,1)} %collective-permute-done.7.refs_1_, bf16[256,4096]{1,0:T(8,128)(2,1)} %collective-permute-done.refs_2_, bf16[256,4096]{1,0:T(8,128)(2,1)} %collective-permute-done.8.refs_3_), custom_call_target="tpu_custom_call" | custom-call | flops 3449999872 | tf_op jit(solution)/shard_map/gather_rows/pallas_call | solution.py:302
  69.1 4.2 %project.4 = (bf16[1024,128]{1,0:T(8,128)(2,1)S(1)}, bf16[1024,128]{1,0:T(8,128)(2,1)S(1)}) custom-call(s32[3]{0:T(128)S(1)} %pad_add_fusion.1.info, bf16[1024,4096]{1,0:T(8,128)(2,1)S(1)} %gather_rows.1.rows_ref, bf16[128,2048]{1,0:T(8,128)(2,1)} %collective-permute-done.1.refs_0_, bf16[128,2048]{1,0:T(8,128)(2,1)S(1)} %copy-done.9, ...), custom_call_target="tpu_custom_call" | custom-call | flops 3449999872 | tf_op jit(solution)/shard_map/project/pallas_call | solution.py:340
  73.5 2.9 %project.6 = bf16[1024,256]{1,0:T(8,128)(2,1)S(1)} custom-call(s32[3]{0:T(128)S(1)} %pad_add_fusion.1.info, bf16[1024,4096]{1,0:T(8,128)(2,1)S(1)} %gather_rows.1.rows_ref, bf16[256,4096]{1,0:T(8,128)(2,1)S(1)} %copy-done.1), custom_call_target="tpu_custom_call" | custom-call | flops 3449999872 | tf_op jit(solution)/shard_map/project/pallas_call | solution.py:340
  80.2 12.5 %collective-permute-done.12.refs_2_ = bf16[128,2048]{1,0:T(8,128)(2,1)S(1)} collective-permute-done((bf16[128,2048]{1,0:T(8,128)(2,1)}, bf16[128,2048]{1,0:T(8,128)(2,1)S(1)}, u32[]{:S(2)}, u32[]{:S(2)}) %collective-permute-start.12) | collective-permute-done | bytes 524320 | tf_op jit(solution)/shard_map/ppermute | solution.py:519
  94.7 2.9 %project.5 = (bf16[1024,128]{1,0:T(8,128)(2,1)S(1)}, bf16[1024,128]{1,0:T(8,128)(2,1)S(1)}) custom-call(s32[3]{0:T(128)S(1)} %pad_add_fusion.1.info, bf16[1024,4096]{1,0:T(8,128)(2,1)S(1)} %gather_rows.1.rows_ref, bf16[128,2048]{1,0:T(8,128)(2,1)S(1)} %collective-permute-done.3.refs_0_, bf16[128,2048]{1,0:T(8,128)(2,1)S(1)} %collective-permute-done.13.refs_1_, ...), custom_call_target="tpu_custom_call" | custom-call | flops 3449999872 | tf_op jit(solution)/shard_map/project/pallas_call | solution.py:340
  100.5 16.1 %collective-permute-done.16 = bf16[1024,128]{1,0:T(8,128)(2,1)S(1)} collective-permute-done((bf16[1024,128]{1,0:T(8,128)(2,1)S(1)}, bf16[1024,128]{1,0:T(8,128)(2,1)S(1)}, u32[]{:S(2)}, u32[]{:S(2)}) %collective-permute-start.16) | collective-permute-done | bytes 262176 | tf_op jit(solution)/shard_map/ppermute | solution.py:519
  117.1 2.9 %project.7 = (bf16[1024,128]{1,0:T(8,128)(2,1)S(1)}, bf16[1024,128]{1,0:T(8,128)(2,1)S(1)}) custom-call(s32[3]{0:T(128)S(1)} %pad_add_fusion.1.info, bf16[1024,4096]{1,0:T(8,128)(2,1)S(1)} %gather_rows.1.rows_ref, bf16[128,2048]{1,0:T(8,128)(2,1)S(1)} %collective-permute-done.11.refs_0_, bf16[128,2048]{1,0:T(8,128)(2,1)S(1)} %collective-permute-done.18.refs_1_, ...), custom_call_target="tpu_custom_call" | custom-call | flops 3449999872 | tf_op jit(solution)/shard_map/project/pallas_call | solution.py:340
  121.7 2.4 %collective-permute-start.20 = (bf16[1024,128]{1,0:T(8,128)(2,1)S(1)}, bf16[1024,128]{1,0:T(8,128)(2,1)S(1)}, u32[]{:S(2)}, u32[]{:S(2)}) collective-permute-start(bf16[1024,128]{1,0:T(8,128)(2,1)S(1)} %get-tuple-element.96), channel_id=1, source_target_pairs={{0,6},{1,7},{2,4},{3,5},{4,2},{5,3},{6,0},{7,1},{8,14},{9,15},{10,... | collective-permute-start | bytes 786440 | tf_op jit(solution)/shard_map/ppermute | solution.py:519
  126.4 4.5 %attention.1 = (f32[2048,512]{1,0:T(8,128)S(1)}, f32[1,2048]{1,0:T(1,128)S(1)}, bf16[8,4,128,128]{3,2,1,0:T(8,128)(2,1)S(1)}) custom-call(s32[5]{0:T(128)S(1)} %pad_add_fusion.info, bf16[2048,512]{1,0:T(8,128)(2,1)S(1)} %copy-done.3, bf16[2048,512]{1,0:T(8,128)(2,1)S(1)} %copy-done.5, bf16[2048,512]{1,0:T(8,128)(2,1)S(1)} %copy-done.7, ...), custom_call_target="tpu_custom_call" | custom-call | flops 9200000000 | tf_op jit(solution)/shard_map/attention/attention/pallas_call | solution.py:498
  132.8 3.5 %collective-permute-done.21 = bf16[1024,128]{1,0:T(8,128)(2,1)S(1)} collective-permute-done((bf16[1024,128]{1,0:T(8,128)(2,1)S(1)}, bf16[1024,128]{1,0:T(8,128)(2,1)S(1)}, u32[]{:S(2)}, u32[]{:S(2)}) %collective-permute-start.21) | collective-permute-done | bytes 262176 | tf_op jit(solution)/shard_map/ppermute | solution.py:519
  136.6 2.6 %collective-permute-done.23.far_ref = bf16[2048,256]{1,0:T(8,128)(2,1)S(1)} collective-permute-done((bf16[2048,256]{1,0:T(8,128)(2,1)S(1)}, bf16[2048,256]{1,0:T(8,128)(2,1)S(1)}, u32[]{:S(2)}, u32[]{:S(2)}) %collective-permute-start.23) | collective-permute-done | bytes 1048608 | tf_op jit(solution)/shard_map/ppermute | solution.py:519
  141.5 2.2 %collective-permute-start.25 = (f32[2,2048]{1,0:T(2,128)S(1)}, f32[2,2048]{1,0:T(2,128)S(1)}, u32[]{:S(2)}, u32[]{:S(2)}) collective-permute-start(f32[2,2048]{1,0:T(2,128)S(1)} %cross.1.refs_0_), channel_id=1, source_target_pairs={{0,4},{1,5},{2,6},{3,7},{4,0},{5,1},{6,2},{7,3},{8,12},{9,13},{10,... | collective-permute-start | bytes 49160 | tf_op jit(solution)/shard_map/ppermute | solution.py:519
  146.3 3.0 %collective-permute-done.26.refs_3_ = f32[2,2048]{1,0:T(2,128)S(1)} collective-permute-done((f32[2,2048]{1,0:T(2,128)S(1)}, f32[2,2048]{1,0:T(2,128)S(1)}, u32[]{:S(2)}, u32[]{:S(2)}) %collective-permute-start.26) | collective-permute-done | bytes 16416 | tf_op jit(solution)/shard_map/ppermute | solution.py:519
  149.9 3.2 %collective-permute-done.27.refs_1_ = f32[2,2048]{1,0:T(2,128)S(1)} collective-permute-done((f32[2,2048]{1,0:T(2,128)S(1)}, f32[2,2048]{1,0:T(2,128)S(1)}, u32[]{:S(2)}, u32[]{:S(2)}) %collective-permute-start.27) | collective-permute-done | bytes 16416 | tf_op jit(solution)/shard_map/ppermute | solution.py:519
  153.1 5.8 %grad_attn.1 = (bf16[2048,512]{1,0:T(8,128)(2,1)S(1)}, bf16[2048,512]{1,0:T(8,128)(2,1)}, f32[8,4,128,128]{3,2,1,0:T(8,128)S(1)}, f32[4,128,128]{2,1,0:T(8,128)S(1)}, bf16[4,128,128]{2,1,0:T(8,128)(2,1)S(1)}) custom-call(s32[5]{0:T(128)S(1)} %pad_add_fusion.info, bf16[2048,256]{1,0:T(8,128)(2,1)S(1)} %get-tuple-element.121.near_ref, ...), custom_call_target="tpu_custom_call" | custom-call | flops 4600000000 | tf_op jit(solution)/shard_map/grad_attn/grad_attn/pallas_call | solution.py:498
  161.0 4.7 %grad_queries.1 = bf16[2048,512]{1,0:T(8,128)(2,1)} custom-call(s32[5]{0:T(128)S(1)} %pad_add_fusion.info, bf16[2048,512]{1,0:T(8,128)(2,1)S(1)} %get-tuple-element.108.grad_ref, bf16[2048,512]{1,0:T(8,128)(2,1)S(1)} %copy-done.5, bf16[2048,512]{1,0:T(8,128)(2,1)S(1)} %copy-done.7, bf16[8,4,128,128]{3,2,1,0:T(8,128)(2,1)S(1)} %get-tuple-element.109.low_ref), custom_call_target="tpu_custom_call" | custom-call | flops 9200000000 | tf_op jit(solution)/shard_map/grad_queries/grad_queries/pallas_call | solution.py:498
  165.7 8.2 %grad_keys_values.1 = (bf16[2048,512]{1,0:T(8,128)(2,1)}, bf16[2048,512]{1,0:T(8,128)(2,1)}) custom-call(s32[5]{0:T(128)S(1)} %pad_add_fusion.info, bf16[2048,512]{1,0:T(8,128)(2,1)S(1)} %get-tuple-element.108.grad_ref, bf16[2048,512]{1,0:T(8,128)(2,1)S(1)} %copy-done.3, bf16[2048,512]{1,0:T(8,128)(2,1)S(1)} %copy-done.5, bf16[2048,512]{1,0:T(8,128)(2,1)S(1)} %copy-done.7, ...), custom_call_target="tpu_custom_call" | custom-call | flops 9200000000 | tf_op jit(solution)/shard_map/grad_keys_values/grad_keys_values/pallas_call | solution.py:498
  (100 shorter events, 43.5 us)
Async XLA Ops:
  2.9 31.8 %collective-permute-start = (bf16[256,4096]{1,0:T(8,128)(2,1)S(1)}, bf16[256,4096]{1,0:T(8,128)(2,1)}, u32[]{:S(2)}, u32[]{:S(2)}) collective-permute-start(bf16[256,4096]{1,0:T(8,128)(2,1)S(1)} %copy-done), channel_id=1, source_target_pairs={{0,8},{8,0},{16,24},{24,16},{1,9},{9,1},{17,25},{25,17},{2,10},{10... | collective-permute-start | bytes 6291464 | tf_op jit(solution)/shard_map/ppermute | solution.py:519
  3.4 55.2 %collective-permute-start.7 = (bf16[256,4096]{1,0:T(8,128)(2,1)S(1)}, bf16[256,4096]{1,0:T(8,128)(2,1)}, u32[]{:S(2)}, u32[]{:S(2)}) collective-permute-start(bf16[256,4096]{1,0:T(8,128)(2,1)S(1)} %copy-done), channel_id=1, source_target_pairs={{0,1},{1,0},{2,3},{3,2},{4,5},{5,4},{6,7},{7,6},{8,9},{9,8},{10,11... | collective-permute-start | bytes 6291464 | tf_op jit(solution)/shard_map/ppermute | solution.py:519
  5.9 26.4 %collective-permute-start.1 = (bf16[128,2048]{1,0:T(8,128)(2,1)S(1)}, bf16[128,2048]{1,0:T(8,128)(2,1)}, u32[]{:S(2)}, u32[]{:S(2)}) collective-permute-start(bf16[128,2048]{1,0:T(8,128)(2,1)S(1)} %get-tuple-element.117), channel_id=1, source_target_pairs={{0,4},{1,5},{2,6},{3,7},{4,0},{5,1},{6,2},{7,3},{8,12},{9,13},{10,... | collective-permute-start | bytes 1572872 | tf_op jit(solution)/shard_map/ppermute | solution.py:519
  8.5 25.8 %collective-permute-start.2 = (bf16[128,2048]{1,0:T(8,128)(2,1)S(1)}, bf16[128,2048]{1,0:T(8,128)(2,1)}, u32[]{:S(2)}, u32[]{:S(2)}) collective-permute-start(bf16[128,2048]{1,0:T(8,128)(2,1)S(1)} %get-tuple-element.117), channel_id=1, source_target_pairs={{0,2},{1,3},{2,0},{3,1},{4,6},{5,7},{6,4},{7,5},{8,10},{9,11},{10,... | collective-permute-start | bytes 1572872 | tf_op jit(solution)/shard_map/ppermute | solution.py:519
  32.3 22.9 %collective-permute-start.4 = (bf16[128,2048]{1,0:T(8,128)(2,1)}, bf16[128,2048]{1,0:T(8,128)(2,1)S(1)}, u32[]{:S(2)}, u32[]{:S(2)}) collective-permute-start(bf16[128,2048]{1,0:T(8,128)(2,1)} %collective-permute-done.1.refs_0_), channel_id=1, source_target_pairs={{0,2},{1,3},{2,0},{3,1},{4,6},{5,7},{6,4},{7,5},{8,10},{9,11},{10,... | collective-permute-start | bytes 1572872 | tf_op jit(solution)/shard_map/ppermute | solution.py:519
  32.7 22.5 %collective-permute-start.5 = (bf16[128,2048]{1,0:T(8,128)(2,1)}, bf16[128,2048]{1,0:T(8,128)(2,1)S(1)}, u32[]{:S(2)}, u32[]{:S(2)}) collective-permute-start(bf16[128,2048]{1,0:T(8,128)(2,1)} %collective-permute-done.1.refs_0_), channel_id=1, source_target_pairs={{0,16},{8,24},{16,0},{24,8},{1,17},{9,25},{17,1},{25,9},{2,18},{10... | collective-permute-start | bytes 1572872 | tf_op jit(solution)/shard_map/ppermute | solution.py:519
  34.2 23.5 %collective-permute-start.6 = (bf16[128,2048]{1,0:T(8,128)(2,1)}, bf16[128,2048]{1,0:T(8,128)(2,1)S(1)}, u32[]{:S(2)}, u32[]{:S(2)}) collective-permute-start(bf16[128,2048]{1,0:T(8,128)(2,1)} %collective-permute-done.2.refs_2_), channel_id=1, source_target_pairs={{0,16},{8,24},{16,0},{24,8},{1,17},{9,25},{17,1},{25,9},{2,18},{10... | collective-permute-start | bytes 1572872 | tf_op jit(solution)/shard_map/ppermute | solution.py:519
  34.8 26.3 %collective-permute-start.3 = (bf16[128,2048]{1,0:T(8,128)(2,1)}, bf16[128,2048]{1,0:T(8,128)(2,1)S(1)}, u32[]{:S(2)}, u32[]{:S(2)}) collective-permute-start(bf16[128,2048]{1,0:T(8,128)(2,1)} %get-tuple-element.74), channel_id=1, source_target_pairs={{0,4},{1,5},{2,6},{3,7},{4,0},{5,1},{6,2},{7,3},{8,12},{9,13},{10,... | collective-permute-start | bytes 1572872 | tf_op jit(solution)/shard_map/ppermute | solution.py:519
  61.1 17.2 %collective-permute-start.11 = (bf16[128,2048]{1,0:T(8,128)(2,1)S(1)}, bf16[128,2048]{1,0:T(8,128)(2,1)S(1)}, u32[]{:S(2)}, u32[]{:S(2)}) collective-permute-start(bf16[128,2048]{1,0:T(8,128)(2,1)S(1)} %collective-permute-done.3.refs_0_), channel_id=1, source_target_pairs={{0,2},{1,3},{2,0},{3,1},{4,6},{5,7},{6,4},{7,5},{8,10},{9,11},{10,... | collective-permute-start | bytes 1572872 | tf_op jit(solution)/shard_map/ppermute | solution.py:519
  61.1 31.6 %collective-permute-start.13 = (bf16[128,2048]{1,0:T(8,128)(2,1)S(1)}, bf16[128,2048]{1,0:T(8,128)(2,1)S(1)}, u32[]{:S(2)}, u32[]{:S(2)}) collective-permute-start(bf16[128,2048]{1,0:T(8,128)(2,1)S(1)} %collective-permute-done.3.refs_0_), channel_id=1, source_target_pairs={{0,16},{8,24},{16,0},{24,8},{1,17},{9,25},{17,1},{25,9},{2,18},{10... | collective-permute-start | bytes 1572872 | tf_op jit(solution)/shard_map/ppermute | solution.py:519
  62.7 30.0 %collective-permute-start.12 = (bf16[128,2048]{1,0:T(8,128)(2,1)}, bf16[128,2048]{1,0:T(8,128)(2,1)S(1)}, u32[]{:S(2)}, u32[]{:S(2)}) collective-permute-start(bf16[128,2048]{1,0:T(8,128)(2,1)} %get-tuple-element.74), channel_id=1, source_target_pairs={{0,2},{1,3},{2,0},{3,1},{4,6},{5,7},{6,4},{7,5},{8,10},{9,11},{10,... | collective-permute-start | bytes 1572872 | tf_op jit(solution)/shard_map/ppermute | solution.py:519
  64.7 28.0 %collective-permute-start.14 = (bf16[128,2048]{1,0:T(8,128)(2,1)S(1)}, bf16[128,2048]{1,0:T(8,128)(2,1)S(1)}, u32[]{:S(2)}, u32[]{:S(2)}) collective-permute-start(bf16[128,2048]{1,0:T(8,128)(2,1)S(1)} %collective-permute-done.4.refs_2_), channel_id=1, source_target_pairs={{0,16},{8,24},{16,0},{24,8},{1,17},{9,25},{17,1},{25,9},{2,18},{10... | collective-permute-start | bytes 1572872 | tf_op jit(solution)/shard_map/ppermute | solution.py:519
  76.5 21.8 %collective-permute-start.9 = (bf16[1024,128]{1,0:T(8,128)(2,1)S(1)}, bf16[1024,128]{1,0:T(8,128)(2,1)S(1)}, u32[]{:S(2)}, u32[]{:S(2)}) collective-permute-start(bf16[1024,128]{1,0:T(8,128)(2,1)S(1)} %get-tuple-element.72), channel_id=1, source_target_pairs={{0,4},{1,5},{2,6},{3,7},{4,0},{5,1},{6,2},{7,3},{8,12},{9,13},{10,... | collective-permute-start | bytes 786440 | tf_op jit(solution)/shard_map/ppermute | solution.py:519
  78.3 22.1 %collective-permute-start.10 = (bf16[1024,128]{1,0:T(8,128)(2,1)S(1)}, bf16[1024,128]{1,0:T(8,128)(2,1)S(1)}, u32[]{:S(2)}, u32[]{:S(2)}) collective-permute-start(bf16[1024,128]{1,0:T(8,128)(2,1)S(1)} %get-tuple-element.73), channel_id=1, source_target_pairs={{0,2},{1,3},{2,0},{3,1},{4,6},{5,7},{6,4},{7,5},{8,10},{9,11},{10,... | collective-permute-start | bytes 786440 | tf_op jit(solution)/shard_map/ppermute | solution.py:519
  92.7 24.0 %collective-permute-start.18 = (bf16[128,2048]{1,0:T(8,128)(2,1)S(1)}, bf16[128,2048]{1,0:T(8,128)(2,1)S(1)}, u32[]{:S(2)}, u32[]{:S(2)}) collective-permute-start(bf16[128,2048]{1,0:T(8,128)(2,1)S(1)} %collective-permute-done.11.refs_0_), channel_id=1, source_target_pairs={{0,16},{8,24},{16,0},{24,8},{1,17},{9,25},{17,1},{25,9},{2,18},{10... | collective-permute-start | bytes 1572872 | tf_op jit(solution)/shard_map/ppermute | solution.py:519
  94.2 22.9 %collective-permute-start.19 = (bf16[128,2048]{1,0:T(8,128)(2,1)S(1)}, bf16[128,2048]{1,0:T(8,128)(2,1)S(1)}, u32[]{:S(2)}, u32[]{:S(2)}) collective-permute-start(bf16[128,2048]{1,0:T(8,128)(2,1)S(1)} %collective-permute-done.12.refs_2_), channel_id=1, source_target_pairs={{0,16},{8,24},{16,0},{24,8},{1,17},{9,25},{17,1},{25,9},{2,18},{10... | collective-permute-start | bytes 1572872 | tf_op jit(solution)/shard_map/ppermute | solution.py:519
  97.6 19.0 %collective-permute-start.16 = (bf16[1024,128]{1,0:T(8,128)(2,1)S(1)}, bf16[1024,128]{1,0:T(8,128)(2,1)S(1)}, u32[]{:S(2)}, u32[]{:S(2)}) collective-permute-start(bf16[1024,128]{1,0:T(8,128)(2,1)S(1)} %get-tuple-element.85), channel_id=1, source_target_pairs={{0,4},{1,5},{2,6},{3,7},{4,0},{5,1},{6,2},{7,3},{8,12},{9,13},{10,... | collective-permute-start | bytes 786440 | tf_op jit(solution)/shard_map/ppermute | solution.py:519
  98.3 23.3 %collective-permute-start.17 = (bf16[1024,128]{1,0:T(8,128)(2,1)S(1)}, bf16[1024,128]{1,0:T(8,128)(2,1)S(1)}, u32[]{:S(2)}, u32[]{:S(2)}) collective-permute-start(bf16[1024,128]{1,0:T(8,128)(2,1)S(1)} %get-tuple-element.86), channel_id=1, source_target_pairs={{0,6},{1,7},{2,4},{3,5},{4,2},{5,3},{6,0},{7,1},{8,14},{9,15},{10,... | collective-permute-start | bytes 786440 | tf_op jit(solution)/shard_map/ppermute | solution.py:519
  121.7 11.1 %collective-permute-start.20 = (bf16[1024,128]{1,0:T(8,128)(2,1)S(1)}, bf16[1024,128]{1,0:T(8,128)(2,1)S(1)}, u32[]{:S(2)}, u32[]{:S(2)}) collective-permute-start(bf16[1024,128]{1,0:T(8,128)(2,1)S(1)} %get-tuple-element.96), channel_id=1, source_target_pairs={{0,6},{1,7},{2,4},{3,5},{4,2},{5,3},{6,0},{7,1},{8,14},{9,15},{10,... | collective-permute-start | bytes 786440 | tf_op jit(solution)/shard_map/ppermute | solution.py:519
  124.2 12.2 %collective-permute-start.21 = (bf16[1024,128]{1,0:T(8,128)(2,1)S(1)}, bf16[1024,128]{1,0:T(8,128)(2,1)S(1)}, u32[]{:S(2)}, u32[]{:S(2)}) collective-permute-start(bf16[1024,128]{1,0:T(8,128)(2,1)S(1)} %get-tuple-element.97), channel_id=1, source_target_pairs={{0,2},{1,3},{2,0},{3,1},{4,6},{5,7},{6,4},{7,5},{8,10},{9,11},{10,... | collective-permute-start | bytes 786440 | tf_op jit(solution)/shard_map/ppermute | solution.py:519
  143.8 5.5 %collective-permute-start.26 = (f32[2,2048]{1,0:T(2,128)S(1)}, f32[2,2048]{1,0:T(2,128)S(1)}, u32[]{:S(2)}, u32[]{:S(2)}) collective-permute-start(f32[2,2048]{1,0:T(2,128)S(1)} %cross.1.refs_0_), channel_id=1, source_target_pairs={{0,6},{1,7},{2,4},{3,5},{4,2},{5,3},{6,0},{7,1},{8,14},{9,15},{10,... | collective-permute-start | bytes 49160 | tf_op jit(solution)/shard_map/ppermute | solution.py:519
  158.8 6.8 %collective-permute-start.29 = (bf16[4,128,128]{2,1,0:T(8,128)(2,1)S(1)}, bf16[4,128,128]{2,1,0:T(8,128)(2,1)S(1)}, u32[]{:S(2)}, u32[]{:S(2)}) collective-permute-start(bf16[4,128,128]{2,1,0:T(8,128)(2,1)S(1)} %get-tuple-element.112), channel_id=1, source_target_pairs={{0,16},{8,24},{16,0},{24,8},{1,17},{9,25},{17,1},{25,9},{2,18},{10... | collective-permute-start | bytes 393224 | tf_op jit(solution)/shard_map/ppermute | solution.py:519
  159.3 6.3 %collective-permute-start.30 = (bf16[4,128,128]{2,1,0:T(8,128)(2,1)S(1)}, bf16[4,128,128]{2,1,0:T(8,128)(2,1)S(1)}, u32[]{:S(2)}, u32[]{:S(2)}) collective-permute-start(bf16[4,128,128]{2,1,0:T(8,128)(2,1)S(1)} %get-tuple-element.112), channel_id=1, source_target_pairs={{0,24},{8,16},{16,8},{24,0},{1,25},{9,17},{17,9},{25,1},{2,26},{10... | collective-permute-start | bytes 393224 | tf_op jit(solution)/shard_map/ppermute | solution.py:519
  159.4 6.3 %collective-permute-start.28 = (f32[4,128,128]{2,1,0:T(8,128)S(1)}, f32[4,128,128]{2,1,0:T(8,128)S(1)}, u32[]{:S(2)}, u32[]{:S(2)}) collective-permute-start(f32[4,128,128]{2,1,0:T(8,128)S(1)} %get-tuple-element.111), channel_id=1, source_target_pairs={{0,8},{8,0},{16,24},{24,16},{1,9},{9,1},{17,25},{25,17},{2,10},{10... | collective-permute-start | bytes 786440 | tf_op jit(solution)/shard_map/ppermute | solution.py:519
  (23 other events, 105.9 us)

commit v5 on v4

--- a/solution.py
+++ b/solution.py
@@ -398,6 +398,7 @@
     order += [(1, hop) for hop in hops[:1]]
     order += [(0, hop) for hop in hops if hop & (hop - 1) != 0]
     order += [(1, hop) for hop in hops[1:]]
+    order[0], order[1] = order[1], order[0]
     order[-2], order[-1] = order[-1], order[-2]
     waves = [order[i : i + 2] for i in range(0, len(order), 2)]
 
@@ -441,7 +442,6 @@
             for key, product in zip(spread, products):
                 arrived[key] = flip(product, "head", 2 * key[1])
         if step >= 2 and size < lax.axis_size("seq") and (step >= 4 or size == 1):
-            total, _ = lax.optimization_barrier((total, products[0]))
             total, into = middle(total, flip(total, "seq", size), into, size)
             size *= 2
         if last_step:
@@ -573,7 +573,7 @@
                 [all_states, one_state],
                 [states, state],
                 scratch,
-                3.0,
+                12.0,
             )
         kept["before"] = before
         return key_total

time: 174 us -> 171 us (0.983)
  waiting for transfers between devices: 80.5 us -> 73.8 us
  starting transfers between devices: 36.2 us -> 39 us
    ppermute x31, waiting for transfers between devices: 80.5 us -> 73.8 us  [flip(): lax.ppermute(a, axis, [(i, i ^ bit) for i in range(lax.axis_size(axis))])]
    ppermute x31, starting transfers between devices: 36.2 us -> 39 us  [flip(): lax.ppermute(a, axis, [(i, i ^ bit) for i in range(lax.axis_size(axis))])]
  transfers between devices with their start and end apart: 31 -> 31, of which waited for: 15 -> 15; matrix products, arithmetic and copies ran while one was open for 1% -> 1% of each run, Pallas kernels for 17% -> 18%
where the time goes in v5:
time: 171 us
  waiting for transfers between devices  73.8 us (43%)
  Pallas kernels  46.3 us (27%)
  starting transfers between devices  39 us (23%)
  local copies, waits for them, and re-layouts  10.5 us (6%)
    ppermute x31, waiting for transfers between devices, flip(): lax.ppermute(a, axis, [(i, i ^ bit) for i in range(lax.axis_size(axis))])  73.8 us
    ppermute x31, starting transfers between devices, flip(): lax.ppermute(a, axis, [(i, i ^ bit) for i in range(lax.axis_size(axis))])  39 us
    pallas_call x6, Pallas kernels, call(): pl.pallas_call(kernel, grid_spec=pltpu.PrefetchScalarGridSpec(num_scalar_...  26.9 us
    pallas_call x4, Pallas kernels, project(): pl.pallas_call(functools.partial(project_kernel, len(shards[0])), grid_sp...  12.9 us
    unnamed x32, local copies, waits for them, and re-layouts  6.19 us
    pallas_call x1, Pallas kernels, gather_rows(): pl.pallas_call(gather_kernel, grid_spec=pltpu.PrefetchScalarGridSpec(num_...  3.58 us
  transfers between devices with their start and end apart: 31, of which 15 were waited for; matrix products, arithmetic and copies ran while one was open for 1% of the time, Pallas kernels for 18%

profile of v5, /device:TPU:0, one launch (start us, length us, event | category | flops | bytes accessed | tf_op | source)
XLA Modules:
  0.0 170.7 jit_solution(1880120066657207456)
XLA Ops:
  3.4 2.6 %collective-permute-start.1 = (bf16[128,2048]{1,0:T(8,128)(2,1)S(1)}, bf16[128,2048]{1,0:T(8,128)(2,1)}, u32[]{:S(2)}, u32[]{:S(2)}) collective-permute-start(bf16[128,2048]{1,0:T(8,128)(2,1)S(1)} %get-tuple-element.113), channel_id=1, source_target_pairs={{0,2},{1,3},{2,0},{3,1},{4,6},{5,7},{6,4},{7,5},{8,10},{9,11},{10,... | collective-permute-start | bytes 1572872 | tf_op jit(solution)/shard_map/ppermute | solution.py:519
  5.9 2.6 %collective-permute-start.2 = (bf16[128,2048]{1,0:T(8,128)(2,1)S(1)}, bf16[128,2048]{1,0:T(8,128)(2,1)}, u32[]{:S(2)}, u32[]{:S(2)}) collective-permute-start(bf16[128,2048]{1,0:T(8,128)(2,1)S(1)} %get-tuple-element.113), channel_id=1, source_target_pairs={{0,4},{1,5},{2,6},{3,7},{4,0},{5,1},{6,2},{7,3},{8,12},{9,13},{10,... | collective-permute-start | bytes 1572872 | tf_op jit(solution)/shard_map/ppermute | solution.py:519
  10.1 19.7 %collective-permute-done.1.refs_0_ = bf16[128,2048]{1,0:T(8,128)(2,1)} collective-permute-done((bf16[128,2048]{1,0:T(8,128)(2,1)S(1)}, bf16[128,2048]{1,0:T(8,128)(2,1)}, u32[]{:S(2)}, u32[]{:S(2)}) %collective-permute-start.1) | collective-permute-done | bytes 524320 | tf_op jit(solution)/shard_map/ppermute | solution.py:519
  34.3 2.6 %collective-permute-start.3 = (bf16[128,2048]{1,0:T(8,128)(2,1)}, bf16[128,2048]{1,0:T(8,128)(2,1)S(1)}, u32[]{:S(2)}, u32[]{:S(2)}) collective-permute-start(bf16[128,2048]{1,0:T(8,128)(2,1)} %get-tuple-element.72), channel_id=1, source_target_pairs={{0,4},{1,5},{2,6},{3,7},{4,0},{5,1},{6,2},{7,3},{8,12},{9,13},{10,... | collective-permute-start | bytes 1572872 | tf_op jit(solution)/shard_map/ppermute | solution.py:519
  40.0 2.3 %key_states.1 = (f32[8,4,128,128]{3,2,1,0:T(8,128)S(1)}, f32[4,128,128]{2,1,0:T(8,128)S(1)}) custom-call(s32[5]{0:T(128)S(1)} %pad_add_fusion.info, bf16[2048,512]{1,0:T(8,128)(2,1)S(1)} %copy-done.4, bf16[2048,512]{1,0:T(8,128)(2,1)S(1)} %copy-done.6), custom_call_target="tpu_custom_call" | custom-call | flops 13799999488 | tf_op jit(solution)/shard_map/key_states/key_states/pallas_call | solution.py:498
  45.1 9.3 %collective-permute-done.4.refs_2_ = bf16[128,2048]{1,0:T(8,128)(2,1)S(1)} collective-permute-done((bf16[128,2048]{1,0:T(8,128)(2,1)}, bf16[128,2048]{1,0:T(8,128)(2,1)S(1)}, u32[]{:S(2)}, u32[]{:S(2)}) %collective-permute-start.4) | collective-permute-done | bytes 524320 | tf_op jit(solution)/shard_map/ppermute | solution.py:519
  56.1 3.5 %collective-permute-done.3.refs_0_ = bf16[128,2048]{1,0:T(8,128)(2,1)S(1)} collective-permute-done((bf16[128,2048]{1,0:T(8,128)(2,1)}, bf16[128,2048]{1,0:T(8,128)(2,1)S(1)}, u32[]{:S(2)}, u32[]{:S(2)}) %collective-permute-start.3) | collective-permute-done | bytes 524320 | tf_op jit(solution)/shard_map/ppermute | solution.py:519
  66.0 3.6 %gather_rows.1.rows_ref = bf16[1024,4096]{1,0:T(8,128)(2,1)S(1)} custom-call(s32[3]{0:T(128)S(1)} %pad_add_fusion.1.info, bf16[256,4096]{1,0:T(8,128)(2,1)S(1)} %copy-done, bf16[256,4096]{1,0:T(8,128)(2,1)} %collective-permute-done.7.refs_1_, bf16[256,4096]{1,0:T(8,128)(2,1)} %collective-permute-done.refs_2_, bf16[256,4096]{1,0:T(8,128)(2,1)} %collective-permute-done.8.refs_3_), custom_call_target="tpu_custom_call" | custom-call | flops 3449999872 | tf_op jit(solution)/shard_map/gather_rows/pallas_call | solution.py:302
  69.7 4.2 %project.4 = (bf16[1024,128]{1,0:T(8,128)(2,1)S(1)}, bf16[1024,128]{1,0:T(8,128)(2,1)S(1)}) custom-call(s32[3]{0:T(128)S(1)} %pad_add_fusion.1.info, bf16[1024,4096]{1,0:T(8,128)(2,1)S(1)} %gather_rows.1.rows_ref, bf16[128,2048]{1,0:T(8,128)(2,1)} %collective-permute-done.1.refs_0_, bf16[128,2048]{1,0:T(8,128)(2,1)S(1)} %copy-done.9, ...), custom_call_target="tpu_custom_call" | custom-call | flops 3449999872 | tf_op jit(solution)/shard_map/project/pallas_call | solution.py:340
  73.9 3.0 %project.6 = bf16[1024,256]{1,0:T(8,128)(2,1)S(1)} custom-call(s32[3]{0:T(128)S(1)} %pad_add_fusion.1.info, bf16[1024,4096]{1,0:T(8,128)(2,1)S(1)} %gather_rows.1.rows_ref, bf16[256,4096]{1,0:T(8,128)(2,1)S(1)} %copy-done.1), custom_call_target="tpu_custom_call" | custom-call | flops 3449999872 | tf_op jit(solution)/shard_map/project/pallas_call | solution.py:340
  76.9 2.6 %collective-permute-start.10 = (bf16[1024,128]{1,0:T(8,128)(2,1)S(1)}, bf16[1024,128]{1,0:T(8,128)(2,1)S(1)}, u32[]{:S(2)}, u32[]{:S(2)}) collective-permute-start(bf16[1024,128]{1,0:T(8,128)(2,1)S(1)} %get-tuple-element.71), channel_id=1, source_target_pairs={{0,4},{1,5},{2,6},{3,7},{4,0},{5,1},{6,2},{7,3},{8,12},{9,13},{10,... | collective-permute-start | bytes 786440 | tf_op jit(solution)/shard_map/ppermute | solution.py:519
  79.6 12.3 %collective-permute-done.12.refs_2_ = bf16[128,2048]{1,0:T(8,128)(2,1)S(1)} collective-permute-done((bf16[128,2048]{1,0:T(8,128)(2,1)}, bf16[128,2048]{1,0:T(8,128)(2,1)S(1)}, u32[]{:S(2)}, u32[]{:S(2)}) %collective-permute-start.12) | collective-permute-done | bytes 524320 | tf_op jit(solution)/shard_map/ppermute | solution.py:519
  93.9 2.9 %project.5 = (bf16[1024,128]{1,0:T(8,128)(2,1)S(1)}, bf16[1024,128]{1,0:T(8,128)(2,1)S(1)}) custom-call(s32[3]{0:T(128)S(1)} %pad_add_fusion.1.info, bf16[1024,4096]{1,0:T(8,128)(2,1)S(1)} %gather_rows.1.rows_ref, bf16[128,2048]{1,0:T(8,128)(2,1)S(1)} %collective-permute-done.3.refs_0_, bf16[128,2048]{1,0:T(8,128)(2,1)S(1)} %collective-permute-done.13.refs_1_, ...), custom_call_target="tpu_custom_call" | custom-call | flops 3449999872 | tf_op jit(solution)/shard_map/project/pallas_call | solution.py:340
  99.3 15.0 %collective-permute-done.16 = bf16[1024,128]{1,0:T(8,128)(2,1)S(1)} collective-permute-done((bf16[1024,128]{1,0:T(8,128)(2,1)S(1)}, bf16[1024,128]{1,0:T(8,128)(2,1)S(1)}, u32[]{:S(2)}, u32[]{:S(2)}) %collective-permute-start.16) | collective-permute-done | bytes 262176 | tf_op jit(solution)/shard_map/ppermute | solution.py:519
  115.6 2.9 %project.7 = (bf16[1024,128]{1,0:T(8,128)(2,1)S(1)}, bf16[1024,128]{1,0:T(8,128)(2,1)S(1)}) custom-call(s32[3]{0:T(128)S(1)} %pad_add_fusion.1.info, bf16[1024,4096]{1,0:T(8,128)(2,1)S(1)} %gather_rows.1.rows_ref, bf16[128,2048]{1,0:T(8,128)(2,1)S(1)} %collective-permute-done.11.refs_0_, bf16[128,2048]{1,0:T(8,128)(2,1)S(1)} %collective-permute-done.18.refs_1_, ...), custom_call_target="tpu_custom_call" | custom-call | flops 3449999872 | tf_op jit(solution)/shard_map/project/pallas_call | solution.py:340
  120.6 4.4 %collective-permute-start.21 = (bf16[1024,128]{1,0:T(8,128)(2,1)S(1)}, bf16[1024,128]{1,0:T(8,128)(2,1)S(1)}, u32[]{:S(2)}, u32[]{:S(2)}) collective-permute-start(bf16[1024,128]{1,0:T(8,128)(2,1)S(1)} %get-tuple-element.94), channel_id=1, source_target_pairs={{0,2},{1,3},{2,0},{3,1},{4,6},{5,7},{6,4},{7,5},{8,10},{9,11},{10,... | collective-permute-start | bytes 786440 | tf_op jit(solution)/shard_map/ppermute | solution.py:519
  126.3 4.5 %attention.1 = (f32[2048,512]{1,0:T(8,128)S(1)}, f32[1,2048]{1,0:T(1,128)S(1)}, bf16[8,4,128,128]{3,2,1,0:T(8,128)(2,1)S(1)}) custom-call(s32[5]{0:T(128)S(1)} %pad_add_fusion.info, bf16[2048,512]{1,0:T(8,128)(2,1)S(1)} %copy-done.3, bf16[2048,512]{1,0:T(8,128)(2,1)S(1)} %copy-done.5, bf16[2048,512]{1,0:T(8,128)(2,1)S(1)} %copy-done.7, ...), custom_call_target="tpu_custom_call" | custom-call | flops 9200000000 | tf_op jit(solution)/shard_map/attention/attention/pallas_call | solution.py:498
  130.8 2.6 %collective-permute-done.21 = bf16[1024,128]{1,0:T(8,128)(2,1)S(1)} collective-permute-done((bf16[1024,128]{1,0:T(8,128)(2,1)S(1)}, bf16[1024,128]{1,0:T(8,128)(2,1)S(1)}, u32[]{:S(2)}, u32[]{:S(2)}) %collective-permute-start.21) | collective-permute-done | bytes 262176 | tf_op jit(solution)/shard_map/ppermute | solution.py:519
  133.6 2.6 %collective-permute-done.23.far_ref = bf16[2048,256]{1,0:T(8,128)(2,1)S(1)} collective-permute-done((bf16[2048,256]{1,0:T(8,128)(2,1)S(1)}, bf16[2048,256]{1,0:T(8,128)(2,1)S(1)}, u32[]{:S(2)}, u32[]{:S(2)}) %collective-permute-start.23) | collective-permute-done | bytes 1048608 | tf_op jit(solution)/shard_map/ppermute | solution.py:519
  143.3 2.7 %collective-permute-done.26.refs_3_ = f32[2,2048]{1,0:T(2,128)S(1)} collective-permute-done((f32[2,2048]{1,0:T(2,128)S(1)}, f32[2,2048]{1,0:T(2,128)S(1)}, u32[]{:S(2)}, u32[]{:S(2)}) %collective-permute-start.26) | collective-permute-done | bytes 16416 | tf_op jit(solution)/shard_map/ppermute | solution.py:519
  147.5 2.3 %collective-permute-done.27.refs_1_ = f32[2,2048]{1,0:T(2,128)S(1)} collective-permute-done((f32[2,2048]{1,0:T(2,128)S(1)}, f32[2,2048]{1,0:T(2,128)S(1)}, u32[]{:S(2)}, u32[]{:S(2)}) %collective-permute-start.27) | collective-permute-done | bytes 16416 | tf_op jit(solution)/shard_map/ppermute | solution.py:519
  149.7 5.8 %grad_attn.1 = (bf16[2048,512]{1,0:T(8,128)(2,1)S(1)}, bf16[2048,512]{1,0:T(8,128)(2,1)}, f32[8,4,128,128]{3,2,1,0:T(8,128)S(1)}, f32[4,128,128]{2,1,0:T(8,128)S(1)}, bf16[4,128,128]{2,1,0:T(8,128)(2,1)S(1)}) custom-call(s32[5]{0:T(128)S(1)} %pad_add_fusion.info, bf16[2048,256]{1,0:T(8,128)(2,1)S(1)} %get-tuple-element.117.near_ref, ...), custom_call_target="tpu_custom_call" | custom-call | flops 4600000000 | tf_op jit(solution)/shard_map/grad_attn/grad_attn/pallas_call | solution.py:498
  157.7 4.7 %grad_queries.1 = bf16[2048,512]{1,0:T(8,128)(2,1)} custom-call(s32[5]{0:T(128)S(1)} %pad_add_fusion.info, bf16[2048,512]{1,0:T(8,128)(2,1)S(1)} %get-tuple-element.104.grad_ref, bf16[2048,512]{1,0:T(8,128)(2,1)S(1)} %copy-done.5, bf16[2048,512]{1,0:T(8,128)(2,1)S(1)} %copy-done.7, bf16[8,4,128,128]{3,2,1,0:T(8,128)(2,1)S(1)} %get-tuple-element.105.low_ref), custom_call_target="tpu_custom_call" | custom-call | flops 9200000000 | tf_op jit(solution)/shard_map/grad_queries/grad_queries/pallas_call | solution.py:498
  162.8 7.9 %grad_keys_values.1 = (bf16[2048,512]{1,0:T(8,128)(2,1)}, bf16[2048,512]{1,0:T(8,128)(2,1)}) custom-call(s32[5]{0:T(128)S(1)} %pad_add_fusion.info, bf16[2048,512]{1,0:T(8,128)(2,1)S(1)} %get-tuple-element.104.grad_ref, bf16[2048,512]{1,0:T(8,128)(2,1)S(1)} %copy-done.3, bf16[2048,512]{1,0:T(8,128)(2,1)S(1)} %copy-done.5, bf16[2048,512]{1,0:T(8,128)(2,1)S(1)} %copy-done.7, ...), custom_call_target="tpu_custom_call" | custom-call | flops 9200000000 | tf_op jit(solution)/shard_map/grad_keys_values/grad_keys_values/pallas_call | solution.py:498
  (100 shorter events, 43.5 us)
Async XLA Ops:
  2.9 31.3 %collective-permute-start = (bf16[256,4096]{1,0:T(8,128)(2,1)S(1)}, bf16[256,4096]{1,0:T(8,128)(2,1)}, u32[]{:S(2)}, u32[]{:S(2)}) collective-permute-start(bf16[256,4096]{1,0:T(8,128)(2,1)S(1)} %copy-done), channel_id=1, source_target_pairs={{0,8},{8,0},{16,24},{24,16},{1,9},{9,1},{17,25},{25,17},{2,10},{10... | collective-permute-start | bytes 6291464 | tf_op jit(solution)/shard_map/ppermute | solution.py:519
  3.4 26.4 %collective-permute-start.1 = (bf16[128,2048]{1,0:T(8,128)(2,1)S(1)}, bf16[128,2048]{1,0:T(8,128)(2,1)}, u32[]{:S(2)}, u32[]{:S(2)}) collective-permute-start(bf16[128,2048]{1,0:T(8,128)(2,1)S(1)} %get-tuple-element.113), channel_id=1, source_target_pairs={{0,2},{1,3},{2,0},{3,1},{4,6},{5,7},{6,4},{7,5},{8,10},{9,11},{10,... | collective-permute-start | bytes 1572872 | tf_op jit(solution)/shard_map/ppermute | solution.py:519
  5.9 26.3 %collective-permute-start.2 = (bf16[128,2048]{1,0:T(8,128)(2,1)S(1)}, bf16[128,2048]{1,0:T(8,128)(2,1)}, u32[]{:S(2)}, u32[]{:S(2)}) collective-permute-start(bf16[128,2048]{1,0:T(8,128)(2,1)S(1)} %get-tuple-element.113), channel_id=1, source_target_pairs={{0,4},{1,5},{2,6},{3,7},{4,0},{5,1},{6,2},{7,3},{8,12},{9,13},{10,... | collective-permute-start | bytes 1572872 | tf_op jit(solution)/shard_map/ppermute | solution.py:519
  8.5 47.6 %collective-permute-start.7 = (bf16[256,4096]{1,0:T(8,128)(2,1)S(1)}, bf16[256,4096]{1,0:T(8,128)(2,1)}, u32[]{:S(2)}, u32[]{:S(2)}) collective-permute-start(bf16[256,4096]{1,0:T(8,128)(2,1)S(1)} %copy-done), channel_id=1, source_target_pairs={{0,1},{1,0},{2,3},{3,2},{4,5},{5,4},{6,7},{7,6},{8,9},{9,8},{10,11... | collective-permute-start | bytes 6291464 | tf_op jit(solution)/shard_map/ppermute | solution.py:519
  29.8 24.6 %collective-permute-start.5 = (bf16[128,2048]{1,0:T(8,128)(2,1)}, bf16[128,2048]{1,0:T(8,128)(2,1)S(1)}, u32[]{:S(2)}, u32[]{:S(2)}) collective-permute-start(bf16[128,2048]{1,0:T(8,128)(2,1)} %collective-permute-done.1.refs_0_), channel_id=1, source_target_pairs={{0,16},{8,24},{16,0},{24,8},{1,17},{9,25},{17,1},{25,9},{2,18},{10... | collective-permute-start | bytes 1572872 | tf_op jit(solution)/shard_map/ppermute | solution.py:519
  32.3 22.1 %collective-permute-start.4 = (bf16[128,2048]{1,0:T(8,128)(2,1)}, bf16[128,2048]{1,0:T(8,128)(2,1)S(1)}, u32[]{:S(2)}, u32[]{:S(2)}) collective-permute-start(bf16[128,2048]{1,0:T(8,128)(2,1)} %collective-permute-done.2.refs_2_), channel_id=1, source_target_pairs={{0,2},{1,3},{2,0},{3,1},{4,6},{5,7},{6,4},{7,5},{8,10},{9,11},{10,... | collective-permute-start | bytes 1572872 | tf_op jit(solution)/shard_map/ppermute | solution.py:519
  32.7 22.5 %collective-permute-start.6 = (bf16[128,2048]{1,0:T(8,128)(2,1)}, bf16[128,2048]{1,0:T(8,128)(2,1)S(1)}, u32[]{:S(2)}, u32[]{:S(2)}) collective-permute-start(bf16[128,2048]{1,0:T(8,128)(2,1)} %collective-permute-done.2.refs_2_), channel_id=1, source_target_pairs={{0,16},{8,24},{16,0},{24,8},{1,17},{9,25},{17,1},{25,9},{2,18},{10... | collective-permute-start | bytes 1572872 | tf_op jit(solution)/shard_map/ppermute | solution.py:519
  34.3 25.3 %collective-permute-start.3 = (bf16[128,2048]{1,0:T(8,128)(2,1)}, bf16[128,2048]{1,0:T(8,128)(2,1)S(1)}, u32[]{:S(2)}, u32[]{:S(2)}) collective-permute-start(bf16[128,2048]{1,0:T(8,128)(2,1)} %get-tuple-element.72), channel_id=1, source_target_pairs={{0,4},{1,5},{2,6},{3,7},{4,0},{5,1},{6,2},{7,3},{8,12},{9,13},{10,... | collective-permute-start | bytes 1572872 | tf_op jit(solution)/shard_map/ppermute | solution.py:519
  59.6 6.4 %collective-permute-start.8 = (bf16[256,4096]{1,0:T(8,128)(2,1)}, bf16[256,4096]{1,0:T(8,128)(2,1)}, u32[]{:S(2)}, u32[]{:S(2)}) collective-permute-start(bf16[256,4096]{1,0:T(8,128)(2,1)} %collective-permute-done.7.refs_1_), channel_id=1, source_target_pairs={{0,8},{8,0},{16,24},{24,16},{1,9},{9,1},{17,25},{25,17},{2,10},{10... | collective-permute-start | bytes 6291464 | tf_op jit(solution)/shard_map/ppermute | solution.py:519
  60.2 16.7 %collective-permute-start.11 = (bf16[128,2048]{1,0:T(8,128)(2,1)S(1)}, bf16[128,2048]{1,0:T(8,128)(2,1)S(1)}, u32[]{:S(2)}, u32[]{:S(2)}) collective-permute-start(bf16[128,2048]{1,0:T(8,128)(2,1)S(1)} %collective-permute-done.3.refs_0_), channel_id=1, source_target_pairs={{0,2},{1,3},{2,0},{3,1},{4,6},{5,7},{6,4},{7,5},{8,10},{9,11},{10,... | collective-permute-start | bytes 1572872 | tf_op jit(solution)/shard_map/ppermute | solution.py:519
  60.2 31.6 %collective-permute-start.13 = (bf16[128,2048]{1,0:T(8,128)(2,1)S(1)}, bf16[128,2048]{1,0:T(8,128)(2,1)S(1)}, u32[]{:S(2)}, u32[]{:S(2)}) collective-permute-start(bf16[128,2048]{1,0:T(8,128)(2,1)S(1)} %collective-permute-done.3.refs_0_), channel_id=1, source_target_pairs={{0,16},{8,24},{16,0},{24,8},{1,17},{9,25},{17,1},{25,9},{2,18},{10... | collective-permute-start | bytes 1572872 | tf_op jit(solution)/shard_map/ppermute | solution.py:519
  60.8 31.1 %collective-permute-start.12 = (bf16[128,2048]{1,0:T(8,128)(2,1)}, bf16[128,2048]{1,0:T(8,128)(2,1)S(1)}, u32[]{:S(2)}, u32[]{:S(2)}) collective-permute-start(bf16[128,2048]{1,0:T(8,128)(2,1)} %get-tuple-element.72), channel_id=1, source_target_pairs={{0,2},{1,3},{2,0},{3,1},{4,6},{5,7},{6,4},{7,5},{8,10},{9,11},{10,... | collective-permute-start | bytes 1572872 | tf_op jit(solution)/shard_map/ppermute | solution.py:519
  63.9 27.9 %collective-permute-start.14 = (bf16[128,2048]{1,0:T(8,128)(2,1)S(1)}, bf16[128,2048]{1,0:T(8,128)(2,1)S(1)}, u32[]{:S(2)}, u32[]{:S(2)}) collective-permute-start(bf16[128,2048]{1,0:T(8,128)(2,1)S(1)} %collective-permute-done.4.refs_2_), channel_id=1, source_target_pairs={{0,16},{8,24},{16,0},{24,8},{1,17},{9,25},{17,1},{25,9},{2,18},{10... | collective-permute-start | bytes 1572872 | tf_op jit(solution)/shard_map/ppermute | solution.py:519
  73.8 23.2 %collective-permute-start.9 = (bf16[1024,128]{1,0:T(8,128)(2,1)S(1)}, bf16[1024,128]{1,0:T(8,128)(2,1)S(1)}, u32[]{:S(2)}, u32[]{:S(2)}) collective-permute-start(bf16[1024,128]{1,0:T(8,128)(2,1)S(1)} %get-tuple-element.70), channel_id=1, source_target_pairs={{0,2},{1,3},{2,0},{3,1},{4,6},{5,7},{6,4},{7,5},{8,10},{9,11},{10,... | collective-permute-start | bytes 786440 | tf_op jit(solution)/shard_map/ppermute | solution.py:519
  76.9 22.3 %collective-permute-start.10 = (bf16[1024,128]{1,0:T(8,128)(2,1)S(1)}, bf16[1024,128]{1,0:T(8,128)(2,1)S(1)}, u32[]{:S(2)}, u32[]{:S(2)}) collective-permute-start(bf16[1024,128]{1,0:T(8,128)(2,1)S(1)} %get-tuple-element.71), channel_id=1, source_target_pairs={{0,4},{1,5},{2,6},{3,7},{4,0},{5,1},{6,2},{7,3},{8,12},{9,13},{10,... | collective-permute-start | bytes 786440 | tf_op jit(solution)/shard_map/ppermute | solution.py:519
  91.8 22.7 %collective-permute-start.18 = (bf16[128,2048]{1,0:T(8,128)(2,1)S(1)}, bf16[128,2048]{1,0:T(8,128)(2,1)S(1)}, u32[]{:S(2)}, u32[]{:S(2)}) collective-permute-start(bf16[128,2048]{1,0:T(8,128)(2,1)S(1)} %collective-permute-done.11.refs_0_), channel_id=1, source_target_pairs={{0,16},{8,24},{16,0},{24,8},{1,17},{9,25},{17,1},{25,9},{2,18},{10... | collective-permute-start | bytes 1572872 | tf_op jit(solution)/shard_map/ppermute | solution.py:519
  92.3 22.7 %collective-permute-start.19 = (bf16[128,2048]{1,0:T(8,128)(2,1)S(1)}, bf16[128,2048]{1,0:T(8,128)(2,1)S(1)}, u32[]{:S(2)}, u32[]{:S(2)}) collective-permute-start(bf16[128,2048]{1,0:T(8,128)(2,1)S(1)} %collective-permute-done.12.refs_2_), channel_id=1, source_target_pairs={{0,16},{8,24},{16,0},{24,8},{1,17},{9,25},{17,1},{25,9},{2,18},{10... | collective-permute-start | bytes 1572872 | tf_op jit(solution)/shard_map/ppermute | solution.py:519
  96.8 17.5 %collective-permute-start.16 = (bf16[1024,128]{1,0:T(8,128)(2,1)S(1)}, bf16[1024,128]{1,0:T(8,128)(2,1)S(1)}, u32[]{:S(2)}, u32[]{:S(2)}) collective-permute-start(bf16[1024,128]{1,0:T(8,128)(2,1)S(1)} %get-tuple-element.82), channel_id=1, source_target_pairs={{0,4},{1,5},{2,6},{3,7},{4,0},{5,1},{6,2},{7,3},{8,12},{9,13},{10,... | collective-permute-start | bytes 786440 | tf_op jit(solution)/shard_map/ppermute | solution.py:519
  97.1 17.3 %collective-permute-start.17 = (bf16[1024,128]{1,0:T(8,128)(2,1)S(1)}, bf16[1024,128]{1,0:T(8,128)(2,1)S(1)}, u32[]{:S(2)}, u32[]{:S(2)}) collective-permute-start(bf16[1024,128]{1,0:T(8,128)(2,1)S(1)} %get-tuple-element.83), channel_id=1, source_target_pairs={{0,6},{1,7},{2,4},{3,5},{4,2},{5,3},{6,0},{7,1},{8,14},{9,15},{10,... | collective-permute-start | bytes 786440 | tf_op jit(solution)/shard_map/ppermute | solution.py:519
  115.1 9.9 %collective-permute-start.22 = (bf16[4,128,128]{2,1,0:T(8,128)(2,1)S(1)}, bf16[4,128,128]{2,1,0:T(8,128)(2,1)S(1)}, u32[]{:S(2)}, u32[]{:S(2)}) collective-permute-start(bf16[4,128,128]{2,1,0:T(8,128)(2,1)S(1)} %get-tuple-element.97.total_ref), channel_id=1, source_target_pairs={{0,16},{8,24},{16,0},{24,8},{1,17},{9,25},{17,1},{25,9},{2,18},{10... | collective-permute-start | bytes 393224 | tf_op jit(solution)/shard_map/ppermute | solution.py:519
  118.5 12.3 %collective-permute-start.20 = (bf16[1024,128]{1,0:T(8,128)(2,1)S(1)}, bf16[1024,128]{1,0:T(8,128)(2,1)S(1)}, u32[]{:S(2)}, u32[]{:S(2)}) collective-permute-start(bf16[1024,128]{1,0:T(8,128)(2,1)S(1)} %get-tuple-element.93), channel_id=1, source_target_pairs={{0,6},{1,7},{2,4},{3,5},{4,2},{5,3},{6,0},{7,1},{8,14},{9,15},{10,... | collective-permute-start | bytes 786440 | tf_op jit(solution)/shard_map/ppermute | solution.py:519
  120.6 12.8 %collective-permute-start.21 = (bf16[1024,128]{1,0:T(8,128)(2,1)S(1)}, bf16[1024,128]{1,0:T(8,128)(2,1)S(1)}, u32[]{:S(2)}, u32[]{:S(2)}) collective-permute-start(bf16[1024,128]{1,0:T(8,128)(2,1)S(1)} %get-tuple-element.94), channel_id=1, source_target_pairs={{0,2},{1,3},{2,0},{3,1},{4,6},{5,7},{6,4},{7,5},{8,10},{9,11},{10,... | collective-permute-start | bytes 786440 | tf_op jit(solution)/shard_map/ppermute | solution.py:519
  155.5 6.8 %collective-permute-start.29 = (bf16[4,128,128]{2,1,0:T(8,128)(2,1)S(1)}, bf16[4,128,128]{2,1,0:T(8,128)(2,1)S(1)}, u32[]{:S(2)}, u32[]{:S(2)}) collective-permute-start(bf16[4,128,128]{2,1,0:T(8,128)(2,1)S(1)} %get-tuple-element.108), channel_id=1, source_target_pairs={{0,16},{8,24},{16,0},{24,8},{1,17},{9,25},{17,1},{25,9},{2,18},{10... | collective-permute-start | bytes 393224 | tf_op jit(solution)/shard_map/ppermute | solution.py:519
  157.0 5.8 %collective-permute-start.30 = (bf16[4,128,128]{2,1,0:T(8,128)(2,1)S(1)}, bf16[4,128,128]{2,1,0:T(8,128)(2,1)S(1)}, u32[]{:S(2)}, u32[]{:S(2)}) collective-permute-start(bf16[4,128,128]{2,1,0:T(8,128)(2,1)S(1)} %get-tuple-element.108), channel_id=1, source_target_pairs={{0,24},{8,16},{16,8},{24,0},{1,25},{9,17},{17,9},{25,1},{2,26},{10... | collective-permute-start | bytes 393224 | tf_op jit(solution)/shard_map/ppermute | solution.py:519
  (23 other events, 106.7 us)

commit v6 on v5

--- a/solution.py
+++ b/solution.py
@@ -348,7 +348,7 @@
         ),
         out_shape=outs,
         name="project",
-        cost_estimate=cost(3.0),
+        cost_estimate=cost(5.0),
         compiler_params=pltpu.CompilerParams(vmem_limit_bytes=PROJECT_VMEM),
     )(info, *args)
 

time: 171 us -> 171 us (level)
  no operation moved by 1% of the time
where the time goes in v6:
time: 171 us
  waiting for transfers between devices  73.8 us (43%)
  Pallas kernels  46.3 us (27%)
  starting transfers between devices  39 us (23%)
  local copies, waits for them, and re-layouts  10.5 us (6%)
    ppermute x31, waiting for transfers between devices, flip(): lax.ppermute(a, axis, [(i, i ^ bit) for i in range(lax.axis_size(axis))])  73.8 us
    ppermute x31, starting transfers between devices, flip(): lax.ppermute(a, axis, [(i, i ^ bit) for i in range(lax.axis_size(axis))])  39 us
    pallas_call x6, Pallas kernels, call(): pl.pallas_call(kernel, grid_spec=pltpu.PrefetchScalarGridSpec(num_scalar_...  26.9 us
    pallas_call x4, Pallas kernels, project(): pl.pallas_call(functools.partial(project_kernel, len(shards[0])), grid_sp...  12.9 us
    unnamed x32, local copies, waits for them, and re-layouts  6.19 us
    pallas_call x1, Pallas kernels, gather_rows(): pl.pallas_call(gather_kernel, grid_spec=pltpu.PrefetchScalarGridSpec(num_...  3.58 us
  transfers between devices with their start and end apart: 31, of which 15 were waited for; matrix products, arithmetic and copies ran while one was open for 1% of the time, Pallas kernels for 18%

profile of v6, /device:TPU:0, one launch (start us, length us, event | category | flops | bytes accessed | tf_op | source)
XLA Modules:
  0.0 170.7 jit_solution(1880120066657207456)
XLA Ops:
  3.4 2.6 %collective-permute-start.1 = (bf16[128,2048]{1,0:T(8,128)(2,1)S(1)}, bf16[128,2048]{1,0:T(8,128)(2,1)}, u32[]{:S(2)}, u32[]{:S(2)}) collective-permute-start(bf16[128,2048]{1,0:T(8,128)(2,1)S(1)} %get-tuple-element.113), channel_id=1, source_target_pairs={{0,2},{1,3},{2,0},{3,1},{4,6},{5,7},{6,4},{7,5},{8,10},{9,11},{10,... | collective-permute-start | bytes 1572872 | tf_op jit(solution)/shard_map/ppermute | solution.py:519
  5.9 2.6 %collective-permute-start.2 = (bf16[128,2048]{1,0:T(8,128)(2,1)S(1)}, bf16[128,2048]{1,0:T(8,128)(2,1)}, u32[]{:S(2)}, u32[]{:S(2)}) collective-permute-start(bf16[128,2048]{1,0:T(8,128)(2,1)S(1)} %get-tuple-element.113), channel_id=1, source_target_pairs={{0,4},{1,5},{2,6},{3,7},{4,0},{5,1},{6,2},{7,3},{8,12},{9,13},{10,... | collective-permute-start | bytes 1572872 | tf_op jit(solution)/shard_map/ppermute | solution.py:519
  10.1 19.7 %collective-permute-done.1.refs_0_ = bf16[128,2048]{1,0:T(8,128)(2,1)} collective-permute-done((bf16[128,2048]{1,0:T(8,128)(2,1)S(1)}, bf16[128,2048]{1,0:T(8,128)(2,1)}, u32[]{:S(2)}, u32[]{:S(2)}) %collective-permute-start.1) | collective-permute-done | bytes 524320 | tf_op jit(solution)/shard_map/ppermute | solution.py:519
  34.3 2.6 %collective-permute-start.3 = (bf16[128,2048]{1,0:T(8,128)(2,1)}, bf16[128,2048]{1,0:T(8,128)(2,1)S(1)}, u32[]{:S(2)}, u32[]{:S(2)}) collective-permute-start(bf16[128,2048]{1,0:T(8,128)(2,1)} %get-tuple-element.72), channel_id=1, source_target_pairs={{0,4},{1,5},{2,6},{3,7},{4,0},{5,1},{6,2},{7,3},{8,12},{9,13},{10,... | collective-permute-start | bytes 1572872 | tf_op jit(solution)/shard_map/ppermute | solution.py:519
  40.0 2.3 %key_states.1 = (f32[8,4,128,128]{3,2,1,0:T(8,128)S(1)}, f32[4,128,128]{2,1,0:T(8,128)S(1)}) custom-call(s32[5]{0:T(128)S(1)} %pad_add_fusion.info, bf16[2048,512]{1,0:T(8,128)(2,1)S(1)} %copy-done.4, bf16[2048,512]{1,0:T(8,128)(2,1)S(1)} %copy-done.6), custom_call_target="tpu_custom_call" | custom-call | flops 13799999488 | tf_op jit(solution)/shard_map/key_states/key_states/pallas_call | solution.py:498
  45.1 9.3 %collective-permute-done.4.refs_2_ = bf16[128,2048]{1,0:T(8,128)(2,1)S(1)} collective-permute-done((bf16[128,2048]{1,0:T(8,128)(2,1)}, bf16[128,2048]{1,0:T(8,128)(2,1)S(1)}, u32[]{:S(2)}, u32[]{:S(2)}) %collective-permute-start.4) | collective-permute-done | bytes 524320 | tf_op jit(solution)/shard_map/ppermute | solution.py:519
  56.1 3.5 %collective-permute-done.3.refs_0_ = bf16[128,2048]{1,0:T(8,128)(2,1)S(1)} collective-permute-done((bf16[128,2048]{1,0:T(8,128)(2,1)}, bf16[128,2048]{1,0:T(8,128)(2,1)S(1)}, u32[]{:S(2)}, u32[]{:S(2)}) %collective-permute-start.3) | collective-permute-done | bytes 524320 | tf_op jit(solution)/shard_map/ppermute | solution.py:519
  66.0 3.6 %gather_rows.1.rows_ref = bf16[1024,4096]{1,0:T(8,128)(2,1)S(1)} custom-call(s32[3]{0:T(128)S(1)} %pad_add_fusion.1.info, bf16[256,4096]{1,0:T(8,128)(2,1)S(1)} %copy-done, bf16[256,4096]{1,0:T(8,128)(2,1)} %collective-permute-done.7.refs_1_, bf16[256,4096]{1,0:T(8,128)(2,1)} %collective-permute-done.refs_2_, bf16[256,4096]{1,0:T(8,128)(2,1)} %collective-permute-done.8.refs_3_), custom_call_target="tpu_custom_call" | custom-call | flops 3449999872 | tf_op jit(solution)/shard_map/gather_rows/pallas_call | solution.py:302
  69.7 4.2 %project.4 = (bf16[1024,128]{1,0:T(8,128)(2,1)S(1)}, bf16[1024,128]{1,0:T(8,128)(2,1)S(1)}) custom-call(s32[3]{0:T(128)S(1)} %pad_add_fusion.1.info, bf16[1024,4096]{1,0:T(8,128)(2,1)S(1)} %gather_rows.1.rows_ref, bf16[128,2048]{1,0:T(8,128)(2,1)} %collective-permute-done.1.refs_0_, bf16[128,2048]{1,0:T(8,128)(2,1)S(1)} %copy-done.9, ...), custom_call_target="tpu_custom_call" | custom-call | flops 5750000128 | tf_op jit(solution)/shard_map/project/pallas_call | solution.py:340
  73.9 3.0 %project.6 = bf16[1024,256]{1,0:T(8,128)(2,1)S(1)} custom-call(s32[3]{0:T(128)S(1)} %pad_add_fusion.1.info, bf16[1024,4096]{1,0:T(8,128)(2,1)S(1)} %gather_rows.1.rows_ref, bf16[256,4096]{1,0:T(8,128)(2,1)S(1)} %copy-done.1), custom_call_target="tpu_custom_call" | custom-call | flops 5750000128 | tf_op jit(solution)/shard_map/project/pallas_call | solution.py:340
  76.9 2.6 %collective-permute-start.10 = (bf16[1024,128]{1,0:T(8,128)(2,1)S(1)}, bf16[1024,128]{1,0:T(8,128)(2,1)S(1)}, u32[]{:S(2)}, u32[]{:S(2)}) collective-permute-start(bf16[1024,128]{1,0:T(8,128)(2,1)S(1)} %get-tuple-element.71), channel_id=1, source_target_pairs={{0,4},{1,5},{2,6},{3,7},{4,0},{5,1},{6,2},{7,3},{8,12},{9,13},{10,... | collective-permute-start | bytes 786440 | tf_op jit(solution)/shard_map/ppermute | solution.py:519
  79.6 12.3 %collective-permute-done.12.refs_2_ = bf16[128,2048]{1,0:T(8,128)(2,1)S(1)} collective-permute-done((bf16[128,2048]{1,0:T(8,128)(2,1)}, bf16[128,2048]{1,0:T(8,128)(2,1)S(1)}, u32[]{:S(2)}, u32[]{:S(2)}) %collective-permute-start.12) | collective-permute-done | bytes 524320 | tf_op jit(solution)/shard_map/ppermute | solution.py:519
  93.9 2.9 %project.5 = (bf16[1024,128]{1,0:T(8,128)(2,1)S(1)}, bf16[1024,128]{1,0:T(8,128)(2,1)S(1)}) custom-call(s32[3]{0:T(128)S(1)} %pad_add_fusion.1.info, bf16[1024,4096]{1,0:T(8,128)(2,1)S(1)} %gather_rows.1.rows_ref, bf16[128,2048]{1,0:T(8,128)(2,1)S(1)} %collective-permute-done.3.refs_0_, bf16[128,2048]{1,0:T(8,128)(2,1)S(1)} %collective-permute-done.13.refs_1_, ...), custom_call_target="tpu_custom_call" | custom-call | flops 5750000128 | tf_op jit(solution)/shard_map/project/pallas_call | solution.py:340
  99.3 15.0 %collective-permute-done.16 = bf16[1024,128]{1,0:T(8,128)(2,1)S(1)} collective-permute-done((bf16[1024,128]{1,0:T(8,128)(2,1)S(1)}, bf16[1024,128]{1,0:T(8,128)(2,1)S(1)}, u32[]{:S(2)}, u32[]{:S(2)}) %collective-permute-start.16) | collective-permute-done | bytes 262176 | tf_op jit(solution)/shard_map/ppermute | solution.py:519
  115.6 2.9 %project.7 = (bf16[1024,128]{1,0:T(8,128)(2,1)S(1)}, bf16[1024,128]{1,0:T(8,128)(2,1)S(1)}) custom-call(s32[3]{0:T(128)S(1)} %pad_add_fusion.1.info, bf16[1024,4096]{1,0:T(8,128)(2,1)S(1)} %gather_rows.1.rows_ref, bf16[128,2048]{1,0:T(8,128)(2,1)S(1)} %collective-permute-done.11.refs_0_, bf16[128,2048]{1,0:T(8,128)(2,1)S(1)} %collective-permute-done.18.refs_1_, ...), custom_call_target="tpu_custom_call" | custom-call | flops 5750000128 | tf_op jit(solution)/shard_map/project/pallas_call | solution.py:340
  120.6 4.4 %collective-permute-start.21 = (bf16[1024,128]{1,0:T(8,128)(2,1)S(1)}, bf16[1024,128]{1,0:T(8,128)(2,1)S(1)}, u32[]{:S(2)}, u32[]{:S(2)}) collective-permute-start(bf16[1024,128]{1,0:T(8,128)(2,1)S(1)} %get-tuple-element.94), channel_id=1, source_target_pairs={{0,2},{1,3},{2,0},{3,1},{4,6},{5,7},{6,4},{7,5},{8,10},{9,11},{10,... | collective-permute-start | bytes 786440 | tf_op jit(solution)/shard_map/ppermute | solution.py:519
  126.3 4.5 %attention.1 = (f32[2048,512]{1,0:T(8,128)S(1)}, f32[1,2048]{1,0:T(1,128)S(1)}, bf16[8,4,128,128]{3,2,1,0:T(8,128)(2,1)S(1)}) custom-call(s32[5]{0:T(128)S(1)} %pad_add_fusion.info, bf16[2048,512]{1,0:T(8,128)(2,1)S(1)} %copy-done.3, bf16[2048,512]{1,0:T(8,128)(2,1)S(1)} %copy-done.5, bf16[2048,512]{1,0:T(8,128)(2,1)S(1)} %copy-done.7, ...), custom_call_target="tpu_custom_call" | custom-call | flops 9200000000 | tf_op jit(solution)/shard_map/attention/attention/pallas_call | solution.py:498
  130.8 2.6 %collective-permute-done.21 = bf16[1024,128]{1,0:T(8,128)(2,1)S(1)} collective-permute-done((bf16[1024,128]{1,0:T(8,128)(2,1)S(1)}, bf16[1024,128]{1,0:T(8,128)(2,1)S(1)}, u32[]{:S(2)}, u32[]{:S(2)}) %collective-permute-start.21) | collective-permute-done | bytes 262176 | tf_op jit(solution)/shard_map/ppermute | solution.py:519
  133.6 2.6 %collective-permute-done.23.far_ref = bf16[2048,256]{1,0:T(8,128)(2,1)S(1)} collective-permute-done((bf16[2048,256]{1,0:T(8,128)(2,1)S(1)}, bf16[2048,256]{1,0:T(8,128)(2,1)S(1)}, u32[]{:S(2)}, u32[]{:S(2)}) %collective-permute-start.23) | collective-permute-done | bytes 1048608 | tf_op jit(solution)/shard_map/ppermute | solution.py:519
  143.3 2.7 %collective-permute-done.26.refs_3_ = f32[2,2048]{1,0:T(2,128)S(1)} collective-permute-done((f32[2,2048]{1,0:T(2,128)S(1)}, f32[2,2048]{1,0:T(2,128)S(1)}, u32[]{:S(2)}, u32[]{:S(2)}) %collective-permute-start.26) | collective-permute-done | bytes 16416 | tf_op jit(solution)/shard_map/ppermute | solution.py:519
  147.5 2.3 %collective-permute-done.27.refs_1_ = f32[2,2048]{1,0:T(2,128)S(1)} collective-permute-done((f32[2,2048]{1,0:T(2,128)S(1)}, f32[2,2048]{1,0:T(2,128)S(1)}, u32[]{:S(2)}, u32[]{:S(2)}) %collective-permute-start.27) | collective-permute-done | bytes 16416 | tf_op jit(solution)/shard_map/ppermute | solution.py:519
  149.7 5.8 %grad_attn.1 = (bf16[2048,512]{1,0:T(8,128)(2,1)S(1)}, bf16[2048,512]{1,0:T(8,128)(2,1)}, f32[8,4,128,128]{3,2,1,0:T(8,128)S(1)}, f32[4,128,128]{2,1,0:T(8,128)S(1)}, bf16[4,128,128]{2,1,0:T(8,128)(2,1)S(1)}) custom-call(s32[5]{0:T(128)S(1)} %pad_add_fusion.info, bf16[2048,256]{1,0:T(8,128)(2,1)S(1)} %get-tuple-element.117.near_ref, ...), custom_call_target="tpu_custom_call" | custom-call | flops 4600000000 | tf_op jit(solution)/shard_map/grad_attn/grad_attn/pallas_call | solution.py:498
  157.7 4.7 %grad_queries.1 = bf16[2048,512]{1,0:T(8,128)(2,1)} custom-call(s32[5]{0:T(128)S(1)} %pad_add_fusion.info, bf16[2048,512]{1,0:T(8,128)(2,1)S(1)} %get-tuple-element.104.grad_ref, bf16[2048,512]{1,0:T(8,128)(2,1)S(1)} %copy-done.5, bf16[2048,512]{1,0:T(8,128)(2,1)S(1)} %copy-done.7, bf16[8,4,128,128]{3,2,1,0:T(8,128)(2,1)S(1)} %get-tuple-element.105.low_ref), custom_call_target="tpu_custom_call" | custom-call | flops 9200000000 | tf_op jit(solution)/shard_map/grad_queries/grad_queries/pallas_call | solution.py:498
  162.8 7.9 %grad_keys_values.1 = (bf16[2048,512]{1,0:T(8,128)(2,1)}, bf16[2048,512]{1,0:T(8,128)(2,1)}) custom-call(s32[5]{0:T(128)S(1)} %pad_add_fusion.info, bf16[2048,512]{1,0:T(8,128)(2,1)S(1)} %get-tuple-element.104.grad_ref, bf16[2048,512]{1,0:T(8,128)(2,1)S(1)} %copy-done.3, bf16[2048,512]{1,0:T(8,128)(2,1)S(1)} %copy-done.5, bf16[2048,512]{1,0:T(8,128)(2,1)S(1)} %copy-done.7, ...), custom_call_target="tpu_custom_call" | custom-call | flops 9200000000 | tf_op jit(solution)/shard_map/grad_keys_values/grad_keys_values/pallas_call | solution.py:498
  (100 shorter events, 43.5 us)
Async XLA Ops:
  2.9 31.3 %collective-permute-start = (bf16[256,4096]{1,0:T(8,128)(2,1)S(1)}, bf16[256,4096]{1,0:T(8,128)(2,1)}, u32[]{:S(2)}, u32[]{:S(2)}) collective-permute-start(bf16[256,4096]{1,0:T(8,128)(2,1)S(1)} %copy-done), channel_id=1, source_target_pairs={{0,8},{8,0},{16,24},{24,16},{1,9},{9,1},{17,25},{25,17},{2,10},{10... | collective-permute-start | bytes 6291464 | tf_op jit(solution)/shard_map/ppermute | solution.py:519
  3.4 26.4 %collective-permute-start.1 = (bf16[128,2048]{1,0:T(8,128)(2,1)S(1)}, bf16[128,2048]{1,0:T(8,128)(2,1)}, u32[]{:S(2)}, u32[]{:S(2)}) collective-permute-start(bf16[128,2048]{1,0:T(8,128)(2,1)S(1)} %get-tuple-element.113), channel_id=1, source_target_pairs={{0,2},{1,3},{2,0},{3,1},{4,6},{5,7},{6,4},{7,5},{8,10},{9,11},{10,... | collective-permute-start | bytes 1572872 | tf_op jit(solution)/shard_map/ppermute | solution.py:519
  5.9 26.3 %collective-permute-start.2 = (bf16[128,2048]{1,0:T(8,128)(2,1)S(1)}, bf16[128,2048]{1,0:T(8,128)(2,1)}, u32[]{:S(2)}, u32[]{:S(2)}) collective-permute-start(bf16[128,2048]{1,0:T(8,128)(2,1)S(1)} %get-tuple-element.113), channel_id=1, source_target_pairs={{0,4},{1,5},{2,6},{3,7},{4,0},{5,1},{6,2},{7,3},{8,12},{9,13},{10,... | collective-permute-start | bytes 1572872 | tf_op jit(solution)/shard_map/ppermute | solution.py:519
  8.5 47.6 %collective-permute-start.7 = (bf16[256,4096]{1,0:T(8,128)(2,1)S(1)}, bf16[256,4096]{1,0:T(8,128)(2,1)}, u32[]{:S(2)}, u32[]{:S(2)}) collective-permute-start(bf16[256,4096]{1,0:T(8,128)(2,1)S(1)} %copy-done), channel_id=1, source_target_pairs={{0,1},{1,0},{2,3},{3,2},{4,5},{5,4},{6,7},{7,6},{8,9},{9,8},{10,11... | collective-permute-start | bytes 6291464 | tf_op jit(solution)/shard_map/ppermute | solution.py:519
  29.8 24.6 %collective-permute-start.5 = (bf16[128,2048]{1,0:T(8,128)(2,1)}, bf16[128,2048]{1,0:T(8,128)(2,1)S(1)}, u32[]{:S(2)}, u32[]{:S(2)}) collective-permute-start(bf16[128,2048]{1,0:T(8,128)(2,1)} %collective-permute-done.1.refs_0_), channel_id=1, source_target_pairs={{0,16},{8,24},{16,0},{24,8},{1,17},{9,25},{17,1},{25,9},{2,18},{10... | collective-permute-start | bytes 1572872 | tf_op jit(solution)/shard_map/ppermute | solution.py:519
  32.3 22.1 %collective-permute-start.4 = (bf16[128,2048]{1,0:T(8,128)(2,1)}, bf16[128,2048]{1,0:T(8,128)(2,1)S(1)}, u32[]{:S(2)}, u32[]{:S(2)}) collective-permute-start(bf16[128,2048]{1,0:T(8,128)(2,1)} %collective-permute-done.2.refs_2_), channel_id=1, source_target_pairs={{0,2},{1,3},{2,0},{3,1},{4,6},{5,7},{6,4},{7,5},{8,10},{9,11},{10,... | collective-permute-start | bytes 1572872 | tf_op jit(solution)/shard_map/ppermute | solution.py:519
  32.7 22.5 %collective-permute-start.6 = (bf16[128,2048]{1,0:T(8,128)(2,1)}, bf16[128,2048]{1,0:T(8,128)(2,1)S(1)}, u32[]{:S(2)}, u32[]{:S(2)}) collective-permute-start(bf16[128,2048]{1,0:T(8,128)(2,1)} %collective-permute-done.2.refs_2_), channel_id=1, source_target_pairs={{0,16},{8,24},{16,0},{24,8},{1,17},{9,25},{17,1},{25,9},{2,18},{10... | collective-permute-start | bytes 1572872 | tf_op jit(solution)/shard_map/ppermute | solution.py:519
  34.3 25.3 %collective-permute-start.3 = (bf16[128,2048]{1,0:T(8,128)(2,1)}, bf16[128,2048]{1,0:T(8,128)(2,1)S(1)}, u32[]{:S(2)}, u32[]{:S(2)}) collective-permute-start(bf16[128,2048]{1,0:T(8,128)(2,1)} %get-tuple-element.72), channel_id=1, source_target_pairs={{0,4},{1,5},{2,6},{3,7},{4,0},{5,1},{6,2},{7,3},{8,12},{9,13},{10,... | collective-permute-start | bytes 1572872 | tf_op jit(solution)/shard_map/ppermute | solution.py:519
  59.6 6.4 %collective-permute-start.8 = (bf16[256,4096]{1,0:T(8,128)(2,1)}, bf16[256,4096]{1,0:T(8,128)(2,1)}, u32[]{:S(2)}, u32[]{:S(2)}) collective-permute-start(bf16[256,4096]{1,0:T(8,128)(2,1)} %collective-permute-done.7.refs_1_), channel_id=1, source_target_pairs={{0,8},{8,0},{16,24},{24,16},{1,9},{9,1},{17,25},{25,17},{2,10},{10... | collective-permute-start | bytes 6291464 | tf_op jit(solution)/shard_map/ppermute | solution.py:519
  60.2 16.7 %collective-permute-start.11 = (bf16[128,2048]{1,0:T(8,128)(2,1)S(1)}, bf16[128,2048]{1,0:T(8,128)(2,1)S(1)}, u32[]{:S(2)}, u32[]{:S(2)}) collective-permute-start(bf16[128,2048]{1,0:T(8,128)(2,1)S(1)} %collective-permute-done.3.refs_0_), channel_id=1, source_target_pairs={{0,2},{1,3},{2,0},{3,1},{4,6},{5,7},{6,4},{7,5},{8,10},{9,11},{10,... | collective-permute-start | bytes 1572872 | tf_op jit(solution)/shard_map/ppermute | solution.py:519
  60.2 31.6 %collective-permute-start.13 = (bf16[128,2048]{1,0:T(8,128)(2,1)S(1)}, bf16[128,2048]{1,0:T(8,128)(2,1)S(1)}, u32[]{:S(2)}, u32[]{:S(2)}) collective-permute-start(bf16[128,2048]{1,0:T(8,128)(2,1)S(1)} %collective-permute-done.3.refs_0_), channel_id=1, source_target_pairs={{0,16},{8,24},{16,0},{24,8},{1,17},{9,25},{17,1},{25,9},{2,18},{10... | collective-permute-start | bytes 1572872 | tf_op jit(solution)/shard_map/ppermute | solution.py:519
  60.8 31.1 %collective-permute-start.12 = (bf16[128,2048]{1,0:T(8,128)(2,1)}, bf16[128,2048]{1,0:T(8,128)(2,1)S(1)}, u32[]{:S(2)}, u32[]{:S(2)}) collective-permute-start(bf16[128,2048]{1,0:T(8,128)(2,1)} %get-tuple-element.72), channel_id=1, source_target_pairs={{0,2},{1,3},{2,0},{3,1},{4,6},{5,7},{6,4},{7,5},{8,10},{9,11},{10,... | collective-permute-start | bytes 1572872 | tf_op jit(solution)/shard_map/ppermute | solution.py:519
  63.9 27.9 %collective-permute-start.14 = (bf16[128,2048]{1,0:T(8,128)(2,1)S(1)}, bf16[128,2048]{1,0:T(8,128)(2,1)S(1)}, u32[]{:S(2)}, u32[]{:S(2)}) collective-permute-start(bf16[128,2048]{1,0:T(8,128)(2,1)S(1)} %collective-permute-done.4.refs_2_), channel_id=1, source_target_pairs={{0,16},{8,24},{16,0},{24,8},{1,17},{9,25},{17,1},{25,9},{2,18},{10... | collective-permute-start | bytes 1572872 | tf_op jit(solution)/shard_map/ppermute | solution.py:519
  73.8 23.2 %collective-permute-start.9 = (bf16[1024,128]{1,0:T(8,128)(2,1)S(1)}, bf16[1024,128]{1,0:T(8,128)(2,1)S(1)}, u32[]{:S(2)}, u32[]{:S(2)}) collective-permute-start(bf16[1024,128]{1,0:T(8,128)(2,1)S(1)} %get-tuple-element.70), channel_id=1, source_target_pairs={{0,2},{1,3},{2,0},{3,1},{4,6},{5,7},{6,4},{7,5},{8,10},{9,11},{10,... | collective-permute-start | bytes 786440 | tf_op jit(solution)/shard_map/ppermute | solution.py:519
  76.9 22.3 %collective-permute-start.10 = (bf16[1024,128]{1,0:T(8,128)(2,1)S(1)}, bf16[1024,128]{1,0:T(8,128)(2,1)S(1)}, u32[]{:S(2)}, u32[]{:S(2)}) collective-permute-start(bf16[1024,128]{1,0:T(8,128)(2,1)S(1)} %get-tuple-element.71), channel_id=1, source_target_pairs={{0,4},{1,5},{2,6},{3,7},{4,0},{5,1},{6,2},{7,3},{8,12},{9,13},{10,... | collective-permute-start | bytes 786440 | tf_op jit(solution)/shard_map/ppermute | solution.py:519
  91.8 22.7 %collective-permute-start.18 = (bf16[128,2048]{1,0:T(8,128)(2,1)S(1)}, bf16[128,2048]{1,0:T(8,128)(2,1)S(1)}, u32[]{:S(2)}, u32[]{:S(2)}) collective-permute-start(bf16[128,2048]{1,0:T(8,128)(2,1)S(1)} %collective-permute-done.11.refs_0_), channel_id=1, source_target_pairs={{0,16},{8,24},{16,0},{24,8},{1,17},{9,25},{17,1},{25,9},{2,18},{10... | collective-permute-start | bytes 1572872 | tf_op jit(solution)/shard_map/ppermute | solution.py:519
  92.3 22.7 %collective-permute-start.19 = (bf16[128,2048]{1,0:T(8,128)(2,1)S(1)}, bf16[128,2048]{1,0:T(8,128)(2,1)S(1)}, u32[]{:S(2)}, u32[]{:S(2)}) collective-permute-start(bf16[128,2048]{1,0:T(8,128)(2,1)S(1)} %collective-permute-done.12.refs_2_), channel_id=1, source_target_pairs={{0,16},{8,24},{16,0},{24,8},{1,17},{9,25},{17,1},{25,9},{2,18},{10... | collective-permute-start | bytes 1572872 | tf_op jit(solution)/shard_map/ppermute | solution.py:519
  96.8 17.5 %collective-permute-start.16 = (bf16[1024,128]{1,0:T(8,128)(2,1)S(1)}, bf16[1024,128]{1,0:T(8,128)(2,1)S(1)}, u32[]{:S(2)}, u32[]{:S(2)}) collective-permute-start(bf16[1024,128]{1,0:T(8,128)(2,1)S(1)} %get-tuple-element.82), channel_id=1, source_target_pairs={{0,4},{1,5},{2,6},{3,7},{4,0},{5,1},{6,2},{7,3},{8,12},{9,13},{10,... | collective-permute-start | bytes 786440 | tf_op jit(solution)/shard_map/ppermute | solution.py:519
  97.1 17.3 %collective-permute-start.17 = (bf16[1024,128]{1,0:T(8,128)(2,1)S(1)}, bf16[1024,128]{1,0:T(8,128)(2,1)S(1)}, u32[]{:S(2)}, u32[]{:S(2)}) collective-permute-start(bf16[1024,128]{1,0:T(8,128)(2,1)S(1)} %get-tuple-element.83), channel_id=1, source_target_pairs={{0,6},{1,7},{2,4},{3,5},{4,2},{5,3},{6,0},{7,1},{8,14},{9,15},{10,... | collective-permute-start | bytes 786440 | tf_op jit(solution)/shard_map/ppermute | solution.py:519
  115.1 9.9 %collective-permute-start.22 = (bf16[4,128,128]{2,1,0:T(8,128)(2,1)S(1)}, bf16[4,128,128]{2,1,0:T(8,128)(2,1)S(1)}, u32[]{:S(2)}, u32[]{:S(2)}) collective-permute-start(bf16[4,128,128]{2,1,0:T(8,128)(2,1)S(1)} %get-tuple-element.97.total_ref), channel_id=1, source_target_pairs={{0,16},{8,24},{16,0},{24,8},{1,17},{9,25},{17,1},{25,9},{2,18},{10... | collective-permute-start | bytes 393224 | tf_op jit(solution)/shard_map/ppermute | solution.py:519
  118.5 12.3 %collective-permute-start.20 = (bf16[1024,128]{1,0:T(8,128)(2,1)S(1)}, bf16[1024,128]{1,0:T(8,128)(2,1)S(1)}, u32[]{:S(2)}, u32[]{:S(2)}) collective-permute-start(bf16[1024,128]{1,0:T(8,128)(2,1)S(1)} %get-tuple-element.93), channel_id=1, source_target_pairs={{0,6},{1,7},{2,4},{3,5},{4,2},{5,3},{6,0},{7,1},{8,14},{9,15},{10,... | collective-permute-start | bytes 786440 | tf_op jit(solution)/shard_map/ppermute | solution.py:519
  120.6 12.8 %collective-permute-start.21 = (bf16[1024,128]{1,0:T(8,128)(2,1)S(1)}, bf16[1024,128]{1,0:T(8,128)(2,1)S(1)}, u32[]{:S(2)}, u32[]{:S(2)}) collective-permute-start(bf16[1024,128]{1,0:T(8,128)(2,1)S(1)} %get-tuple-element.94), channel_id=1, source_target_pairs={{0,2},{1,3},{2,0},{3,1},{4,6},{5,7},{6,4},{7,5},{8,10},{9,11},{10,... | collective-permute-start | bytes 786440 | tf_op jit(solution)/shard_map/ppermute | solution.py:519
  155.5 6.8 %collective-permute-start.29 = (bf16[4,128,128]{2,1,0:T(8,128)(2,1)S(1)}, bf16[4,128,128]{2,1,0:T(8,128)(2,1)S(1)}, u32[]{:S(2)}, u32[]{:S(2)}) collective-permute-start(bf16[4,128,128]{2,1,0:T(8,128)(2,1)S(1)} %get-tuple-element.108), channel_id=1, source_target_pairs={{0,16},{8,24},{16,0},{24,8},{1,17},{9,25},{17,1},{25,9},{2,18},{10... | collective-permute-start | bytes 393224 | tf_op jit(solution)/shard_map/ppermute | solution.py:519
  157.0 5.8 %collective-permute-start.30 = (bf16[4,128,128]{2,1,0:T(8,128)(2,1)S(1)}, bf16[4,128,128]{2,1,0:T(8,128)(2,1)S(1)}, u32[]{:S(2)}, u32[]{:S(2)}) collective-permute-start(bf16[4,128,128]{2,1,0:T(8,128)(2,1)S(1)} %get-tuple-element.108), channel_id=1, source_target_pairs={{0,24},{8,16},{16,8},{24,0},{1,25},{9,17},{17,9},{25,1},{2,26},{10... | collective-permute-start | bytes 393224 | tf_op jit(solution)/shard_map/ppermute | solution.py:519
  (23 other events, 106.7 us)
